TPU v7x, 32 devices: a whole 2x2x4 slice. The times are simulated.
32 devices in a mesh: seq: 8 (over z, y), batch: 4 (over x, core).
Axes of the slice: x: 2, y: 2, z: 4, core: 2. Of those that a mesh axis runs over, the one named last changes fastest.
Arguments:
- inputs: float32 [8, 1024, 1024], P('batch', 'seq'), may hold values from -6 to 6
- segments: int32 [8, 1024], P('batch', 'seq'), may hold values from 0 to 15, as said below
- w_gate: bfloat16 [1024, 1536], P(('seq', 'batch')), may hold values from -0.1875 to 0.1875
- w_input: bfloat16 [1024, 1536], P(('seq', 'batch')), may hold values from -0.1875 to 0.1875
- w_recur: bfloat16 [1536, 1536], P(('seq', 'batch')), may hold values from -0.15625 to 0.15625
- w_inject: bfloat16 [1536, 1536], P(('seq', 'batch')), may hold values from -0.15625 to 0.15625
- w_output: bfloat16 [1536, 1024], P(('seq', 'batch')), may hold values from -0.15625 to 0.15625
- w_hidden: bfloat16 [1024, 3072], P(('seq', 'batch')), may hold values from -0.1875 to 0.1875
- w_upward: bfloat16 [1024, 3072], P(('seq', 'batch')), may hold values from -0.1875 to 0.1875
- w_down: bfloat16 [3072, 1024], P(('seq', 'batch')), may hold values from -0.109375 to 0.109375
- gain_one: float32 [1024], replicated, may hold values from 0.5 to 1.5
- gain_two: float32 [1024], replicated, may hold values from 0.5 to 1.5
- conv_taps: float32 [4, 1536], replicated, may hold values from -3 to 3
- conv_bias: float32 [1536], replicated, may hold values from -3 to 3
- recur_bias: float32 [1536], replicated, may hold values from -3 to 3
- inject_bias: float32 [1536], replicated, may hold values from -3 to 3
- decay_param: float32 [1536], replicated, may hold values from -13 to -4.6
- cotangent: float32 [8, 1024, 1024], P('batch', 'seq'), may hold values from -6 to 6
Outputs:
- output: float32 [8, 1024, 1024], P('batch', 'seq')
- grad_inputs: float32 [8, 1024, 1024], P('batch', 'seq')
- grad_gate: float32 [1024, 1536], P(('seq', 'batch'))
- grad_input: float32 [1024, 1536], P(('seq', 'batch'))
- grad_recur: float32 [1536, 1536], P(('seq', 'batch'))
- grad_inject: float32 [1536, 1536], P(('seq', 'batch'))
- grad_output: float32 [1536, 1024], P(('seq', 'batch'))
- grad_hidden: float32 [1024, 3072], P(('seq', 'batch'))
- grad_upward: float32 [1024, 3072], P(('seq', 'batch'))
- grad_down: float32 [3072, 1024], P(('seq', 'batch'))
- grad_gain_one: float32 [1024], P(('seq', 'batch'))
- grad_gain_two: float32 [1024], P(('seq', 'batch'))
- grad_taps: float32 [4, 1536], P(None, ('seq', 'batch'))
- grad_conv_bias: float32 [1536], P(('seq', 'batch'))
- grad_recur_bias: float32 [1536], P(('seq', 'batch'))
- grad_inject_bias: float32 [1536], P(('seq', 'batch'))
- grad_decay_param: float32 [1536], P(('seq', 'batch'))
Inputs may be any that keep to these rules, and one draw needn't show every extreme that they name: `segments`: along each row the ids start at 0 and never fall, stepping by 0 or 1; in each aligned block of 2 rows one row is a single segment and every other row reaches the largest id.
All inputs are finite; a program needn't handle non-finite values.
Results may differ from a plain program's by a relative error of at most 0.0087.
Values may be sent and summed in bfloat16 or wider, within the bound.
A program may use at most 320 MiB of HBM per device.

v0:
```python
import jax
import jax.numpy as jnp
from jax import lax
from jax.sharding import PartitionSpec as P

EPSILON = 1e-06
DECAY_SCALE = 8.0
FLOOR_TERM = 0.01


def shifted(array, axis, by):
    peers = lax.axis_size(axis)
    pairs = [(i, i + by) for i in range(peers) if 0 <= i + by < peers]
    return lax.ppermute(array, axis, pairs)


def prefix(value, axis, join, neutral, backward):
    count, mine = (lax.axis_size(axis), lax.axis_index(axis))
    pieces = jax.tree.map(lambda part: lax.all_gather(part, axis), value)
    if backward:
        pieces = jax.tree.map(lambda part: part[::-1], pieces)
        mine = count - 1 - mine
    so_far = jax.tree.map(
        lambda part, zero: jnp.full_like(part, 0) + jnp.asarray(zero, part.dtype), value, neutral
    )

    def turn(position, so_far):
        longer = join(so_far, jax.tree.map(lambda part: part[position], pieces))
        return jax.tree.map(lambda new, old: jnp.where(position < mine, new, old), longer, so_far)

    return lax.fori_loop(0, count - 1, turn, so_far)


def shortened(array):
    return jax.tree.map(lambda a: a.astype(jnp.bfloat16) if a.dtype == jnp.float32 else a, array)


def combine(earlier, later):
    return (earlier[0] * later[0], later[1] + later[0] * earlier[1])


def matmul_plain(left, right):
    return jnp.dot(left, right, preferred_element_type=jnp.float32)


def matmul_tleft(left, right):
    return jnp.einsum("ta,tb->ab", left, right, preferred_element_type=jnp.float32)


def matmul_tright(left, right):
    return jnp.einsum("ta,ba->tb", left, right, preferred_element_type=jnp.float32)


def norm_forward(values, gain):
    scaler = lax.rsqrt(jnp.mean(values * values, axis=-1, keepdims=True) + EPSILON)
    return (values * scaler * gain, scaler)


def norm_back(values, scaler, gain, incoming):
    scaled = incoming * gain
    grad_gain = jnp.sum(incoming * values * scaler, axis=0)
    inner = jnp.mean(scaled * values, axis=-1, keepdims=True)
    return (scaler * (scaled - values * scaler * scaler * inner), grad_gain)


def local(
    inputs,
    segments,
    w_gate,
    w_input,
    w_recur,
    w_inject,
    w_output,
    w_hidden,
    w_upward,
    w_down,
    gain_one,
    gain_two,
    conv_taps,
    conv_bias,
    recur_bias,
    inject_bias,
    decay_param,
    cotangent,
):
    row_count, positions, features = inputs.shape
    (
        gate_full,
        input_full,
        recur_full,
        inject_full,
        output_full,
        hidden_full,
        upward_full,
        down_full,
    ) = (
        lax.all_gather(w_gate, ("seq", "batch"), axis=0, tiled=True),
        lax.all_gather(w_input, ("seq", "batch"), axis=0, tiled=True),
        lax.all_gather(w_recur, ("seq", "batch"), axis=0, tiled=True),
        lax.all_gather(w_inject, ("seq", "batch"), axis=0, tiled=True),
        lax.all_gather(w_output, ("seq", "batch"), axis=0, tiled=True),
        lax.all_gather(w_hidden, ("seq", "batch"), axis=0, tiled=True),
        lax.all_gather(w_upward, ("seq", "batch"), axis=0, tiled=True),
        lax.all_gather(w_down, ("seq", "batch"), axis=0, tiled=True),
    )
    channels = gate_full.shape[1]
    tokens_here = row_count * positions
    flat_in = inputs.reshape(tokens_here, features)
    normed, scale_one = norm_forward(flat_in, gain_one)
    normed_low = normed.astype(jnp.bfloat16)
    gate_pre = matmul_plain(normed_low, gate_full)
    gate_act, gate_pull = jax.vjp(jax.nn.gelu, gate_pre)
    branch = matmul_plain(normed_low, input_full).reshape(row_count, positions, channels)
    seg_marks = segments.astype(jnp.float32) + 1.0
    prior_branch, prior_marks = shifted(
        (branch[:, positions - 3 :], seg_marks[:, positions - 3 :]), "seq", 1
    )
    ext_branch = jnp.concatenate([prior_branch, branch], axis=1)
    ext_marks = jnp.concatenate([prior_marks, seg_marks], axis=1)
    sames = []
    lagged = []
    for offset in range(4):
        sames.append(
            (ext_marks[:, 3 - offset : 3 - offset + positions] == seg_marks).astype(jnp.float32)[
                :, :, None
            ]
        )
        lagged.append(ext_branch[:, 3 - offset : 3 - offset + positions])
    conv_out = conv_bias + conv_taps[0] * branch
    for offset in range(1, 4):
        conv_out = conv_out + conv_taps[offset] * lagged[offset] * sames[offset]
    conv_low = conv_out.reshape(tokens_here, channels).astype(jnp.bfloat16)
    recur_gate = jax.nn.sigmoid(matmul_plain(conv_low, recur_full) + recur_bias).reshape(
        row_count, positions, channels
    )
    inject_gate = jax.nn.sigmoid(matmul_plain(conv_low, inject_full) + inject_bias).reshape(
        row_count, positions, channels
    )
    base_rate = jax.nn.softplus(decay_param)
    decays = jnp.exp(-DECAY_SCALE * recur_gate * base_rate)
    carry_mult = decays * sames[1]
    normalizer = jnp.sqrt(1.0 - decays * decays + FLOOR_TERM)
    injected = normalizer * inject_gate * conv_out
    cumul, local_state = lax.associative_scan(combine, (carry_mult, injected), axis=1)
    ones_rows = jnp.ones((row_count, channels), jnp.float32)
    zeros_rows = jnp.zeros((row_count, channels), jnp.float32)
    entry = prefix(
        (cumul[:, -1], local_state[:, -1]), "seq", combine, (ones_rows, zeros_rows), False
    )[1]
    states = local_state + cumul * entry[:, None]
    states_before = jnp.concatenate([entry[:, None], states[:, :-1]], axis=1)
    states_flat = states.reshape(tokens_here, channels)
    mixed = (states_flat * gate_act).astype(jnp.bfloat16)
    resid = flat_in + matmul_plain(mixed, output_full)
    normed_two, scale_two = norm_forward(resid, gain_two)
    normed_two_low = normed_two.astype(jnp.bfloat16)
    hidden_pre = matmul_plain(normed_two_low, hidden_full)
    upward_pre = matmul_plain(normed_two_low, upward_full)
    hidden_act, hidden_pull = jax.vjp(jax.nn.gelu, hidden_pre)
    product = (hidden_act * upward_pre).astype(jnp.bfloat16)
    output = resid + matmul_plain(product, down_full)
    grad_out = cotangent.reshape(tokens_here, features)
    grad_out_low = grad_out.astype(jnp.bfloat16)
    grad_down = matmul_tleft(product, grad_out_low)
    grad_product = matmul_tright(grad_out_low, down_full)
    grad_hidden_pre = hidden_pull(grad_product * upward_pre)[0].astype(jnp.bfloat16)
    grad_upward_pre = (grad_product * hidden_act).astype(jnp.bfloat16)
    grad_hidden = matmul_tleft(normed_two_low, grad_hidden_pre)
    grad_upward = matmul_tleft(normed_two_low, grad_upward_pre)
    grad_normed_two = matmul_tright(grad_hidden_pre, hidden_full) + matmul_tright(
        grad_upward_pre, upward_full
    )
    grad_resid_norm, grad_gain_two = norm_back(resid, scale_two, gain_two, grad_normed_two)
    grad_resid = grad_out + grad_resid_norm
    grad_resid_low = grad_resid.astype(jnp.bfloat16)
    grad_output = matmul_tleft(mixed, grad_resid_low)
    grad_mixed = matmul_tright(grad_resid_low, output_full)
    grad_gate_pre = gate_pull(grad_mixed * states_flat)[0].astype(jnp.bfloat16)
    grad_states = (grad_mixed * gate_act).reshape(row_count, positions, channels)
    next_mult = jnp.concatenate([carry_mult[:, 1:], jnp.ones_like(carry_mult[:, :1])], axis=1)
    tail_prod, local_grad = lax.associative_scan(
        combine, (next_mult, grad_states), axis=1, reverse=True
    )
    incoming = prefix(
        (cumul[:, -1], carry_mult[:, 0] * local_grad[:, 0]),
        "seq",
        combine,
        (ones_rows, zeros_rows),
        True,
    )[1]
    total_grad = local_grad + tail_prod * incoming[:, None]
    grad_decays = (
        total_grad * states_before * sames[1]
        - total_grad * inject_gate * conv_out * decays / normalizer
    )
    grad_log = grad_decays * decays
    grad_recur_pre = grad_log * (-DECAY_SCALE * base_rate) * recur_gate * (1.0 - recur_gate)
    grad_decay_param = jnp.sum(
        grad_log * (-DECAY_SCALE * recur_gate), axis=(0, 1)
    ) * jax.nn.sigmoid(decay_param)
    grad_inject_pre = total_grad * normalizer * conv_out * inject_gate * (1.0 - inject_gate)
    grad_recur_bias = jnp.sum(grad_recur_pre, axis=(0, 1))
    grad_inject_bias = jnp.sum(grad_inject_pre, axis=(0, 1))
    grad_recur_low = grad_recur_pre.reshape(tokens_here, channels).astype(jnp.bfloat16)
    grad_inject_low = grad_inject_pre.reshape(tokens_here, channels).astype(jnp.bfloat16)
    grad_recur = matmul_tleft(conv_low, grad_recur_low)
    grad_inject = matmul_tleft(conv_low, grad_inject_low)
    through_gates = matmul_tright(grad_recur_low, recur_full) + matmul_tright(
        grad_inject_low, inject_full
    )
    grad_conv = total_grad * normalizer * inject_gate + through_gates.reshape(
        row_count, positions, channels
    )
    grad_conv_bias = jnp.sum(grad_conv, axis=(0, 1))
    taps_by_channel = jnp.stack(
        [jnp.sum(grad_conv * lagged[offset] * sames[offset], axis=(0, 1)) for offset in range(4)],
        axis=1,
    )
    later_grad, later_marks = (
        shifted(shortened(grad_conv[:, :3]), "seq", -1),
        shifted(seg_marks[:, :3].astype(jnp.bfloat16), "seq", -1).astype(jnp.float32),
    )
    ext_grad = jnp.concatenate([grad_conv, later_grad], axis=1)
    ext_after = jnp.concatenate([seg_marks, later_marks], axis=1)
    grad_branch = conv_taps[0] * grad_conv
    for offset in range(1, 4):
        match = (ext_after[:, offset : offset + positions] == seg_marks).astype(jnp.float32)[
            :, :, None
        ]
        grad_branch = (
            grad_branch + conv_taps[offset] * ext_grad[:, offset : offset + positions] * match
        )
    grad_branch_low = grad_branch.reshape(tokens_here, channels).astype(jnp.bfloat16)
    grad_input = matmul_tleft(normed_low, grad_branch_low)
    grad_gate = matmul_tleft(normed_low, grad_gate_pre)
    grad_normed = matmul_tright(grad_gate_pre, gate_full) + matmul_tright(
        grad_branch_low, input_full
    )
    grad_first_norm, grad_gain_one = norm_back(flat_in, scale_one, gain_one, grad_normed)
    grad_inputs = (grad_resid + grad_first_norm).reshape(row_count, positions, features)
    every = (
        lax.psum_scatter(grad_gate, ("seq", "batch"), scatter_dimension=0, tiled=True),
        lax.psum_scatter(grad_input, ("seq", "batch"), scatter_dimension=0, tiled=True),
        lax.psum_scatter(grad_recur, ("seq", "batch"), scatter_dimension=0, tiled=True),
        lax.psum_scatter(grad_inject, ("seq", "batch"), scatter_dimension=0, tiled=True),
        lax.psum_scatter(grad_output, ("seq", "batch"), scatter_dimension=0, tiled=True),
        lax.psum_scatter(grad_hidden, ("seq", "batch"), scatter_dimension=0, tiled=True),
        lax.psum_scatter(grad_upward, ("seq", "batch"), scatter_dimension=0, tiled=True),
        lax.psum_scatter(grad_down, ("seq", "batch"), scatter_dimension=0, tiled=True),
        lax.psum_scatter(grad_gain_one, ("seq", "batch"), scatter_dimension=0, tiled=True),
        lax.psum_scatter(grad_gain_two, ("seq", "batch"), scatter_dimension=0, tiled=True),
        lax.psum_scatter(taps_by_channel, ("seq", "batch"), scatter_dimension=0, tiled=True),
        lax.psum_scatter(grad_conv_bias, ("seq", "batch"), scatter_dimension=0, tiled=True),
        lax.psum_scatter(grad_recur_bias, ("seq", "batch"), scatter_dimension=0, tiled=True),
        lax.psum_scatter(grad_inject_bias, ("seq", "batch"), scatter_dimension=0, tiled=True),
        lax.psum_scatter(grad_decay_param, ("seq", "batch"), scatter_dimension=0, tiled=True),
    )
    summed = (
        every[0],
        every[1],
        every[2],
        every[3],
        every[4],
        every[5],
        every[6],
        every[7],
        every[8],
        every[9],
        every[10].T,
        every[11],
        every[12],
        every[13],
        every[14],
    )
    return (
        output.reshape(row_count, positions, features),
        grad_inputs,
        summed[0],
        summed[1],
        summed[2],
        summed[3],
        summed[4],
        summed[5],
        summed[6],
        summed[7],
        summed[8],
        summed[9],
        summed[10],
        summed[11],
        summed[12],
        summed[13],
        summed[14],
    )


def solution(mesh):
    return jax.shard_map(
        local,
        mesh=mesh,
        in_specs=(
            P("batch", "seq", None),
            P("batch", "seq"),
            P(("seq", "batch"), None),
            P(("seq", "batch"), None),
            P(("seq", "batch"), None),
            P(("seq", "batch"), None),
            P(("seq", "batch"), None),
            P(("seq", "batch"), None),
            P(("seq", "batch"), None),
            P(("seq", "batch"), None),
            P(),
            P(),
            P(),
            P(),
            P(),
            P(),
            P(),
            P("batch", "seq", None),
        ),
        out_specs=(
            P("batch", "seq", None),
            P("batch", "seq", None),
            P(("seq", "batch"), None),
            P(("seq", "batch"), None),
            P(("seq", "batch"), None),
            P(("seq", "batch"), None),
            P(("seq", "batch"), None),
            P(("seq", "batch"), None),
            P(("seq", "batch"), None),
            P(("seq", "batch"), None),
            P(("seq", "batch")),
            P(("seq", "batch")),
            P(None, ("seq", "batch")),
            P(("seq", "batch")),
            P(("seq", "batch")),
            P(("seq", "batch")),
            P(("seq", "batch")),
        ),
        check_vma=False,
    )
```

profile of v0, /device:TPU:0, one launch (start us, length us, event | category | flops | bytes accessed | tf_op | source)
XLA Modules:
  0.0 2082.4 jit_solution(16141335638511006380)
XLA Ops:
  12.8 4.9 collective-permute-start.1
  23.1 49.5 %all-gather.12.cloned.1.call-done = bf16[1024,1536]{1,0:T(8,128)(2,1)} async-done(((bf16[32,1536]{1,0:T(8,128)(2,1)}), bf16[1024,1536]{1,0:T(8,128)(2,1)}) %all-gather.12.cloned.1.call-update) | async-done | bytes 3145744 | tf_op jit(solution)/shard_map/all_gather | solution.py:98
  83.0 55.0 %all-gather.16.cloned.1.call-done = bf16[1536,1536]{1,0:T(8,128)(2,1)} async-done(((bf16[48,1536]{1,0:T(8,128)(2,1)}), bf16[1536,1536]{1,0:T(8,128)(2,1)}) %all-gather.16.cloned.1.call-update) | async-done | bytes 4718608 | tf_op jit(solution)/shard_map/all_gather | solution.py:100
  138.0 3.8 fusion.20
  141.8 61.6 %all-gather.14.cloned.1.call-done = bf16[1536,1536]{1,0:T(8,128)(2,1)} async-done(((bf16[48,1536]{1,0:T(8,128)(2,1)}), bf16[1536,1536]{1,0:T(8,128)(2,1)}) %all-gather.14.cloned.1.call-update) | async-done | bytes 4718608 | tf_op jit(solution)/shard_map/all_gather | solution.py:99
  203.4 3.9 fusion.18
  209.9 4.3 slice.518
  214.3 4.3 slice.522
  218.6 4.3 slice.517
  222.9 4.3 slice.519
  295.1 4.4 slice.516
  299.6 4.4 slice.515
  310.1 4.3 slice.588
  314.5 4.4 slice.594
  318.9 4.4 slice.584
  405.0 3.5 pad.200
  409.5 30.7 %all-gather.1 = f32[16,1,1536]{2,1,0:T(1,128)S(1)} all-gather(f32[2,1,1536]{2,1,0:T(1,128)S(1)} %slice_add_fusion.2), channel_id=3, replica_groups=mesh['seq'=8,'batch'=4] {'seq'}, dimensions={0}, use_global_device_ids=true | all-gather | bytes 110592 | tf_op jit(solution)/shard_map/all_gather | solution.py:19
  451.9 32.7 %all-gather = f32[16,1,1536]{2,1,0:T(1,128)} all-gather(f32[2,1,1536]{2,1,0:T(1,128)S(1)} %slice_add_fusion.3), channel_id=2, replica_groups=mesh['seq'=8,'batch'=4] {'seq'}, dimensions={0}, use_global_device_ids=true | all-gather | bytes 110592 | tf_op jit(solution)/shard_map/all_gather | solution.py:19
  488.0 6.9 slice.589
  494.9 6.8 slice.595
  501.7 6.9 slice.585
  509.3 5.6 while.28
  515.5 4.7 multiply_add_fusion.2
  520.2 5.1 fusion.45
  530.5 6.4 fusion.96
  536.9 6.4 fusion.97
  543.3 9.9 multiply_convert_fusion
  553.2 5.8 fusion.98
  564.4 3.5 fusion.53
  567.9 4.3 slice.586
  572.2 4.3 slice.590
  576.6 6.8 slice.587
  583.4 6.9 slice.591
  658.8 4.3 slice.581
  728.3 3.5 pad.215
  739.2 6.9 slice.582
  760.2 30.5 %all-gather.2 = f32[16,1,1536]{2,1,0:T(1,128)S(1)} all-gather(f32[2,1,1536]{2,1,0:T(1,128)S(1)} %add_multiply_fusion.20), channel_id=4, replica_groups=mesh['seq'=8,'batch'=4] {'seq'}, dimensions={0}, use_global_device_ids=true | all-gather | bytes 110592 | tf_op jit(solution)/shard_map/all_gather | solution.py:19
  793.2 5.6 while.29
  798.8 3.5 pad.229
  804.4 3.6 pad.228
  811.3 12.9 rev.15
  824.1 12.8 rev.14
  837.0 4.5 fusion.83
  843.2 4.2 fusion.100
  852.6 4.7 fusion.58
  858.4 4.8 fusion.101
  865.4 4.4 collective-permute-done.2
  869.9 4.5 fusion.26
  875.3 3.8 convolution_bitcast_fusion.2
  879.2 6.2 convolution_bitcast_fusion
  885.7 6.1 convolution_bitcast_fusion.1
  892.8 7.8 fusion.102
  900.7 7.8 fusion.103
  909.6 7.8 fusion.104
  921.6 5.8 convolution_add_fusion.6
  929.6 38.5 %all-reduce.64 = (f32[1024]{0:T(1024)S(1)}, f32[1024]{0:T(1024)S(1)}, f32[1536]{0:T(1024)S(1)}, f32[1536]{0:T(1024)S(1)}, f32[1536]{0:T(1024)S(1)}, /*index=5*/f32[1536]{0:T(1024)S(1)}) all-reduce(f32[1024]{0:T(1024)S(1)} %get-tuple-element.251, f32[1024]{0:T(1024)S(1)} %copy-done.88, ...), channel_id=13, replica_groups=mesh['seq'=8,'batch'=4] {'seq','batch'}, use_global_device_ids=true, to_apply=%region_17.18.clone | all-reduce | flops 8192 | bytes 65536
  975.6 91.4 %reduce-scatter.20.cloned.1.call-done = f32[48,1024]{1,0:T(8,128)} async-done(((f32[1536,1024]{1,0:T(8,128)}), f32[48,1024]{1,0:T(8,128)}) %reduce-scatter.20.cloned.1.call-update) | async-done | bytes 196624 | tf_op jit(solution)/shard_map/reduce_scatter | solution.py:246
  1067.1 120.7 %reduce-scatter.12.cloned.1.call-done = f32[32,1536]{1,0:T(8,128)} async-done(((f32[1024,1536]{1,0:T(8,128)}), f32[32,1536]{1,0:T(8,128)}) %reduce-scatter.12.cloned.1.call-update) | async-done | bytes 196624 | tf_op jit(solution)/shard_map/reduce_scatter | solution.py:242
  1187.8 119.7 %reduce-scatter.14.cloned.1.call-done = f32[32,1536]{1,0:T(8,128)} async-done(((f32[1024,1536]{1,0:T(8,128)}), f32[32,1536]{1,0:T(8,128)}) %reduce-scatter.14.cloned.1.call-update) | async-done | bytes 196624 | tf_op jit(solution)/shard_map/reduce_scatter | solution.py:243
  1307.4 142.3 %reduce-scatter.18.cloned.1.call-done = f32[48,1536]{1,0:T(8,128)} async-done(((f32[1536,1536]{1,0:T(8,128)}), f32[48,1536]{1,0:T(8,128)}) %reduce-scatter.18.cloned.1.call-update) | async-done | bytes 294928 | tf_op jit(solution)/shard_map/reduce_scatter | solution.py:245
  1449.8 140.8 %reduce-scatter.16.cloned.1.call-done = f32[48,1536]{1,0:T(8,128)} async-done(((f32[1536,1536]{1,0:T(8,128)}), f32[48,1536]{1,0:T(8,128)}) %reduce-scatter.16.cloned.1.call-update) | async-done | bytes 294928 | tf_op jit(solution)/shard_map/reduce_scatter | solution.py:244
  1590.6 161.9 %reduce-scatter.22.cloned.1.call-done = f32[32,3072]{1,0:T(8,128)} async-done(((f32[1024,3072]{1,0:T(8,128)}), f32[32,3072]{1,0:T(8,128)}) %reduce-scatter.22.cloned.1.call-update) | async-done | bytes 393232 | tf_op jit(solution)/shard_map/reduce_scatter | solution.py:247
  1752.5 161.0 %reduce-scatter.24.cloned.1.call-done = f32[32,3072]{1,0:T(8,128)} async-done(((f32[1024,3072]{1,0:T(8,128)}), f32[32,3072]{1,0:T(8,128)}) %reduce-scatter.24.cloned.1.call-update) | async-done | bytes 393232 | tf_op jit(solution)/shard_map/reduce_scatter | solution.py:248
  1913.5 162.0 %reduce-scatter.26.cloned.1.call-done = f32[96,1024]{1,0:T(8,128)} async-done(((f32[3072,1024]{1,0:T(8,128)}), f32[96,1024]{1,0:T(8,128)}) %reduce-scatter.26.cloned.1.call-update) | async-done | bytes 393232 | tf_op jit(solution)/shard_map/reduce_scatter | solution.py:249
  (503 shorter events, 407.6 us)
Async XLA Ops:
  7.2 13.1 copy-start
  7.2 13.3 copy-start.75
  7.2 13.3 copy-start.71
  7.2 13.4 copy-start.23
  7.2 65.4 %all-gather.12.cloned.1.call-start = ((), (), s32[]{:S(2)}) async-start(), calls=%async_computation.9 | async-start | bytes 3244032 | tf_op jit(solution)/shard_map/all_gather | solution.py:98
  8.0 130.0 %all-gather.16.cloned.1.call-start = ((), (), s32[]{:S(2)}) async-start(), calls=%async_computation.11 | async-start | bytes 4866048 | tf_op jit(solution)/shard_map/all_gather | solution.py:100
  8.7 194.7 %all-gather.14.cloned.1.call-start = ((), (), s32[]{:S(2)}) async-start(), calls=%async_computation.10 | async-start | bytes 4866048 | tf_op jit(solution)/shard_map/all_gather | solution.py:99
  9.5 510.7 %all-gather.18.cloned.1.call-start = ((), (), s32[]{:S(2)}) async-start(), calls=%async_computation.12 | async-start | bytes 3244032 | tf_op jit(solution)/shard_map/all_gather | solution.py:97
  10.0 515.3 %all-gather.20.cloned.1.call-start = ((), (), s32[]{:S(2)}) async-start(), calls=%async_computation.13 | async-start | bytes 3244032 | tf_op jit(solution)/shard_map/all_gather | solution.py:101
  10.6 519.8 %all-gather.22.cloned.1.call-start = ((), (), s32[]{:S(2)}) async-start(), calls=%async_computation.14 | async-start | bytes 6488064 | tf_op jit(solution)/shard_map/all_gather | solution.py:102
  11.2 10.3 copy-start.46
  11.2 525.7 %all-gather.24.cloned.1.call-start = ((), (), s32[]{:S(2)}) async-start(), calls=%async_computation.15 | async-start | bytes 6488064 | tf_op jit(solution)/shard_map/all_gather | solution.py:103
  12.0 531.4 %all-gather.26.cloned.1.call-start = ((), (), s32[]{:S(2)}) async-start(), calls=%async_computation.16 | async-start | bytes 6488064 | tf_op jit(solution)/shard_map/all_gather | solution.py:104
  12.8 66.2 %collective-permute-start.1 = (f32[2,3]{1,0:T(2,128)S(1)}, f32[2,3]{1,0:T(2,128)S(1)}, u32[]{:S(2)}, u32[]{:S(2)}) collective-permute-start(f32[2,3]{1,0:T(2,128)S(1)} %slice.506), channel_id=1, source_target_pairs={{0,4},{4,8},{8,12},{12,16},{16,20},{20,24},{24,28},{1,5},{5,9},{9,... | collective-permute-start | bytes 80 | tf_op jit(solution)/shard_map/ppermute | solution.py:14
  17.6 5.4 collective-permute-start.3
  18.9 955.3 %reduce-scatter.28.cloned.1.call-start = ((), (), s32[]{:S(2)}) async-start(), calls=%async_computation.25 | async-start | bytes 811008
  20.6 60.1 %copy-start.49 = (f32[1536]{0:T(1024)}, f32[1536]{0:T(1024)S(1)}, u32[]{:S(2)}) copy-start(f32[1536]{0:T(1024)S(1)} %get-tuple-element.255) | copy-start | bytes 18436
  20.6 60.1 %copy-start.51 = (f32[1536]{0:T(1024)}, f32[1536]{0:T(1024)S(1)}, u32[]{:S(2)}) copy-start(f32[1536]{0:T(1024)S(1)} %get-tuple-element.256) | copy-start | bytes 18436
  20.6 60.1 %copy-start.53 = (f32[1536]{0:T(1024)}, f32[1536]{0:T(1024)S(1)}, u32[]{:S(2)}) copy-start(f32[1536]{0:T(1024)S(1)} %get-tuple-element.257) | copy-start | bytes 18436
  72.6 8.1 copy-start.83
  75.5 7.4 copy-start.4
  75.6 5.1 collective-permute-start
  79.7 127.7 %copy-start.73 = (f32[2,128]{1,0:T(2,128)}, f32[2,128]{1,0:T(2,128)S(1)}, u32[]{:S(2)}) copy-start(f32[2,128]{1,0:T(2,128)S(1)} %get-tuple-element.368) | copy-start | bytes 3076
  138.0 65.4 %copy-start.90 = (f32[1536]{0:T(1024)S(1)}, f32[1536]{0:T(1024)}, u32[]{:S(2)}) copy-start(f32[1536]{0:T(1024)} %param.36) | copy-start | bytes 18436
  314.5 8.7 copy-start.61
  314.5 8.7 copy-start.62
  314.5 8.7 copy-start.63
  314.5 8.8 copy-start.64
  354.2 7.7 copy-start.58
  359.8 10.1 copy-start.57
  553.2 5.8 copy-start.44
  553.2 5.8 copy-start.43
  553.2 5.8 copy-start.11
  553.2 6.0 copy-start.89
  562.5 5.4 copy-start.8
  652.0 12.0 copy-start.65
  652.0 12.0 copy-start.66
  695.0 7.7 copy-start.60
  700.6 10.1 copy-start.59
  824.1 12.9 copy-start.55
  824.1 12.9 copy-start.74
  837.0 4.5 copy-start.2
  842.0 5.5 copy-start.35
  842.9 4.6 slice-start
  843.2 4.2 copy-start.34
  843.2 4.3 slice-start.1
  852.5 214.5 %reduce-scatter.20.cloned.1.call-start = ((), (), s32[]{:S(2)}) async-start(), calls=%async_computation.21 | async-start | bytes 6488064 | tf_op jit(solution)/shard_map/reduce_scatter | solution.py:246
  857.3 330.4 %reduce-scatter.12.cloned.1.call-start = ((), (), s32[]{:S(2)}) async-start(), calls=%async_computation.17 | async-start | bytes 6488064 | tf_op jit(solution)/shard_map/reduce_scatter | solution.py:242
  863.1 6.7 copy-start.50
  863.1 6.7 copy-start.52
  863.1 6.7 copy-start.54
  863.1 6.7 copy-start.84
  863.2 6.7 copy-start.85
  863.2 6.7 copy-start.86
  863.2 444.2 %reduce-scatter.14.cloned.1.call-start = ((), (), s32[]{:S(2)}) async-start(), calls=%async_computation.18 | async-start | bytes 6488064 | tf_op jit(solution)/shard_map/reduce_scatter | solution.py:243
  864.2 5.7 collective-permute-start.2
  879.1 570.7 %reduce-scatter.18.cloned.1.call-start = ((), (), s32[]{:S(2)}) async-start(), calls=%async_computation.20 | async-start | bytes 9732096 | tf_op jit(solution)/shard_map/reduce_scatter | solution.py:245
  885.4 705.2 %reduce-scatter.16.cloned.1.call-start = ((), (), s32[]{:S(2)}) async-start(), calls=%async_computation.19 | async-start | bytes 9732096 | tf_op jit(solution)/shard_map/reduce_scatter | solution.py:244
  891.8 860.7 %reduce-scatter.22.cloned.1.call-start = ((), (), s32[]{:S(2)}) async-start(), calls=%async_computation.22 | async-start | bytes 12976128 | tf_op jit(solution)/shard_map/reduce_scatter | solution.py:247
  900.7 1012.8 %reduce-scatter.24.cloned.1.call-start = ((), (), s32[]{:S(2)}) async-start(), calls=%async_computation.23 | async-start | bytes 12976128 | tf_op jit(solution)/shard_map/reduce_scatter | solution.py:248
  908.6 1166.9 %reduce-scatter.26.cloned.1.call-start = ((), (), s32[]{:S(2)}) async-start(), calls=%async_computation.24 | async-start | bytes 12976128 | tf_op jit(solution)/shard_map/reduce_scatter | solution.py:249
  921.6 5.8 copy-start.3
  921.6 5.8 copy-start.14
  921.6 5.8 copy-start.78
  (51 other events, 132.3 us)
Sparse Core Ops, SparseCore 0:
  10.9 61.6 all-gather.11
  75.5 62.4 all-gather.15
  140.9 62.4 all-gather.13
  206.1 57.7 all-gather.17
  266.6 57.7 all-gather.19
  327.1 68.3 all-gather.21
  398.3 68.6 all-gather.23
  469.9 67.9 all-gather.25
  852.6 94.9 reduce-scatter.27
  953.7 113.3 reduce-scatter.19
  1074.2 113.5 reduce-scatter.11
  1193.8 113.5 reduce-scatter.13
  1314.9 134.8 reduce-scatter.17
  1456.1 134.4 reduce-scatter.15
  1598.1 154.3 reduce-scatter.21
  1758.9 154.4 reduce-scatter.23
  1920.9 154.4 reduce-scatter.25
where the time goes:
time: 2110 us; the launch traced here: 2080 us
  waiting for transfers between devices  1280 us (61%)
  local copies, waits for them, and re-layouts  365 us (17%)
  other arithmetic  161 us (8%)
  blocking collectives  132 us (6%)
  matrix products  120 us (6%)
    reduce_scatter x1, waiting for transfers between devices, local(): lax.psum_scatter(grad_down, ('seq', 'batch'), scatter_dimension=0, tiled=...  162 us
    reduce_scatter x1, waiting for transfers between devices, local(): lax.psum_scatter(grad_hidden, ('seq', 'batch'), scatter_dimension=0, tile...  162 us
    reduce_scatter x1, waiting for transfers between devices, local(): lax.psum_scatter(grad_upward, ('seq', 'batch'), scatter_dimension=0, tile...  161 us
    reduce_scatter x1, waiting for transfers between devices, local(): lax.psum_scatter(grad_inject, ('seq', 'batch'), scatter_dimension=0, tile...  142 us
    reduce_scatter x1, waiting for transfers between devices, local(): lax.psum_scatter(grad_recur, ('seq', 'batch'), scatter_dimension=0, tiled...  141 us
    slice x49, local copies, waits for them, and re-layouts, local(): lax.associative_scan(combine, (next_mult, grad_states), axis=1, reverse=T...  122 us
    reduce_scatter x1, waiting for transfers between devices, local(): lax.psum_scatter(grad_gate, ('seq', 'batch'), scatter_dimension=0, tiled=...  121 us
    reduce_scatter x1, waiting for transfers between devices, local(): lax.psum_scatter(grad_input, ('seq', 'batch'), scatter_dimension=0, tiled...  120 us
  transfers between devices with their start and end apart: 21, of which 14 were waited for; matrix products, arithmetic and copies ran while one was open for 17% of the time, Pallas kernels for 0%

commit v1 on v0

--- a/solution.py
+++ b/solution.py
@@ -1,11 +1,17 @@
+import functools
+
 import jax
 import jax.numpy as jnp
 from jax import lax
+from jax.experimental import pallas as pl
+from jax.experimental.pallas import tpu as pltpu
 from jax.sharding import PartitionSpec as P
 
 EPSILON = 1e-06
 DECAY_SCALE = 8.0
 FLOOR_TERM = 0.01
+SLOTS = 240
+VMEM_BYTES = 62 << 20
 
 
 def shifted(array, axis, by):
@@ -63,7 +69,7 @@
     return (scaler * (scaled - values * scaler * scaler * inner), grad_gain)
 
 
-def local(
+def gathered_block(
     inputs,
     segments,
     w_gate,
@@ -293,9 +299,1035 @@
     )
 
 
+MESH = pl.DeviceIdType.MESH
+F32, BF16 = (jnp.float32, jnp.bfloat16)
+LANES = 128
+EDGE = 8
+STEP = 32
+DEPTH, PAIR, GROUP = (4, 2, 4)
+RING = DEPTH * PAIR
+
+
+def dot_nn(left, right):
+    return lax.dot_general(left, right, (((1,), (0,)), ((), ())), preferred_element_type=F32)
+
+
+def dot_nt(left, right):
+    return lax.dot_general(left, right, (((1,), (1,)), ((), ())), preferred_element_type=F32)
+
+
+def dot_tn(left, right):
+    return lax.dot_general(left, right, (((0,), (0,)), ((), ())), preferred_element_type=F32)
+
+
+def gelu_parts(value):
+    rate = 0.7978845608028654
+    square = value * value
+    bent = jnp.tanh(rate * (value + 0.044715 * square * value))
+    act = 0.5 * value * (1.0 + bent)
+    slope = 0.5 * (1.0 + bent) + 0.5 * rate * value * (1.0 - bent * bent) * (1.0 + 0.134145 * square)
+    return (act, slope)
+
+
+def at(start, size, of):
+    return pl.ds(pl.multiple_of(start, of), size)
+
+
+def loop(count, body):
+    def turn(i, nothing):
+        body(i)
+        return nothing
+
+    lax.fori_loop(0, count, turn, 0)
+
+
+class Net:
+    def __init__(self, send, recv):
+        self.send, self.recv, self.used, self.open = (send, recv, 0, {})
+
+    def slots(self, count):
+        first = self.used
+        self.used += count
+        return list(range(first, first + count))
+
+    def put(self, src, dst, to, slot, tag=""):
+        copy = pltpu.make_async_remote_copy(
+            src_ref=src,
+            dst_ref=dst,
+            send_sem=self.send.at[slot],
+            recv_sem=self.recv.at[slot],
+            device_id=to,
+            device_id_type=MESH,
+        )
+        copy.start()
+        self.open.setdefault(tag, []).append(copy)
+
+    def got(self, dst, to, slot):
+        pltpu.make_async_remote_copy(
+            src_ref=dst,
+            dst_ref=dst,
+            send_sem=self.send.at[slot],
+            recv_sem=self.recv.at[slot],
+            device_id=to,
+            device_id_type=MESH,
+        ).wait_recv()
+
+    def flush(self, *tags):
+        for tag in tags or list(self.open):
+            for copy in self.open.pop(tag, []):
+                copy.wait_send()
+
+
+def fused(names, *refs):
+    r = dict(zip(names, refs))
+    x, cot, seg, xw, xhu, own_o, own_d, gains, vec = (
+        r[k] for k in ("x", "cot", "seg", "xw", "xhu", "own_o", "own_d", "gains", "vec")
+    )
+    out, gin, fin, fin_hu, g_o, g_d, g_vec = (
+        r[k] for k in ("out", "gin", "fin", "fin_hu", "g_o", "g_d", "g_vec")
+    )
+    w_one, w_ri, w_o, w_hu, w_d = (r[k] for k in ("w_one", "w_ri", "w_o", "w_hu", "w_d"))
+    norm, gout, norm_two, gres, conv, mix = (
+        r[k] for k in ("norm", "gout", "norm_two", "gres", "conv", "mix")
+    )
+    prod, ghu, ggb, gri, part = (r[k] for k in ("prod", "ghu", "ggb", "gri", "part"))
+    brx, tgx, stx, gate_pre, conv_out = (r[k] for k in ("brx", "tgx", "stx", "gate_pre", "conv_out"))
+    rgate, igate, carry, pre = (r[k] for k in ("rgate", "igate", "carry", "pre"))
+    core_in, x_in, pre_f, pre_b = (r[k] for k in ("core_in", "x_in", "pre_f", "pre_b"))
+    acc, gain_acc, vs, vb = (r[k] for k in ("acc", "gain_acc", "vs", "vb"))
+    net = Net(r["send"], r["recv"])
+
+    width = x.shape[1]
+    here = carry.shape[1]
+    chans = carry.shape[2]
+    hid = prod.shape[1]
+    rows = 2 * GROUP
+    half = GROUP * here
+    blk, cblk, fblk = (width // (RING * GROUP), chans // RING, hid // RING)
+    groups = [slice(g * LANES, (g + 1) * LANES) for g in range(chans // LANES)]
+    marks = slice(chans, chans + LANES)
+
+    s = lax.axis_index("seq")
+    b = lax.axis_index("batch")
+    z, y = (s // PAIR, s % PAIR)
+    mate, across, corner = (
+        (b // 2) * 2 + (1 - b % 2),
+        (1 - b // 2) * 2 + b % 2,
+        (1 - b // 2) * 2 + (1 - b % 2),
+    )
+    to_mate, to_across, to_corner = ((s, mate), (s, across), (s, corner))
+    group_peers = [(mate, to_mate), (across, to_across), (corner, to_corner)]
+    to_pair = (z * PAIR + 1 - y, b)
+    far = [lax.rem(z + k, DEPTH) for k in range(DEPTH)]
+    near = [lax.rem(z + DEPTH - k, DEPTH) for k in range(DEPTH)]
+    ring_to = [lax.rem(s + k, RING) for k in range(RING)]
+    ring_from = [lax.rem(s + RING - k, RING) for k in range(RING)]
+
+    barrier = pltpu.get_barrier_semaphore()
+    for _, to in group_peers:
+        pl.semaphore_signal(barrier, inc=1, device_id=to, device_id_type=MESH)
+    for k in range(1, RING):
+        pl.semaphore_signal(barrier, inc=1, device_id=(ring_to[k], b), device_id_type=MESH)
+    pl.semaphore_wait(barrier, 3 + RING - 1)
+
+    class Chunk:
+        pass
+
+    def chunk(block, piece, pieces, y_block, y_piece, z_block, z_piece):
+        c = Chunk()
+        c.block, c.piece, c.pieces = (block, piece, pieces)
+        c.y_block, c.y_piece, c.z_block, c.z_piece = (y_block, y_piece, z_block, z_piece)
+        c.gather_z = net.slots(DEPTH)
+        c.gather_y = net.slots(DEPTH)
+        c.sum_y = net.slots(DEPTH)
+        c.sum_z = net.slots(DEPTH)
+        c.spread = net.slots(3)
+        c.home = net.slots(3)
+        return c
+
+    def flat_chunk(ref, size, step, cols, y_ref, z_ref):
+        def row(base, i):
+            return (at(base * size + i * step, step, 16), cols)
+
+        return chunk(
+            lambda q: ref.at[at(q * size, size, 16), cols],
+            lambda q, i: ref.at[row(q, i)],
+            size // step,
+            lambda q: y_ref.at[at(q * size, size, 16), slice(0, cols.stop - cols.start)],
+            lambda q, i: y_ref.at[at(q * size + i * step, step, 16), slice(0, cols.stop - cols.start)],
+            lambda q: z_ref.at[pl.ds(q * size, size), slice(0, cols.stop - cols.start)],
+            lambda q, i: z_ref.at[at(q * size + i * step, step, 16), slice(0, cols.stop - cols.start)],
+        )
+
+    two = 2 * chans
+    size_one = GROUP * blk
+    one = flat_chunk(
+        w_one, size_one, blk, slice(0, two), norm_two, norm_two.at[pl.ds(DEPTH * size_one, (DEPTH - 1) * size_one)]
+    )
+    ri = chunk(
+        lambda q: w_ri.at[:, q],
+        lambda q, i: w_ri.at[i, q],
+        GROUP,
+        lambda q: r["y_ri"].at[q],
+        lambda q, i: r["y_ri"].at[q, i],
+        lambda q: r["z_ri"].at[q],
+        lambda q, i: r["z_ri"].at[q, i],
+    )
+    wo = flat_chunk(w_o, cblk, 16, slice(0, width), r["y_o"], r["z_o"])
+    hi = flat_chunk(w_hu, size_one, blk, slice(0, hid), r["y_h"], r["z_h"])
+    up = flat_chunk(w_hu, size_one, blk, slice(hid, 2 * hid), r["y_u"], r["z_u"])
+    dn = flat_chunk(w_d, fblk, 16, slice(0, width), r["y_d"], r["z_d"])
+
+    rec = blk + cblk
+    one.source = lambda q: xw.at[at(q * rec, blk, 16)]
+    one.place = lambda q: w_one.at[at(s * size_one + q * blk, blk, 16)]
+    one.result = lambda q: fin.at[at(q * rec, blk, 16)]
+    ri.source = lambda q: xw.at[at(q * rec + blk, cblk, 16)]
+    ri.place = lambda q: w_ri.at[q, s]
+    ri.result = lambda q: fin.at[at(q * rec + blk, cblk, 16)]
+    hi.source = lambda q: xhu.at[at(q * blk, blk, 16), slice(0, hid)]
+    hi.place = lambda q: w_hu.at[at(s * size_one + q * blk, blk, 16), slice(0, hid)]
+    hi.result = lambda q: fin_hu.at[at(q * blk, blk, 16), slice(0, hid)]
+    up.source = lambda q: xhu.at[at(q * blk, blk, 16), slice(hid, 2 * hid)]
+    up.place = lambda q: w_hu.at[at(s * size_one + q * blk, blk, 16), slice(hid, 2 * hid)]
+    up.result = lambda q: fin_hu.at[at(q * blk, blk, 16), slice(hid, 2 * hid)]
+
+    def spread(c):
+        for (peer, to), slot in zip(group_peers, c.spread):
+            net.put(c.source(peer), c.place(b), to, slot)
+        c.place(b)[...] = c.source(b)[...]
+
+    def spread_wait(c):
+        for (peer, to), slot in zip(group_peers, c.spread):
+            net.got(c.place(peer), to, slot)
+
+    def gather(c):
+        for k in (1, 3, 2):
+            net.put(c.block(s), c.block(s), (far[k] * PAIR + y, b), c.gather_z[k])
+        net.put(c.block(s), c.block(s), to_pair, c.gather_y[0])
+
+    def gather_relay(c, k):
+        from_z = near[k] * PAIR + y
+        net.got(c.block(from_z), (from_z, b), c.gather_z[k])
+        net.put(c.block(from_z), c.block(from_z), to_pair, c.gather_y[k])
+
+    def gather_wait(c):
+        for k in range(DEPTH):
+            net.got(c.block(near[k] * PAIR + 1 - y), to_pair, c.gather_y[k])
+
+    def sum_pair(c):
+        for k in (1, 3, 2, 0):
+            net.put(c.block(far[k] * PAIR + 1 - y), c.y_block(far[k]), to_pair, c.sum_y[k])
+
+    def sum_pair_end(c, k):
+        net.got(c.y_block(far[k]), to_pair, c.sum_y[k])
+        mine = far[k] * PAIR + y
+
+        def add(i):
+            total = c.piece(mine, i)[...].astype(F32) + c.y_piece(far[k], i)[...].astype(F32)
+            c.piece(mine, i)[...] = total.astype(BF16)
+
+        loop(c.pieces, add)
+        if k:
+            net.put(c.block(mine), c.z_block(k - 1), (mine, b), c.sum_z[k])
+
+    def sum_end(c, keep):
+        for k in range(1, DEPTH):
+            net.got(c.z_block(k - 1), (near[k] * PAIR + y, b), c.sum_z[k])
+
+        def add(i):
+            total = c.piece(s, i)[...].astype(F32)
+            for k in range(DEPTH - 1):
+                total = total + c.z_piece(k, i)[...].astype(F32)
+            keep(i, total)
+
+        loop(c.pieces, add)
+
+    def sum_end_spread(c):
+        def keep(i, total):
+            c.piece(s, i)[...] = total.astype(BF16)
+
+        sum_end(c, keep)
+        for (peer, to), slot in zip(group_peers, c.home):
+            net.put(c.place(peer), c.result(b), to, slot)
+        c.result(b)[...] = c.place(b)[...]
+
+    def home_wait(c):
+        for (peer, to), slot in zip(group_peers, c.home):
+            net.got(c.result(peer), to, slot)
+
+    def share(view, slots, h):
+        net.put(view(b, h), view(b, h), to_across, slots[3 * h])
+        net.put(view(b, h), view(b, h), to_mate, slots[3 * h + 1])
+
+    def share_relay(view, slots, h):
+        net.got(view(across, h), to_across, slots[3 * h])
+        net.put(view(across, h), view(across, h), to_mate, slots[3 * h + 2])
+
+    def share_end(view, slots, h):
+        net.got(view(mate, h), to_mate, slots[3 * h + 1])
+        net.got(view(corner, h), to_mate, slots[3 * h + 2])
+
+    def token_rows(ref):
+        return lambda q, h: ref.at[at((h * GROUP + q) * here, here, 16)]
+
+    def merge(view, first, slots, h):
+        net.put(view(corner, h), first(h, 1), to_mate, slots[3 * h], "part")
+        net.put(view(mate, h), first(h, 0), to_mate, slots[3 * h + 1], "part")
+
+    def merge_relay(view, first, second, slots, h, parts, tile):
+        net.got(first(h, 1), to_mate, slots[3 * h])
+
+        def add(i):
+            v = tile(view(across, h), i)
+            v[...] = (v[...].astype(F32) + tile(first(h, 1), i)[...].astype(F32)).astype(BF16)
+
+        loop(parts, add)
+        net.put(view(across, h), second(h), to_across, slots[3 * h + 2], "part")
+
+    def merge_end(first, second, slots, h):
+        net.got(first(h, 0), to_mate, slots[3 * h + 1])
+        net.got(second(h), to_across, slots[3 * h + 2])
+
+    def sixteen(ref, i):
+        return ref.at[at(i * 16, 16, 16)]
+
+    first_in = lambda h, slot: core_in.at[h, slot]
+    second_in = lambda h: x_in.at[h]
+    part_rows = token_rows(part)
+
+    def merged(h, i):
+        total = sixteen(part_rows(b, h), i)[...].astype(F32)
+        return total + core_in[h, 0, at(i * 16, 16, 16)].astype(F32) + x_in[h, at(i * 16, 16, 16)].astype(F32)
+
+    def own(ref, h, i):
+        return ref.at[at(h * here + i * 16, 16, 16)]
+
+    tiles16 = here // 16
+    gain_one, gain_two = (gains[0:1], gains[1:2])
+
+    def rms(values):
+        return lax.rsqrt(jnp.mean(values * values, axis=-1, keepdims=True) + EPSILON)
+
+    def norm_grad(index, values, incoming, gain):
+        scaler = rms(values)
+        scaled = incoming * gain
+        inner = jnp.mean(scaled * values, axis=-1, keepdims=True)
+        term = incoming * values * scaler
+        gain_acc[index] += term[0:8] + term[8:16]
+        return scaler * (scaled - values * (scaler * scaler * inner))
+
+    def over(h, body):
+        def row(i):
+            q = h * GROUP + i
+            for start in range(0, here, STEP):
+                for g, lanes in enumerate(groups):
+                    body(q, start, lanes, g)
+
+        loop(GROUP, row)
+
+    def flat(q, start):
+        return at(q * here + start, STEP, STEP)
+
+    def add_to(index, lanes, values):
+        total = values[0:8]
+        for k in range(8, STEP, 8):
+            total = total + values[k : k + 8]
+        acc[index, :, lanes] += total
+
+    def same(q, start, k):
+        now = brx[q, pl.ds(EDGE + start, STEP), marks]
+        return (now == brx[q, pl.ds(EDGE + start - k, STEP), marks]).astype(F32)
+
+    spread(one)
+    acc[...] = jnp.zeros_like(acc)
+    gain_acc[...] = jnp.zeros_like(gain_acc)
+    norm_slots, gout_slots, conv_slots = (net.slots(6), net.slots(6), net.slots(6))
+    two_slots, gres_slots = (net.slots(6), net.slots(6))
+    out_slots, gnt_slots, down_slots, thru_slots, gn_slots = (net.slots(6) for _ in range(5))
+    halo_slot, halo_back = net.slots(2)
+    pre_slots, back_slots, vec_slots, last_slots = (
+        net.slots(RING),
+        net.slots(RING),
+        net.slots(RING),
+        net.slots(3),
+    )
+    norm_rows, gout_rows, two_rows, gres_rows = (token_rows(ref) for ref in (norm, gout, norm_two, gres))
+
+    for h in range(2):
+        def norm_tile(i, h=h):
+            v = own(x, h, i)[...]
+            sixteen(norm_rows(b, h), i)[:, 0:width] = (v * rms(v) * gain_one).astype(BF16)
+            sixteen(norm_rows(b, h), i)[:, width : width + LANES] = own(seg, h, i)[...]
+
+        loop(tiles16, norm_tile)
+        share(norm_rows, norm_slots, h)
+    spread(ri)
+    spread(hi)
+    spread(up)
+    w_o[at(s * cblk, cblk, 16), :] = own_o[...]
+    w_d[at(s * fblk, fblk, 16), :] = own_d[...]
+    spread_wait(one)
+    gather(one)
+    gather(wo)
+    for h in range(2):
+        share_relay(norm_rows, norm_slots, h)
+
+    for h in range(2):
+        def low_tile(i, h=h):
+            sixteen(gout_rows(b, h), i)[...] = own(cot, h, i)[...].astype(BF16)
+
+        loop(tiles16, low_tile)
+
+    @pl.when(s == 0)
+    def _():
+        brx[:, 0:EDGE, :] = jnp.full((rows, EDGE, chans + LANES), -1.0, F32)
+
+    @pl.when(s == RING - 1)
+    def _():
+        tgx[:, here : here + EDGE, :] = jnp.full((rows, EDGE, chans + LANES), -1.0, F32)
+
+    for k in (1, 3, 2):
+        gather_relay(one, k)
+    gather_wait(one)
+
+    for h in range(2):
+        share_end(norm_rows, norm_slots, h)
+
+        def first_mm(i, h=h):
+            q = h * GROUP + i
+            span = at(q * here, here, 16)
+            got = dot_nn(norm[span, 0:width], w_one[...])
+            gate_pre[q] = got[:, 0:chans]
+            brx[q, EDGE : EDGE + here, 0:chans] = got[:, chans:two]
+            ids = norm[span, width : width + LANES].astype(F32)
+            brx[q, EDGE : EDGE + here, marks] = ids
+            tgx[q, 0:here, marks] = ids
+
+        loop(GROUP, first_mm)
+
+    def halo_out():
+        return pltpu.make_async_remote_copy(
+            src_ref=brx.at[:, pl.ds(here, EDGE)],
+            dst_ref=brx.at[:, pl.ds(0, EDGE)],
+            send_sem=net.send.at[halo_slot],
+            recv_sem=net.recv.at[halo_slot],
+            device_id=(ring_to[1], b),
+            device_id_type=MESH,
+        )
+
+    @pl.when(s < RING - 1)
+    def _():
+        halo_out().start()
+
+    spread_wait(ri)
+    gather(ri)
+    for k in (1, 3, 2):
+        gather_relay(wo, k)
+
+    @pl.when(s > 0)
+    def _():
+        net.got(brx.at[:, pl.ds(0, EDGE)], (ring_from[1], b), halo_slot)
+
+    conv_cols = lambda q, h: conv.at[pl.ds(h * half, half), at(q * chans, chans, LANES)]
+    for h in range(2):
+        def conv_tile(q, start, lanes, g):
+            total = vec[4:5, lanes] + vec[0:1, lanes] * brx[q, pl.ds(EDGE + start, STEP), lanes]
+            for k in range(1, 4):
+                lag = brx[q, pl.ds(EDGE + start - k, STEP), lanes]
+                total = total + vec[k : k + 1, lanes] * lag * same(q, start, k)
+            conv_out[q, pl.ds(start, STEP), lanes] = total
+            conv[flat(q, start), at(b * chans + g * LANES, LANES, LANES)] = total.astype(BF16)
+
+        over(h, conv_tile)
+        share(conv_cols, conv_slots, h)
+    for h in range(2):
+        share(gout_rows, gout_slots, h)
+    for h in range(2):
+        share_relay(conv_cols, conv_slots, h)
+    for k in (1, 3, 2):
+        gather_relay(ri, k)
+    spread_wait(hi)
+    gather(hi)
+    gather_wait(ri)
+
+    for h in range(2):
+        share_end(conv_cols, conv_slots, h)
+
+        def gate_mm(i, h=h):
+            q = h * GROUP + i
+            got = dot_nn(conv[at(q * here, here, 16), :], w_ri[...].reshape(GROUP * chans, two))
+            rgate[q] = got[:, 0:chans]
+            igate[q] = got[:, chans:two]
+
+        loop(GROUP, gate_mm)
+
+        def gate_tile(q, start, lanes, g):
+            span = pl.ds(start, STEP)
+            rg = jax.nn.sigmoid(rgate[q, span, lanes] + vec[5:6, lanes])
+            ig = jax.nn.sigmoid(igate[q, span, lanes] + vec[6:7, lanes])
+            rgate[q, span, lanes] = rg
+            igate[q, span, lanes] = ig
+            decay = jnp.exp(rg * vec[7:8, lanes])
+            carry[q, span, lanes] = decay * same(q, start, 1)
+            scale = jnp.sqrt(1.0 - decay * decay + FLOOR_TERM)
+            stx[q, pl.ds(EDGE + start, STEP), lanes] = scale * ig * conv_out[q, span, lanes]
+
+        over(h, gate_tile)
+
+    def ends(p, state):
+        mult = carry[:, p, :]
+        return (state[0] * mult, mult * state[1] + stx[:, EDGE + p, :])
+
+    begin = (jnp.ones((rows, chans), F32), jnp.zeros((rows, chans), F32))
+    product, tail = lax.fori_loop(0, here, ends, begin, unroll=8)
+    pre_f[s, 0:rows] = product
+    pre_f[s, rows : 2 * rows] = tail
+    for k in range(1, RING):
+        net.put(pre_f.at[s], pre_f.at[s], (ring_to[k], b), pre_slots[k])
+    for k in (1, 3, 2):
+        gather_relay(hi, k)
+    spread_wait(up)
+    gather(up)
+    for h in range(2):
+        share_relay(gout_rows, gout_slots, h)
+    for k in range(1, RING):
+        net.got(pre_f.at[ring_from[k]], (ring_from[k], b), pre_slots[k])
+    state = jnp.zeros((rows, chans), F32)
+    for q in range(RING - 1):
+        state = jnp.where(q < s, pre_f[q, rows : 2 * rows] + pre_f[q, 0:rows] * state, state)
+    stx[:, EDGE - 1, :] = state
+
+    def scan(p, state):
+        state = carry[:, p, :] * state + stx[:, EDGE + p, :]
+        stx[:, EDGE + p, :] = state
+        return state
+
+    lax.fori_loop(0, here, scan, state, unroll=8)
+    gather_wait(wo)
+
+    for h in range(2):
+        def mix_tile(q, start, lanes, g):
+            act, _ = gelu_parts(gate_pre[q, pl.ds(start, STEP), lanes])
+            mix[flat(q, start), lanes] = (stx[q, pl.ds(EDGE + start, STEP), lanes] * act).astype(BF16)
+
+        over(h, mix_tile)
+
+        def out_mm(i, h=h):
+            span = at((h * GROUP + i) * here, here, 16)
+            part[span, :] = dot_nn(mix[span, :], w_o[...]).astype(BF16)
+
+        loop(GROUP, out_mm)
+        merge(part_rows, first_in, out_slots, h)
+    for h in range(2):
+        merge_relay(part_rows, first_in, second_in, out_slots, h, tiles16, sixteen)
+    for k in (1, 3, 2):
+        gather_relay(up, k)
+    gather(dn)
+    for h in range(2):
+        merge_end(first_in, second_in, out_slots, h)
+
+        def resid_tile(i, h=h):
+            v = own(x, h, i)[...] + merged(h, i)
+            own(out, h, i)[...] = v
+            sixteen(two_rows(b, h), i)[...] = (v * rms(v) * gain_two).astype(BF16)
+
+        loop(tiles16, resid_tile)
+        share(two_rows, two_slots, h)
+    for h in range(2):
+        share_relay(two_rows, two_slots, h)
+    gather_wait(hi)
+    gather_wait(up)
+
+    for h in range(2):
+        share_end(two_rows, two_slots, h)
+
+        def hidden_mm(i, h=h):
+            span = at((h * GROUP + i) * here, here, 16)
+            pre[...] = dot_nn(norm_two[span, :], w_hu[...])
+
+            def tile(t):
+                rows_t = at(t * 16, 16, 16)
+                flat_t = at((h * GROUP + i) * here + t * 16, 16, 16)
+                for g in range(hid // LANES):
+                    lanes = slice(g * LANES, (g + 1) * LANES)
+                    right = slice(hid + g * LANES, hid + (g + 1) * LANES)
+                    act, slope = gelu_parts(pre[rows_t, lanes])
+                    upward = pre[rows_t, right]
+                    prod[flat_t, lanes] = (act * upward).astype(BF16)
+                    ghu[flat_t, lanes] = (upward * slope).astype(BF16)
+                    ghu[flat_t, right] = act.astype(BF16)
+
+            loop(tiles16, tile)
+
+        loop(GROUP, hidden_mm)
+    for k in (1, 3, 2):
+        gather_relay(dn, k)
+    gather_wait(dn)
+
+    net.flush()
+    for h in range(2):
+        share_end(gout_rows, gout_slots, h)
+
+        def down_back(i, h=h):
+            span = at((h * GROUP + i) * here, here, 16)
+            back = dot_nt(gout[span, :], w_d[...])
+            ghu[span, 0:hid] = (back * ghu[span, 0:hid].astype(F32)).astype(BF16)
+            ghu[span, hid : 2 * hid] = (back * ghu[span, hid : 2 * hid].astype(F32)).astype(BF16)
+            part[span, :] = dot_nt(ghu[span, :], w_hu[...]).astype(BF16)
+
+        loop(GROUP, down_back)
+        merge(part_rows, first_in, gnt_slots, h)
+    for h in range(2):
+        merge_relay(part_rows, first_in, second_in, gnt_slots, h, tiles16, sixteen)
+
+    def grad_hu(i):
+        cols = at(i * 256, 256, LANES)
+        w_hu[at(i * 256, 256, 16), :] = dot_tn(norm_two[:, cols], ghu[...]).astype(BF16)
+
+    loop(width // 256, grad_hu)
+    sum_pair(hi)
+    for h in range(2):
+        merge_end(first_in, second_in, gnt_slots, h)
+
+        def second_norm(i, h=h):
+            back = norm_grad(1, own(out, h, i)[...], merged(h, i), gain_two)
+            own(gin, h, i)[...] = own(cot, h, i)[...] + back
+
+        loop(tiles16, second_norm)
+
+    for h in range(2):
+        def low_resid(i, h=h):
+            sixteen(gres_rows(b, h), i)[...] = own(gin, h, i)[...].astype(BF16)
+
+        loop(tiles16, low_resid)
+        share(gres_rows, gres_slots, h)
+    net.flush("part")
+
+    def down_mm(i):
+        span = at(i * here, here, 16)
+        part[span, :] = dot_nn(prod[span, :], w_d[...]).astype(BF16)
+
+    loop(rows, down_mm)
+    for h in range(2):
+        share_relay(gres_rows, gres_slots, h)
+
+    def grad_down(i):
+        cols = at(i * 256, 256, LANES)
+        w_d[at(i * 256, 256, 16), :] = dot_tn(prod[:, cols], gout[...]).astype(BF16)
+
+    loop(hid // 256, grad_down)
+    sum_pair(dn)
+
+    for h in range(2):
+        share_end(gres_rows, gres_slots, h)
+
+        def out_back(i, h=h):
+            q = h * GROUP + i
+            tgx[q, 0:here, 0:chans] = dot_nt(gres[at(q * here, here, 16), :], w_o[...])
+
+        loop(GROUP, out_back)
+
+        def mix_back(q, start, lanes, g):
+            span = pl.ds(start, STEP)
+            act, slope = gelu_parts(gate_pre[q, span, lanes])
+            back = tgx[q, span, lanes]
+            states = stx[q, pl.ds(EDGE + start, STEP), lanes]
+            ggb[flat(q, start), lanes] = (back * states * slope).astype(BF16)
+            tgx[q, span, lanes] = back * act
+
+        over(h, mix_back)
+
+    def ends_back(i, state):
+        p = here - 1 - i
+        mult = carry[:, p, :]
+        return (state[0] * mult, mult * (tgx[:, p, 0:chans] + state[1]))
+
+    product, tail = lax.fori_loop(0, here, ends_back, begin, unroll=8)
+    pre_b[s, 0:rows] = product
+    pre_b[s, rows : 2 * rows] = tail
+    for k in range(1, RING):
+        net.put(pre_b.at[s], pre_b.at[s], (ring_to[k], b), back_slots[k])
+
+    for h in range(2):
+        merge(part_rows, first_in, down_slots, h)
+
+    w_o[...] = dot_tn(mix[...], gres[...]).astype(BF16)
+    for h in range(2):
+        merge_relay(part_rows, first_in, second_in, down_slots, h, tiles16, sixteen)
+
+    for k in range(1, RING):
+        net.got(pre_b.at[ring_from[k]], (ring_from[k], b), back_slots[k])
+    state = jnp.zeros((rows, chans), F32)
+    for q in range(RING - 1, 0, -1):
+        state = jnp.where(q > s, pre_b[q, rows : 2 * rows] + pre_b[q, 0:rows] * state, state)
+
+    def scan_back(i, state):
+        p = here - 1 - i
+        total = tgx[:, p, 0:chans] + state
+        tgx[:, p, 0:chans] = total
+        return carry[:, p, :] * total
+
+    lax.fori_loop(0, here, scan_back, state, unroll=8)
+
+    for h in range(2):
+        merge_end(first_in, second_in, down_slots, h)
+
+        def out_tile(i, h=h):
+            own(out, h, i)[...] = own(out, h, i)[...] + merged(h, i)
+
+        loop(tiles16, out_tile)
+
+    thru_cols = lambda q, h: ghu.at[pl.ds(h * half, half), at(q * chans, chans, LANES)]
+    thru_first = lambda h, slot: prod.at[pl.ds(h * half, half), pl.ds(slot * chans, chans)]
+    thru_second = lambda h: gout.at[pl.ds(h * half, half), pl.ds(0, chans)]
+    for h in range(2):
+        def gates_back(q, start, lanes, g):
+            span = pl.ds(start, STEP)
+            total = tgx[q, span, lanes]
+            rg, ig, co = (rgate[q, span, lanes], igate[q, span, lanes], conv_out[q, span, lanes])
+            before = stx[q, pl.ds(EDGE + start - 1, STEP), lanes]
+            rate = vec[7:8, lanes]
+            decay = jnp.exp(rg * rate)
+            scale = jnp.sqrt(1.0 - decay * decay + FLOOR_TERM)
+            grad_decay = total * before * same(q, start, 1) - total * ig * co * decay / scale
+            grad_log = grad_decay * decay
+            grad_rg = grad_log * rate * rg * (1.0 - rg)
+            scaled = total * scale
+            grad_ig = scaled * co * ig * (1.0 - ig)
+            tgx[q, span, lanes] = scaled * ig
+            gri[flat(q, start), lanes] = grad_rg.astype(BF16)
+            gri[flat(q, start), slice(chans + g * LANES, chans + (g + 1) * LANES)] = grad_ig.astype(BF16)
+            add_to(5, lanes, grad_rg)
+            add_to(6, lanes, grad_ig)
+            add_to(7, lanes, grad_log * (-DECAY_SCALE * rg))
+
+        over(h, gates_back)
+
+        def thru_mm(i, h=h):
+            span = at((h * GROUP + i) * here, here, 16)
+            got = dot_nt(gri[span, :], w_ri[...].reshape(GROUP * chans, two))
+            ghu[span, :] = got.astype(BF16)
+
+        loop(GROUP, thru_mm)
+        merge(thru_cols, thru_first, thru_slots, h)
+    for h in range(2):
+        merge_relay(thru_cols, thru_first, thru_second, thru_slots, h, half // 16, sixteen)
+
+    def grad_ri(i):
+        got = dot_tn(conv[:, at(i * chans, chans, LANES)], gri[...])
+        w_ri[i] = got.astype(BF16).reshape(RING, cblk, two)
+
+    loop(GROUP, grad_ri)
+    for k in (1, 3, 2, 0):
+        sum_pair_end(hi, k)
+    for k in (1, 3, 2, 0):
+        sum_pair_end(dn, k)
+    sum_pair(up)
+
+    for h in range(2):
+        merge_end(thru_first, thru_second, thru_slots, h)
+
+        def conv_grad(q, start, lanes, g, h=h):
+            span = flat(q, start)
+            total = ghu[span, at(b * chans + g * LANES, LANES, LANES)].astype(F32)
+            total = total + prod[span, lanes].astype(F32) + gout[span, lanes].astype(F32)
+            tgx[q, pl.ds(start, STEP), lanes] += total
+
+        over(h, conv_grad)
+
+    def halo_in():
+        return pltpu.make_async_remote_copy(
+            src_ref=tgx.at[:, pl.ds(0, EDGE)],
+            dst_ref=tgx.at[:, pl.ds(here, EDGE)],
+            send_sem=net.send.at[halo_back],
+            recv_sem=net.recv.at[halo_back],
+            device_id=(ring_from[1], b),
+            device_id_type=MESH,
+        )
+
+    @pl.when(s > 0)
+    def _():
+        halo_in().start()
+
+    sum_pair(wo)
+    sum_pair(ri)
+
+    @pl.when(s < RING - 1)
+    def _():
+        net.got(tgx.at[:, pl.ds(here, EDGE)], (ring_to[1], b), halo_back)
+
+    net.flush("part")
+    for h in range(2):
+        def conv_back(q, start, lanes, g):
+            now = tgx[q, pl.ds(start, STEP), lanes]
+            ids = tgx[q, pl.ds(start, STEP), marks]
+            total = vec[0:1, lanes] * now
+            add_to(4, lanes, now)
+            add_to(0, lanes, now * brx[q, pl.ds(EDGE + start, STEP), lanes])
+            for k in range(1, 4):
+                later = pl.ds(start + k, STEP)
+                match = (tgx[q, later, marks] == ids).astype(F32)
+                total = total + vec[k : k + 1, lanes] * tgx[q, later, lanes] * match
+                lag = brx[q, pl.ds(EDGE + start - k, STEP), lanes]
+                add_to(k, lanes, now * lag * same(q, start, k))
+            ggb[flat(q, start), slice(chans + g * LANES, chans + (g + 1) * LANES)] = total.astype(BF16)
+
+        over(h, conv_back)
+
+        def first_back(i, h=h):
+            span = at((h * GROUP + i) * here, here, 16)
+            part[span, :] = dot_nt(ggb[span, :], w_one[...]).astype(BF16)
+
+        loop(GROUP, first_back)
+        merge(part_rows, first_in, gn_slots, h)
+    for h in range(2):
+        merge_relay(part_rows, first_in, second_in, gn_slots, h, tiles16, sixteen)
+
+    def grad_one(i):
+        cols = at(i * 256, 256, LANES)
+        w_one[at(i * 256, 256, 16), :] = dot_tn(norm[:, cols], ggb[...]).astype(BF16)
+
+    loop(width // 256, grad_one)
+    sum_pair(one)
+    for c in (up, wo, ri):
+        for k in (1, 3, 2, 0):
+            sum_pair_end(c, k)
+
+    for h in range(2):
+        merge_end(first_in, second_in, gn_slots, h)
+
+        def first_norm(i, h=h):
+            back = norm_grad(0, own(x, h, i)[...], merged(h, i), gain_one)
+            own(gin, h, i)[...] = own(gin, h, i)[...] + back
+
+        loop(tiles16, first_norm)
+
+    for k in range(8):
+        vs[s, k : k + 1, 0:chans] = jnp.sum(acc[k], axis=0, keepdims=True)
+    piece = width // 4
+    for k in range(2):
+        total = jnp.sum(gain_acc[k], axis=0, keepdims=True)
+        for j in range(4):
+            vs[s, 4 * k + j : 4 * k + j + 1, chans : chans + piece] = total[:, j * piece : (j + 1) * piece]
+    for k in range(1, RING):
+        net.put(vs.at[s], vs.at[s], (ring_to[k], b), vec_slots[k])
+
+    for k in (1, 3, 2, 0):
+        sum_pair_end(one, k)
+
+    def keep_down(i, total):
+        g_d[at(i * 16, 16, 16), :] = total
+
+    def keep_out(i, total):
+        g_o[at(i * 16, 16, 16), :] = total
+
+    sum_end(dn, keep_down)
+    sum_end_spread(hi)
+    sum_end_spread(up)
+    sum_end(wo, keep_out)
+    for k in range(1, RING):
+        net.got(vs.at[ring_from[k]], (ring_from[k], b), vec_slots[k])
+    total = vs[0]
+    for q in range(1, RING):
+        total = total + vs[q]
+    vb[b] = total
+    for (peer, to), slot in zip(group_peers, last_slots):
+        net.put(vb.at[b], vb.at[b], to, slot)
+    sum_end_spread(ri)
+    sum_end_spread(one)
+    for (peer, to), slot in zip(group_peers, last_slots):
+        net.got(vb.at[peer], to, slot)
+    g_vec[:, 0:chans] = total[:, 0:chans]
+    summed = vb[0, :, chans : chans + piece]
+    for q in range(1, GROUP):
+        summed = summed + vb[q, :, chans : chans + piece]
+    g_vec[:, chans : chans + piece] = summed
+    for c in (hi, up, ri, one):
+        home_wait(c)
+    net.flush()
+
+    @pl.when(s < RING - 1)
+    def _():
+        halo_out().wait_send()
+
+    @pl.when(s > 0)
+    def _():
+        halo_in().wait_send()
+
+
+def by_member(array, parts):
+    lead = array.shape[:-1]
+    split = array.reshape(*lead, RING, GROUP, parts)
+    return jnp.moveaxis(split, -2, 0).reshape(GROUP, *lead, RING * parts)
+
+
+def from_members(array, parts):
+    members, count, _ = array.shape
+    split = array.reshape(members, count, RING, parts)
+    return jnp.moveaxis(split, 0, 2).reshape(count, RING * members * parts)
+
+
+def split_block(
+    inputs,
+    segments,
+    w_gate,
+    w_input,
+    w_recur,
+    w_inject,
+    w_output,
+    w_hidden,
+    w_upward,
+    w_down,
+    gain_one,
+    gain_two,
+    conv_taps,
+    conv_bias,
+    recur_bias,
+    inject_bias,
+    decay_param,
+    cotangent,
+):
+    count, here, width = inputs.shape
+    channels = w_gate.shape[1]
+    chans, hid = (channels // GROUP, w_hidden.shape[1] // GROUP)
+    blk, cblk, fblk = (w_gate.shape[0], w_recur.shape[0], w_down.shape[0])
+    tokens = GROUP * count * here
+    rows = GROUP * count
+    s, b = (lax.axis_index("seq"), lax.axis_index("batch"))
+    ids = jnp.broadcast_to(
+        segments.astype(BF16).reshape(count * here, 1), (count * here, LANES)
+    )
+    first = jnp.concatenate([w_gate, w_recur], axis=0)
+    second = jnp.concatenate([w_input, w_inject], axis=0)
+    xw = jnp.concatenate([by_member(first, cblk), by_member(second, cblk)], axis=-1)
+    xhu = jnp.concatenate([by_member(w_hidden, fblk), by_member(w_upward, fblk)], axis=-1)
+    rate = -DECAY_SCALE * jax.nn.softplus(decay_param)
+    vectors = jnp.concatenate(
+        [conv_taps, jnp.stack([conv_bias, recur_bias, inject_bias, rate])], axis=0
+    ).reshape(8, RING, GROUP, cblk)
+    vec = lax.dynamic_index_in_dim(vectors, b, axis=2, keepdims=False).reshape(8, chans)
+    gains = jnp.stack([gain_one, gain_two])
+
+    wide = chans + LANES
+    size_one = GROUP * blk
+    operands = {
+        "x": inputs.reshape(count * here, width),
+        "cot": cotangent.reshape(count * here, width),
+        "seg": ids,
+        "xw": xw.reshape(GROUP * (blk + cblk), 2 * chans),
+        "xhu": xhu.reshape(GROUP * blk, 2 * hid),
+        "own_o": w_output,
+        "own_d": w_down,
+        "gains": gains,
+        "vec": vec,
+    }
+    piece = width // 4
+    outputs = {
+        "out": ((count * here, width), F32),
+        "gin": ((count * here, width), F32),
+        "fin": ((GROUP * (blk + cblk), 2 * chans), BF16),
+        "fin_hu": ((GROUP * blk, 2 * hid), BF16),
+        "g_o": ((cblk, width), F32),
+        "g_d": ((fblk, width), F32),
+        "g_vec": ((8, chans + piece), F32),
+    }
+    scratch = {
+        "w_one": ((width, 2 * chans), BF16),
+        "w_ri": ((GROUP, RING, cblk, 2 * chans), BF16),
+        "w_o": ((chans, width), BF16),
+        "w_hu": ((width, 2 * hid), BF16),
+        "w_d": ((hid, width), BF16),
+        "norm": ((tokens, width + LANES), BF16),
+        "gout": ((tokens, width), BF16),
+        "norm_two": ((tokens, width), BF16),
+        "gres": ((tokens, width), BF16),
+        "conv": ((tokens, channels), BF16),
+        "mix": ((tokens, chans), BF16),
+        "prod": ((tokens, hid), BF16),
+        "ghu": ((tokens, 2 * hid), BF16),
+        "ggb": ((tokens, 2 * chans), BF16),
+        "gri": ((tokens, 2 * chans), BF16),
+        "part": ((tokens, width), BF16),
+        "brx": ((rows, EDGE + here, wide), F32),
+        "tgx": ((rows, here + EDGE, wide), F32),
+        "stx": ((rows, EDGE + here, chans), F32),
+        "gate_pre": ((rows, here, chans), F32),
+        "conv_out": ((rows, here, chans), F32),
+        "rgate": ((rows, here, chans), F32),
+        "igate": ((rows, here, chans), F32),
+        "carry": ((rows, here, chans), F32),
+        "pre": ((here, 2 * hid), F32),
+        "core_in": ((2, 2, here, width), BF16),
+        "x_in": ((2, here, width), BF16),
+        "pre_f": ((RING, 2 * rows, chans), F32),
+        "pre_b": ((RING, 2 * rows, chans), F32),
+        "y_ri": ((DEPTH, GROUP, cblk, 2 * chans), BF16),
+        "z_ri": ((DEPTH - 1, GROUP, cblk, 2 * chans), BF16),
+        "y_o": ((DEPTH * cblk, width), BF16),
+        "z_o": (((DEPTH - 1) * cblk, width), BF16),
+        "y_h": ((DEPTH * size_one, hid), BF16),
+        "z_h": (((DEPTH - 1) * size_one, hid), BF16),
+        "y_u": ((DEPTH * size_one, hid), BF16),
+        "z_u": (((DEPTH - 1) * size_one, hid), BF16),
+        "y_d": ((DEPTH * fblk, width), BF16),
+        "z_d": (((DEPTH - 1) * fblk, width), BF16),
+        "acc": ((8, 8, chans), F32),
+        "gain_acc": ((2, 8, width), F32),
+        "vs": ((RING, 8, chans + piece), F32),
+        "vb": ((GROUP, 8, chans + piece), F32),
+    }
+    names = [*operands, *outputs, *scratch, "send", "recv"]
+    in_vmem = pl.BlockSpec(memory_space=pltpu.VMEM)
+    got = pl.pallas_call(
+        functools.partial(fused, names),
+        out_shape=[jax.ShapeDtypeStruct(shape, kind) for shape, kind in outputs.values()],
+        in_specs=[in_vmem] * len(operands),
+        out_specs=[in_vmem] * len(outputs),
+        scratch_shapes=[pltpu.VMEM(shape, kind) for shape, kind in scratch.values()]
+        + [pltpu.SemaphoreType.DMA((SLOTS,))] * 2,
+        compiler_params=pltpu.CompilerParams(
+            collective_id=0, has_side_effects=True, vmem_limit_bytes=VMEM_BYTES
+        ),
+        name="block",
+    )(*operands.values())
+    out, gin, fin, fin_hu, g_o, g_d, g_vec = got
+    fin = fin.reshape(GROUP, blk + cblk, 2 * chans)
+    fin_hu = fin_hu.reshape(GROUP, blk, 2 * hid)
+    first = from_members(fin[:, :, :chans], cblk).astype(F32)
+    second = from_members(fin[:, :, chans:], cblk).astype(F32)
+    hidden = from_members(fin_hu[:, :, :hid], fblk).astype(F32)
+    upward = from_members(fin_hu[:, :, hid:], fblk).astype(F32)
+    mine = lax.dynamic_slice_in_dim(g_vec, s * cblk, cblk, axis=1)
+    place = s * GROUP + b
+    gain_sums = g_vec[:, chans:].reshape(2, width)
+    gain_mine = lax.dynamic_slice_in_dim(gain_sums, place * blk, blk, axis=1)
+    slope = jax.nn.sigmoid(lax.dynamic_slice_in_dim(decay_param, place * cblk, cblk))
+    return (
+        out.reshape(count, here, width),
+        gin.reshape(count, here, width),
+        first[:blk],
+        second[:blk],
+        first[blk:],
+        second[blk:],
+        g_o,
+        hidden,
+        upward,
+        g_d,
+        gain_mine[0],
+        gain_mine[1],
+        mine[0:4],
+        mine[4],
+        mine[5],
+        mine[6],
+        mine[7] * slope,
+    )
+
+
 def solution(mesh):
+    fits = dict(mesh.shape) == {"seq": RING, "batch": GROUP}
     return jax.shard_map(
-        local,
+        split_block if fits else gathered_block,
         mesh=mesh,
         in_specs=(
             P("batch", "seq", None),

time: 2110 us -> 390 us (0.18); the launches traced: 2080 us -> 388 us
  waiting for transfers between devices: 1280 us -> 0 us
  Pallas kernels: 0 us -> 352 us
  local copies, waits for them, and re-layouts: 365 us -> 31.6 us
  other arithmetic: 161 us -> 3.44 us
  blocking collectives: 132 us -> 0 us
  matrix products: 120 us -> 0 us
    reduce_scatter x8 -> x0, waiting for transfers between devices: 1100 us -> none  [the longest x1 162 us: local(): lax.psum_scatter(grad_down, ('seq', 'batch'), scatter_dimension=0, tiled=...]
    pallas_call x0 -> x1, Pallas kernels: none -> 352 us  [split_block(): pl.pallas_call(functools.partial(fused, names), out_shape=[jax.ShapeDtype...]
    slice x98 -> x13, local copies, waits for them, and re-layouts: 208 us -> 10.3 us  [the longest x3 2.57 us: split_block(): first[blk:]]
    all_gather x8 -> x0, waiting for transfers between devices: 166 us -> none  [the longest x1 61.6 us: local(): lax.all_gather(w_recur, ('seq', 'batch'), axis=0, tiled=True)]
    dot_general x24 -> x0, matrix products: 120 us -> none  [the longest x8 49 us: matmul_tleft(): jnp.einsum('ta,tb->ab', left, right, preferred_element_type=jnp.float32)]
    pad x48 -> x0, local copies, waits for them, and re-layouts: 107 us -> none  [the longest x24 53.7 us: local(): lax.associative_scan(combine, (next_mult, grad_states), axis=1, reverse=T...]
    all_gather x3 -> x0, blocking collectives: 93.9 us -> none  [prefix(): pieces = jax.tree.map(lambda part: lax.all_gather(part, axis), value)]
    add x42 -> x0, other arithmetic: 74.7 us -> none  [the longest x14 25.3 us: local(): lax.associative_scan(combine, (next_mult, grad_states), axis=1, reverse=T...]
  transfers between devices with their start and end apart: 21 -> 0, of which waited for: 14 -> 0; matrix products, arithmetic and copies ran while one was open for 17% -> 0% of each run, Pallas kernels for 0% -> 0%
where the time goes in v1:
time: 390 us; the launch traced here: 388 us
  Pallas kernels  352 us (90%)
  local copies, waits for them, and re-layouts  31.6 us (8%)
    pallas_call x1, Pallas kernels, split_block(): pl.pallas_call(functools.partial(fused, names), out_shape=[jax.ShapeDtype...  352 us
    unnamed x54, local copies, waits for them, and re-layouts  12 us

profile of v1, /device:TPU:0, one launch (start us, length us, event | category | flops | bytes accessed | tf_op | source)
XLA Modules:
  0.0 388.2 jit_solution(14211350027049961064)
XLA Ops:
  0.7 0.7 copy-done.19
  1.4 0.6 pad_maximum_fusion.4.refs_7_
  2.0 0.1 copy-done.12
  2.1 0.1 concatenate.48
  2.2 0.6 copy-done.13
  2.9 0.6 copy-done.14
  3.6 0.6 copy-done.15
  4.3 0.7 broadcast_in_dim.8.refs_2_
  5.0 0.1 concatenate.44
  5.2 0.7 reshape.129.refs_8_
  5.9 0.2 copy-done.4
  6.1 0.3 reshape.127
  6.4 0.2 concatenate.41
  6.6 0.7 copy-done.5
  7.3 0.3 reshape.128
  7.6 0.2 concatenate.42
  7.9 0.8 pad_maximum_fusion.3.refs_4_
  8.6 0.1 copy-done.9
  8.7 0.2 copy.63
  9.0 0.7 copy-done.10
  9.6 0.2 copy.66
  9.9 0.7 copy-done.7
  10.5 0.2 copy.64
  10.8 0.2 pad_maximum_fusion.1
  11.0 0.4 copy.86
  11.4 0.4 reshape.141
  11.9 0.4 copy-done.8
  12.3 0.2 copy.67
  12.5 0.2 pad_maximum_fusion.2
  12.8 0.4 copy.87
  13.1 0.5 reshape.142
  13.6 0.8 pad_maximum_fusion.refs_3_
  14.4 352.1 %block.1 = (f32[256,1024]{1,0:T(8,128)}, f32[256,1024]{1,0:T(8,128)}, bf16[320,768]{1,0:T(8,128)(2,1)}, bf16[128,1536]{1,0:T(8,128)(2,1)}, f32[48,1024]{1,0:T(8,...) custom-call(f32[256,1024]{1,0:T(8,128)} %bitcast.72, f32[256,1024]{1,0:T(8,128)} %bitcast.73, ...), custom_call_target="tpu_custom_call" | custom-call | tf_op jit(solution)/shard_map/block/pallas_call | solution.py:1282
  366.5 0.7 copy-done.16
  367.4 0.6 divide_multiply_fusion
  368.0 0.5 slice_bitcast_fusion.3
  368.5 0.5 slice_bitcast_fusion
  369.0 0.6 slice.75
  369.6 1.1 fusion.1
  370.7 0.2 copy.91
  371.0 0.2 copy.90
  371.3 0.6 copy.79
  371.9 1.1 slice.62
  373.0 0.6 copy.81
  373.6 1.1 slice.65
  374.8 0.3 slice.84
  375.0 0.8 copy.82
  375.9 1.5 slice.67
  377.4 0.3 slice.85
  377.6 0.8 copy.83
  378.5 1.5 slice.69
  380.0 0.3 reshape.140
  380.3 0.3 copy.101
  380.6 1.2 reshape.136
  381.8 0.3 reshape.139
  382.1 0.3 copy.102
  382.4 1.2 reshape.135
  383.6 1.0 copy.113
  384.6 0.6 copy-done
  385.2 1.0 copy.114
  386.2 0.1 copy-done.6
  386.4 0.7 copy.115
  387.0 0.4 copy-done.2
  387.4 0.7 copy.116
  (45 shorter events, 0.8 us)
Async XLA Ops:
  0.7 0.7 copy-start.19
  0.7 0.7 copy-start.18
  0.7 0.7 copy-start.17
  1.4 0.7 copy-start.12
  2.1 0.7 copy-start.13
  2.8 0.7 copy-start.14
  3.5 0.7 copy-start.15
  4.3 0.7 copy-start.11
  5.1 0.9 copy-start.4
  6.4 0.9 copy-start.5
  7.8 0.9 copy-start.9
  8.7 0.9 copy-start.10
  9.6 0.9 copy-start.7
  11.4 0.9 copy-start.8
  366.5 0.7 copy-start.16
  378.5 1.5 copy-start.3
  382.1 1.6 copy-start.1
  383.6 1.6 copy-start
  385.2 1.1 copy-start.6
  386.4 1.1 copy-start.2

commit v2 on v1

--- a/solution.py
+++ b/solution.py
@@ -380,12 +380,10 @@
 
 def fused(names, *refs):
     r = dict(zip(names, refs))
-    x, cot, seg, xw, xhu, own_o, own_d, gains, vec = (
-        r[k] for k in ("x", "cot", "seg", "xw", "xhu", "own_o", "own_d", "gains", "vec")
-    )
-    out, gin, fin, fin_hu, g_o, g_d, g_vec = (
+    out_hbm, gin_hbm, fin, fin_hu, g_o, g_d, g_vec = (
         r[k] for k in ("out", "gin", "fin", "fin_hu", "g_o", "g_d", "g_vec")
     )
+    x, cot, out, gin, vec, gains = (r[k] for k in ("x", "cot", "out_own", "gin_own", "vec", "gains"))
     w_one, w_ri, w_o, w_hu, w_d = (r[k] for k in ("w_one", "w_ri", "w_o", "w_hu", "w_d"))
     norm, gout, norm_two, gres, conv, mix = (
         r[k] for k in ("norm", "gout", "norm_two", "gres", "conv", "mix")
@@ -423,12 +421,50 @@
     ring_to = [lax.rem(s + k, RING) for k in range(RING)]
     ring_from = [lax.rem(s + RING - k, RING) for k in range(RING)]
 
+    def fetch(slot, src, dst):
+        copy = pltpu.make_async_copy(src, dst, r["local"].at[slot])
+        copy.start()
+        return copy
+
+    raw = ghu
+    sides = (slice(0, raw.shape[1]), slice(raw.shape[1], 2 * raw.shape[1]))
+    spots, place = ({}, 0)
+    fetched = {}
+    for name, tall in (("w_gate", blk), ("w_input", blk), ("w_recur", cblk), ("w_inject", cblk)):
+        spots[name] = place
+        fetched[name] = [fetch(len(fetched), r["hbm_" + name], raw.at[pl.ds(place, tall)])]
+        place += tall
+    fetched["x"] = [fetch(4, r["hbm_x"], x)]
+    fetched["seg"] = [fetch(5, r["hbm_seg"], r["seg"])]
+    for k, name in enumerate(("gain_one", "gain_two")):
+        fetched[name] = [fetch(6 + k, r["hbm_" + name], gains.at[k])]
+    for k, name in enumerate(("w_hidden", "w_upward")):
+        spots[name] = place
+        fetched[name] = [
+            fetch(8 + 2 * k + j, r["hbm_" + name].at[:, side], raw.at[pl.ds(place + j * blk, blk)])
+            for j, side in enumerate(sides)
+        ]
+        place += 2 * blk
+    fetched["own"] = [
+        fetch(12, r["hbm_w_output"], w_o.at[at(s * cblk, cblk, 16)]),
+        fetch(13, r["hbm_w_down"], w_d.at[at(s * fblk, fblk, 16)]),
+    ]
+    fetched["vec"] = [fetch(14, r["hbm_conv_taps"], r["taps"])] + [
+        fetch(15 + k, r["hbm_" + name], r["biases"].at[k])
+        for k, name in enumerate(("conv_bias", "recur_bias", "inject_bias", "decay_param"))
+    ]
+    fetched["cot"] = [fetch(19, r["hbm_cot"], cot)]
+
+    def fetch_wait(*which):
+        for name in which:
+            for copy in fetched[name]:
+                copy.wait()
+
     barrier = pltpu.get_barrier_semaphore()
     for _, to in group_peers:
         pl.semaphore_signal(barrier, inc=1, device_id=to, device_id_type=MESH)
     for k in range(1, RING):
         pl.semaphore_signal(barrier, inc=1, device_id=(ring_to[k], b), device_id_type=MESH)
-    pl.semaphore_wait(barrier, 3 + RING - 1)
 
     class Chunk:
         pass
@@ -479,18 +515,31 @@
     dn = flat_chunk(w_d, fblk, 16, slice(0, width), r["y_d"], r["z_d"])
 
     rec = blk + cblk
-    one.source = lambda q: xw.at[at(q * rec, blk, 16)]
+    xhu = gri.at[pl.ds(GROUP * rec, 2 * GROUP * blk)]
+    one.source = lambda q: gri.at[at(q * rec, blk, 16)]
     one.place = lambda q: w_one.at[at(s * size_one + q * blk, blk, 16)]
     one.result = lambda q: fin.at[at(q * rec, blk, 16)]
-    ri.source = lambda q: xw.at[at(q * rec + blk, cblk, 16)]
+    ri.source = lambda q: gri.at[at(q * rec + blk, cblk, 16)]
     ri.place = lambda q: w_ri.at[q, s]
     ri.result = lambda q: fin.at[at(q * rec + blk, cblk, 16)]
-    hi.source = lambda q: xhu.at[at(q * blk, blk, 16), slice(0, hid)]
+    hi.source = lambda q: xhu.at[at(q * blk, blk, 16)]
     hi.place = lambda q: w_hu.at[at(s * size_one + q * blk, blk, 16), slice(0, hid)]
     hi.result = lambda q: fin_hu.at[at(q * blk, blk, 16), slice(0, hid)]
-    up.source = lambda q: xhu.at[at(q * blk, blk, 16), slice(hid, 2 * hid)]
+    up.source = lambda q: xhu.at[at((GROUP + q) * blk, blk, 16)]
     up.place = lambda q: w_hu.at[at(s * size_one + q * blk, blk, 16), slice(hid, 2 * hid)]
     up.result = lambda q: fin_hu.at[at(q * blk, blk, 16), slice(hid, 2 * hid)]
+
+    def member_cols(array, q, parts):
+        pieces = [array[:, parts * (GROUP * k + q) : parts * (GROUP * k + q + 1)] for k in range(RING)]
+        return jnp.concatenate(pieces, axis=1)
+
+    def prepare(c, tall, parts, *names):
+        for q in range(GROUP):
+            for k, name in enumerate(names):
+                array = raw[spots[name] : spots[name] + tall, :]
+                if array.shape[1] < RING * GROUP * parts:
+                    array = jnp.concatenate([array, raw[spots[name] + tall : spots[name] + 2 * tall, :]], axis=1)
+                c.source(q)[:, k * RING * parts : (k + 1) * RING * parts] = member_cols(array, q, parts)
 
     def spread(c):
         for (peer, to), slot in zip(group_peers, c.spread):
@@ -501,23 +550,30 @@
         for (peer, to), slot in zip(group_peers, c.spread):
             net.got(c.place(peer), to, slot)
 
-    def gather(c):
-        for k in (1, 3, 2):
+    def gz(c, *which):
+        for k in which:
             net.put(c.block(s), c.block(s), (far[k] * PAIR + y, b), c.gather_z[k])
+
+    def gy(c):
         net.put(c.block(s), c.block(s), to_pair, c.gather_y[0])
 
-    def gather_relay(c, k):
-        from_z = near[k] * PAIR + y
-        net.got(c.block(from_z), (from_z, b), c.gather_z[k])
-        net.put(c.block(from_z), c.block(from_z), to_pair, c.gather_y[k])
+    def gr(c, *which):
+        for k in which:
+            from_z = near[k] * PAIR + y
+            net.got(c.block(from_z), (from_z, b), c.gather_z[k])
+            net.put(c.block(from_z), c.block(from_z), to_pair, c.gather_y[k])
 
     def gather_wait(c):
         for k in range(DEPTH):
             net.got(c.block(near[k] * PAIR + 1 - y), to_pair, c.gather_y[k])
 
-    def sum_pair(c):
-        for k in (1, 3, 2, 0):
+    def sp(c, *which):
+        for k in which:
             net.put(c.block(far[k] * PAIR + 1 - y), c.y_block(far[k]), to_pair, c.sum_y[k])
+
+    def se(c, *which):
+        for k in which:
+            sum_pair_end(c, k)
 
     def sum_pair_end(c, k):
         net.got(c.y_block(far[k]), to_pair, c.sum_y[k])
@@ -604,7 +660,6 @@
         return ref.at[at(h * here + i * 16, 16, 16)]
 
     tiles16 = here // 16
-    gain_one, gain_two = (gains[0:1], gains[1:2])
 
     def rms(values):
         return lax.rsqrt(jnp.mean(values * values, axis=-1, keepdims=True) + EPSILON)
@@ -639,9 +694,6 @@
         now = brx[q, pl.ds(EDGE + start, STEP), marks]
         return (now == brx[q, pl.ds(EDGE + start - k, STEP), marks]).astype(F32)
 
-    spread(one)
-    acc[...] = jnp.zeros_like(acc)
-    gain_acc[...] = jnp.zeros_like(gain_acc)
     norm_slots, gout_slots, conv_slots = (net.slots(6), net.slots(6), net.slots(6))
     two_slots, gres_slots = (net.slots(6), net.slots(6))
     out_slots, gnt_slots, down_slots, thru_slots, gn_slots = (net.slots(6) for _ in range(5))
@@ -653,31 +705,52 @@
         net.slots(3),
     )
     norm_rows, gout_rows, two_rows, gres_rows = (token_rows(ref) for ref in (norm, gout, norm_two, gres))
-
-    for h in range(2):
+    conv_cols = lambda q, h: conv.at[pl.ds(h * half, half), at(q * chans, chans, LANES)]
+
+    fetch_wait("w_gate", "w_input")
+    prepare(one, blk, cblk, "w_gate", "w_input")
+    fetch_wait("x", "seg", "gain_one", "gain_two")
+    gain_one, gain_two = (gains[0:1], gains[1:2])
+    pl.semaphore_wait(barrier, 3 + RING - 1)
+    spread(one)
+    for h in range(2):
+        ids = r["seg"][h : h + 1, :].astype(F32)
+        norm[at((h * GROUP + b) * here, here, 16), width : width + LANES] = jnp.transpose(
+            jnp.broadcast_to(ids, (here, here))
+        ).astype(BF16)
+
         def norm_tile(i, h=h):
             v = own(x, h, i)[...]
             sixteen(norm_rows(b, h), i)[:, 0:width] = (v * rms(v) * gain_one).astype(BF16)
-            sixteen(norm_rows(b, h), i)[:, width : width + LANES] = own(seg, h, i)[...]
 
         loop(tiles16, norm_tile)
         share(norm_rows, norm_slots, h)
+    fetch_wait("w_recur", "w_inject")
+    prepare(ri, cblk, cblk, "w_recur", "w_inject")
     spread(ri)
+    spread_wait(one)
+    gz(one, 1, 3, 2)
+    gy(one)
+    fetch_wait("w_hidden")
+    prepare(hi, blk, fblk, "w_hidden")
     spread(hi)
+    fetch_wait("w_upward")
+    prepare(up, blk, fblk, "w_upward")
     spread(up)
-    w_o[at(s * cblk, cblk, 16), :] = own_o[...]
-    w_d[at(s * fblk, fblk, 16), :] = own_d[...]
-    spread_wait(one)
-    gather(one)
-    gather(wo)
-    for h in range(2):
-        share_relay(norm_rows, norm_slots, h)
-
-    for h in range(2):
-        def low_tile(i, h=h):
-            sixteen(gout_rows(b, h), i)[...] = own(cot, h, i)[...].astype(BF16)
-
-        loop(tiles16, low_tile)
+
+    fetch_wait("vec")
+    log_of = lambda grown: jnp.log(grown)
+    biases = jnp.concatenate([r["biases"][k].reshape(1, -1) for k in range(4)], axis=0)
+    small = jnp.exp(biases[3:4])
+    grown = 1.0 + small
+    rate = jnp.where(grown == 1.0, small, log_of(grown) * small / jnp.where(grown == 1.0, 1.0, grown - 1.0))
+    sources = jnp.concatenate([r["taps"][...], biases[0:3], -DECAY_SCALE * rate], axis=0)
+    for q in range(GROUP):
+        r["vecs"][q, 0:8] = member_cols(sources, q, cblk)
+        r["vecs"][q, 8:16] = member_cols(jnp.broadcast_to(jax.nn.sigmoid(biases[3:4]), (8, GROUP * chans)), q, cblk)
+    vec[...] = r["vecs"][b]
+    acc[...] = jnp.zeros_like(acc)
+    gain_acc[...] = jnp.zeros_like(gain_acc)
 
     @pl.when(s == 0)
     def _():
@@ -687,24 +760,34 @@
     def _():
         tgx[:, here : here + EDGE, :] = jnp.full((rows, EDGE, chans + LANES), -1.0, F32)
 
-    for k in (1, 3, 2):
-        gather_relay(one, k)
+    gr(one, 1)
+    share_relay(norm_rows, norm_slots, 0)
+    gr(one, 3)
+    fetch_wait("cot")
+    for h in range(2):
+        def low_tile(i, h=h):
+            sixteen(gout_rows(b, h), i)[...] = own(cot, h, i)[...].astype(BF16)
+
+        loop(tiles16, low_tile)
+    share_relay(norm_rows, norm_slots, 1)
+    gr(one, 2)
+    spread_wait(ri)
+    gy(ri)
+    gz(ri, 1)
+    share_end(norm_rows, norm_slots, 0)
     gather_wait(one)
 
     for h in range(2):
-        share_end(norm_rows, norm_slots, h)
-
-        def first_mm(i, h=h):
-            q = h * GROUP + i
-            span = at(q * here, here, 16)
-            got = dot_nn(norm[span, 0:width], w_one[...])
-            gate_pre[q] = got[:, 0:chans]
-            brx[q, EDGE : EDGE + here, 0:chans] = got[:, chans:two]
-            ids = norm[span, width : width + LANES].astype(F32)
-            brx[q, EDGE : EDGE + here, marks] = ids
-            tgx[q, 0:here, marks] = ids
-
-        loop(GROUP, first_mm)
+        if h:
+            share_end(norm_rows, norm_slots, h)
+        span = pl.ds(h * half, half)
+        block = slice(h * GROUP, (h + 1) * GROUP)
+        got = dot_nn(norm[span, 0:width], w_one[...]).reshape(GROUP, here, two)
+        gate_pre[block] = got[:, :, 0:chans]
+        brx[block, EDGE : EDGE + here, 0:chans] = got[:, :, chans:two]
+        ids = norm[span, width : width + LANES].astype(F32).reshape(GROUP, here, LANES)
+        brx[block, EDGE : EDGE + here, marks] = ids
+        tgx[block, 0:here, marks] = ids
 
     def halo_out():
         return pltpu.make_async_remote_copy(
@@ -720,16 +803,13 @@
     def _():
         halo_out().start()
 
-    spread_wait(ri)
-    gather(ri)
-    for k in (1, 3, 2):
-        gather_relay(wo, k)
+    gz(ri, 3, 2)
+    gr(ri, 1)
 
     @pl.when(s > 0)
     def _():
         net.got(brx.at[:, pl.ds(0, EDGE)], (ring_from[1], b), halo_slot)
 
-    conv_cols = lambda q, h: conv.at[pl.ds(h * half, half), at(q * chans, chans, LANES)]
     for h in range(2):
         def conv_tile(q, start, lanes, g):
             total = vec[4:5, lanes] + vec[0:1, lanes] * brx[q, pl.ds(EDGE + start, STEP), lanes]
@@ -743,24 +823,29 @@
         share(conv_cols, conv_slots, h)
     for h in range(2):
         share(gout_rows, gout_slots, h)
-    for h in range(2):
-        share_relay(conv_cols, conv_slots, h)
-    for k in (1, 3, 2):
-        gather_relay(ri, k)
+    gr(ri, 3)
+    fetch_wait("own")
+    gy(wo)
+    gz(wo, 1, 3, 2)
+    share_relay(conv_cols, conv_slots, 0)
     spread_wait(hi)
-    gather(hi)
+    gy(hi)
+    gr(ri, 2)
+    share_relay(conv_cols, conv_slots, 1)
+    gr(wo, 1, 3, 2)
+    gz(hi, 1, 3)
+    spread_wait(up)
+    share_end(conv_cols, conv_slots, 0)
     gather_wait(ri)
 
     for h in range(2):
-        share_end(conv_cols, conv_slots, h)
-
-        def gate_mm(i, h=h):
-            q = h * GROUP + i
-            got = dot_nn(conv[at(q * here, here, 16), :], w_ri[...].reshape(GROUP * chans, two))
-            rgate[q] = got[:, 0:chans]
-            igate[q] = got[:, chans:two]
-
-        loop(GROUP, gate_mm)
+        if h:
+            share_end(conv_cols, conv_slots, h)
+        block = slice(h * GROUP, (h + 1) * GROUP)
+        got = dot_nn(conv[pl.ds(h * half, half), :], w_ri[...].reshape(GROUP * chans, two))
+        got = got.reshape(GROUP, here, two)
+        rgate[block] = got[:, :, 0:chans]
+        igate[block] = got[:, :, chans:two]
 
         def gate_tile(q, start, lanes, g):
             span = pl.ds(start, STEP)
@@ -785,12 +870,17 @@
     pre_f[s, rows : 2 * rows] = tail
     for k in range(1, RING):
         net.put(pre_f.at[s], pre_f.at[s], (ring_to[k], b), pre_slots[k])
-    for k in (1, 3, 2):
-        gather_relay(hi, k)
-    spread_wait(up)
-    gather(up)
-    for h in range(2):
-        share_relay(gout_rows, gout_slots, h)
+    gr(hi, 1, 3)
+    gz(hi, 2)
+    gy(up)
+    gz(up, 1)
+
+    for h in range(2):
+        def act_tile(q, start, lanes, g):
+            span = pl.ds(start, STEP)
+            tgx[q, span, lanes] = gelu_parts(gate_pre[q, span, lanes])[0]
+
+        over(h, act_tile)
     for k in range(1, RING):
         net.got(pre_f.at[ring_from[k]], (ring_from[k], b), pre_slots[k])
     state = jnp.zeros((rows, chans), F32)
@@ -808,22 +898,23 @@
 
     for h in range(2):
         def mix_tile(q, start, lanes, g):
-            act, _ = gelu_parts(gate_pre[q, pl.ds(start, STEP), lanes])
+            act = tgx[q, pl.ds(start, STEP), lanes]
             mix[flat(q, start), lanes] = (stx[q, pl.ds(EDGE + start, STEP), lanes] * act).astype(BF16)
 
         over(h, mix_tile)
-
-        def out_mm(i, h=h):
-            span = at((h * GROUP + i) * here, here, 16)
-            part[span, :] = dot_nn(mix[span, :], w_o[...]).astype(BF16)
-
-        loop(GROUP, out_mm)
+        span = pl.ds(h * half, half)
+        part[span, :] = dot_nn(mix[span, :], w_o[...]).astype(BF16)
         merge(part_rows, first_in, out_slots, h)
+    gr(hi, 2)
+    gr(up, 1)
+    gz(up, 3, 2)
+    for h in range(2):
+        share_relay(gout_rows, gout_slots, h)
     for h in range(2):
         merge_relay(part_rows, first_in, second_in, out_slots, h, tiles16, sixteen)
-    for k in (1, 3, 2):
-        gather_relay(up, k)
-    gather(dn)
+    gr(up, 3)
+    gy(dn)
+    gz(dn, 1, 3, 2)
     for h in range(2):
         merge_end(first_in, second_in, out_slots, h)
 
@@ -834,99 +925,97 @@
 
         loop(tiles16, resid_tile)
         share(two_rows, two_slots, h)
-    for h in range(2):
-        share_relay(two_rows, two_slots, h)
+        if h == 0:
+            gr(up, 2)
+    share_relay(two_rows, two_slots, 0)
+    gr(dn, 1)
+    share_relay(two_rows, two_slots, 1)
     gather_wait(hi)
     gather_wait(up)
 
     for h in range(2):
         share_end(two_rows, two_slots, h)
-
-        def hidden_mm(i, h=h):
-            span = at((h * GROUP + i) * here, here, 16)
-            pre[...] = dot_nn(norm_two[span, :], w_hu[...])
-
-            def tile(t):
-                rows_t = at(t * 16, 16, 16)
-                flat_t = at((h * GROUP + i) * here + t * 16, 16, 16)
-                for g in range(hid // LANES):
-                    lanes = slice(g * LANES, (g + 1) * LANES)
-                    right = slice(hid + g * LANES, hid + (g + 1) * LANES)
-                    act, slope = gelu_parts(pre[rows_t, lanes])
-                    upward = pre[rows_t, right]
-                    prod[flat_t, lanes] = (act * upward).astype(BF16)
-                    ghu[flat_t, lanes] = (upward * slope).astype(BF16)
-                    ghu[flat_t, right] = act.astype(BF16)
-
-            loop(tiles16, tile)
-
-        loop(GROUP, hidden_mm)
-    for k in (1, 3, 2):
-        gather_relay(dn, k)
+        span = pl.ds(h * half, half)
+        for j in range(hid // 256):
+            left = slice(j * 256, j * 256 + 256)
+            right = slice(hid + j * 256, hid + j * 256 + 256)
+            pre[:, 0:256] = dot_nn(norm_two[span, :], w_hu[:, left])
+            pre[:, 256:512] = dot_nn(norm_two[span, :], w_hu[:, right])
+
+            def tile(i, h=h, j=j):
+                rows_t = at(i * STEP, STEP, STEP)
+                flat_t = at(h * half + i * STEP, STEP, STEP)
+                for g in range(2):
+                    first = slice(j * 256 + g * LANES, j * 256 + (g + 1) * LANES)
+                    second = slice(hid + j * 256 + g * LANES, hid + j * 256 + (g + 1) * LANES)
+                    act, slope = gelu_parts(pre[rows_t, g * LANES : (g + 1) * LANES])
+                    upward = pre[rows_t, 256 + g * LANES : 256 + (g + 1) * LANES]
+                    prod[flat_t, first] = (act * upward).astype(BF16)
+                    ghu[flat_t, first] = (upward * slope).astype(BF16)
+                    ghu[flat_t, second] = act.astype(BF16)
+
+            loop(half // STEP, tile)
+        if h == 0:
+            gr(dn, 3)
+    gr(dn, 2)
+    for h in range(2):
+        share_end(gout_rows, gout_slots, h)
     gather_wait(dn)
 
     net.flush()
     for h in range(2):
-        share_end(gout_rows, gout_slots, h)
-
-        def down_back(i, h=h):
-            span = at((h * GROUP + i) * here, here, 16)
-            back = dot_nt(gout[span, :], w_d[...])
-            ghu[span, 0:hid] = (back * ghu[span, 0:hid].astype(F32)).astype(BF16)
-            ghu[span, hid : 2 * hid] = (back * ghu[span, hid : 2 * hid].astype(F32)).astype(BF16)
-            part[span, :] = dot_nt(ghu[span, :], w_hu[...]).astype(BF16)
-
-        loop(GROUP, down_back)
+        span = pl.ds(h * half, half)
+        for j in range(hid // 256):
+            left = slice(j * 256, j * 256 + 256)
+            right = slice(hid + j * 256, hid + j * 256 + 256)
+            back = dot_nt(gout[span, :], w_d[left, :])
+            ghu[span, left] = (back * ghu[span, left].astype(F32)).astype(BF16)
+            ghu[span, right] = (back * ghu[span, right].astype(F32)).astype(BF16)
+        for j in range(2):
+            cols = slice(j * width // 2, (j + 1) * width // 2)
+            part[span, cols] = dot_nt(ghu[span, :], w_hu[cols, :]).astype(BF16)
         merge(part_rows, first_in, gnt_slots, h)
     for h in range(2):
         merge_relay(part_rows, first_in, second_in, gnt_slots, h, tiles16, sixteen)
 
-    def grad_hu(i):
-        cols = at(i * 256, 256, LANES)
-        w_hu[at(i * 256, 256, 16), :] = dot_tn(norm_two[:, cols], ghu[...]).astype(BF16)
-
-    loop(width // 256, grad_hu)
-    sum_pair(hi)
+    for j in range(2):
+        def grad_hu(i, j=j):
+            cols = at(i * 256, 256, LANES)
+            side = slice(j * hid, (j + 1) * hid)
+            w_hu[at(i * 256, 256, 16), side] = dot_tn(norm_two[:, cols], ghu[:, side]).astype(BF16)
+
+        loop(width // 256, grad_hu)
+        sp(up if j else hi, 1, 3, 2, 0) if j == 0 else sp(up, 1, 3)
+
     for h in range(2):
         merge_end(first_in, second_in, gnt_slots, h)
 
         def second_norm(i, h=h):
             back = norm_grad(1, own(out, h, i)[...], merged(h, i), gain_two)
-            own(gin, h, i)[...] = own(cot, h, i)[...] + back
+            total = own(cot, h, i)[...] + back
+            own(gin, h, i)[...] = total
+            sixteen(gres_rows(b, h), i)[...] = total.astype(BF16)
 
         loop(tiles16, second_norm)
-
-    for h in range(2):
-        def low_resid(i, h=h):
-            sixteen(gres_rows(b, h), i)[...] = own(gin, h, i)[...].astype(BF16)
-
-        loop(tiles16, low_resid)
         share(gres_rows, gres_slots, h)
+        if h == 0:
+            se(hi, 1, 3)
     net.flush("part")
-
-    def down_mm(i):
-        span = at(i * here, here, 16)
+    for h in range(2):
+        span = pl.ds(h * half, half)
         part[span, :] = dot_nn(prod[span, :], w_d[...]).astype(BF16)
-
-    loop(rows, down_mm)
-    for h in range(2):
-        share_relay(gres_rows, gres_slots, h)
-
-    def grad_down(i):
-        cols = at(i * 256, 256, LANES)
-        w_d[at(i * 256, 256, 16), :] = dot_tn(prod[:, cols], gout[...]).astype(BF16)
-
-    loop(hid // 256, grad_down)
-    sum_pair(dn)
+    share_relay(gres_rows, gres_slots, 0)
+    for j in range(2):
+        cols = slice(j * hid // 2, (j + 1) * hid // 2)
+        w_d[cols, :] = dot_tn(prod[:, cols], gout[...]).astype(BF16)
+    se(hi, 2, 0)
+    share_relay(gres_rows, gres_slots, 1)
 
     for h in range(2):
         share_end(gres_rows, gres_slots, h)
-
-        def out_back(i, h=h):
-            q = h * GROUP + i
-            tgx[q, 0:here, 0:chans] = dot_nt(gres[at(q * here, here, 16), :], w_o[...])
-
-        loop(GROUP, out_back)
+        block = slice(h * GROUP, (h + 1) * GROUP)
+        got = dot_nt(gres[pl.ds(h * half, half), :], w_o[...])
+        tgx[block, 0:here, 0:chans] = got.reshape(GROUP, here, chans)
 
         def mix_back(q, start, lanes, g):
             span = pl.ds(start, STEP)
@@ -948,6 +1037,8 @@
     pre_b[s, rows : 2 * rows] = tail
     for k in range(1, RING):
         net.put(pre_b.at[s], pre_b.at[s], (ring_to[k], b), back_slots[k])
+    sp(up, 2, 0)
+    sp(dn, 1, 3)
 
     for h in range(2):
         merge(part_rows, first_in, down_slots, h)
@@ -955,6 +1046,7 @@
     w_o[...] = dot_tn(mix[...], gres[...]).astype(BF16)
     for h in range(2):
         merge_relay(part_rows, first_in, second_in, down_slots, h, tiles16, sixteen)
+    se(up, 1, 3)
 
     for k in range(1, RING):
         net.got(pre_b.at[ring_from[k]], (ring_from[k], b), back_slots[k])
@@ -969,14 +1061,6 @@
         return carry[:, p, :] * total
 
     lax.fori_loop(0, here, scan_back, state, unroll=8)
-
-    for h in range(2):
-        merge_end(first_in, second_in, down_slots, h)
-
-        def out_tile(i, h=h):
-            own(out, h, i)[...] = own(out, h, i)[...] + merged(h, i)
-
-        loop(tiles16, out_tile)
 
     thru_cols = lambda q, h: ghu.at[pl.ds(h * half, half), at(q * chans, chans, LANES)]
     thru_first = lambda h, slot: prod.at[pl.ds(h * half, half), pl.ds(slot * chans, chans)]
@@ -1003,14 +1087,24 @@
             add_to(7, lanes, grad_log * (-DECAY_SCALE * rg))
 
         over(h, gates_back)
-
-        def thru_mm(i, h=h):
-            span = at((h * GROUP + i) * here, here, 16)
-            got = dot_nt(gri[span, :], w_ri[...].reshape(GROUP * chans, two))
-            ghu[span, :] = got.astype(BF16)
-
-        loop(GROUP, thru_mm)
+        span = pl.ds(h * half, half)
+        for j in range(2):
+            pair = slice(2 * j, 2 * j + 2)
+            got = dot_nt(gri[span, :], w_ri[pair].reshape(2 * chans, two))
+            ghu[span, 2 * j * chans : 2 * (j + 1) * chans] = got.astype(BF16)
+        if h:
+            for k in range(2):
+                merge_end(first_in, second_in, down_slots, k)
+
+                def out_tile(i, k=k):
+                    own(out, k, i)[...] = own(out, k, i)[...] + merged(k, i)
+
+                loop(tiles16, out_tile)
         merge(thru_cols, thru_first, thru_slots, h)
+        if h == 0:
+            se(up, 2, 0)
+            sp(dn, 2, 0)
+    leave_out = fetch(0, out, out_hbm)
     for h in range(2):
         merge_relay(thru_cols, thru_first, thru_second, thru_slots, h, half // 16, sixteen)
 
@@ -1019,11 +1113,9 @@
         w_ri[i] = got.astype(BF16).reshape(RING, cblk, two)
 
     loop(GROUP, grad_ri)
-    for k in (1, 3, 2, 0):
-        sum_pair_end(hi, k)
-    for k in (1, 3, 2, 0):
-        sum_pair_end(dn, k)
-    sum_pair(up)
+    se(dn, 1, 3)
+    sp(ri, 1)
+    se(dn, 2, 0)
 
     for h in range(2):
         merge_end(thru_first, thru_second, thru_slots, h)
@@ -1050,8 +1142,8 @@
     def _():
         halo_in().start()
 
-    sum_pair(wo)
-    sum_pair(ri)
+    sp(ri, 3, 2, 0)
+    sp(wo, 1, 3, 2, 0)
 
     @pl.when(s < RING - 1)
     def _():
@@ -1074,12 +1166,10 @@
             ggb[flat(q, start), slice(chans + g * LANES, chans + (g + 1) * LANES)] = total.astype(BF16)
 
         over(h, conv_back)
-
-        def first_back(i, h=h):
-            span = at((h * GROUP + i) * here, here, 16)
-            part[span, :] = dot_nt(ggb[span, :], w_one[...]).astype(BF16)
-
-        loop(GROUP, first_back)
+        span = pl.ds(h * half, half)
+        for j in range(2):
+            cols = slice(j * width // 2, (j + 1) * width // 2)
+            part[span, cols] = dot_nt(ggb[span, :], w_one[cols, :]).astype(BF16)
         merge(part_rows, first_in, gn_slots, h)
     for h in range(2):
         merge_relay(part_rows, first_in, second_in, gn_slots, h, tiles16, sixteen)
@@ -1089,10 +1179,8 @@
         w_one[at(i * 256, 256, 16), :] = dot_tn(norm[:, cols], ggb[...]).astype(BF16)
 
     loop(width // 256, grad_one)
-    sum_pair(one)
-    for c in (up, wo, ri):
-        for k in (1, 3, 2, 0):
-            sum_pair_end(c, k)
+    sp(one, 1, 3, 2, 0)
+    se(ri, 1, 3)
 
     for h in range(2):
         merge_end(first_in, second_in, gn_slots, h)
@@ -1102,9 +1190,13 @@
             own(gin, h, i)[...] = own(gin, h, i)[...] + back
 
         loop(tiles16, first_norm)
+        if h == 0:
+            se(ri, 2, 0)
+    leave_gin = fetch(1, gin, gin_hbm)
 
     for k in range(8):
-        vs[s, k : k + 1, 0:chans] = jnp.sum(acc[k], axis=0, keepdims=True)
+        total = jnp.sum(acc[k], axis=0, keepdims=True)
+        vs[s, k : k + 1, 0:chans] = total * vec[8:9, :] if k == 7 else total
     piece = width // 4
     for k in range(2):
         total = jnp.sum(gain_acc[k], axis=0, keepdims=True)
@@ -1113,18 +1205,18 @@
     for k in range(1, RING):
         net.put(vs.at[s], vs.at[s], (ring_to[k], b), vec_slots[k])
 
-    for k in (1, 3, 2, 0):
-        sum_pair_end(one, k)
-
     def keep_down(i, total):
         g_d[at(i * 16, 16, 16), :] = total
 
     def keep_out(i, total):
         g_o[at(i * 16, 16, 16), :] = total
 
-    sum_end(dn, keep_down)
     sum_end_spread(hi)
     sum_end_spread(up)
+    se(wo, 1, 3, 2, 0)
+    sum_end(dn, keep_down)
+    se(one, 1, 3, 2, 0)
+    sum_end_spread(ri)
     sum_end(wo, keep_out)
     for k in range(1, RING):
         net.got(vs.at[ring_from[k]], (ring_from[k], b), vec_slots[k])
@@ -1134,7 +1226,6 @@
     vb[b] = total
     for (peer, to), slot in zip(group_peers, last_slots):
         net.put(vb.at[b], vb.at[b], to, slot)
-    sum_end_spread(ri)
     sum_end_spread(one)
     for (peer, to), slot in zip(group_peers, last_slots):
         net.got(vb.at[peer], to, slot)
@@ -1146,6 +1237,8 @@
     for c in (hi, up, ri, one):
         home_wait(c)
     net.flush()
+    leave_out.wait()
+    leave_gin.wait()
 
     @pl.when(s < RING - 1)
     def _():
@@ -1156,16 +1249,49 @@
         halo_in().wait_send()
 
 
-def by_member(array, parts):
-    lead = array.shape[:-1]
-    split = array.reshape(*lead, RING, GROUP, parts)
-    return jnp.moveaxis(split, -2, 0).reshape(GROUP, *lead, RING * parts)
-
-
-def from_members(array, parts):
-    members, count, _ = array.shape
-    split = array.reshape(members, count, RING, parts)
-    return jnp.moveaxis(split, 0, 2).reshape(count, RING * members * parts)
+def finish(names, *refs):
+    r = dict(zip(names, refs))
+    r["to_o"][...] = r["g_o"][...]
+    r["to_d"][...] = r["g_d"][...]
+    place = lax.axis_index("seq") * GROUP + lax.axis_index("batch")
+    s = lax.axis_index("seq")
+    blk, cblk, fblk = (r["to_gate"].shape[0], r["to_recur"].shape[0], r["to_d"].shape[0])
+    chans, hid = (RING * cblk, RING * fblk)
+    rec = blk + cblk
+
+    def joined(pieces, parts):
+        pieces = [piece.astype(F32) for piece in pieces]
+        return jnp.concatenate(
+            [pieces[q][:, k * parts : (k + 1) * parts] for k in range(RING) for q in range(GROUP)], axis=1
+        )
+
+    fin, fin_hu, g_vec = (r["fin"], r["fin_hu"], r["g_vec"])
+    for name, first, tall, left in (
+        ("to_gate", 0, blk, 0),
+        ("to_input", 0, blk, chans),
+        ("to_recur", blk, cblk, 0),
+        ("to_inject", blk, cblk, chans),
+    ):
+        spans = [slice(q * rec + first, q * rec + first + tall) for q in range(GROUP)]
+        r[name][...] = joined([fin[span, left : left + chans] for span in spans], cblk)
+    for name, left in (("to_hidden", 0), ("to_upward", hid)):
+        spans = [slice(q * blk, (q + 1) * blk) for q in range(GROUP)]
+        r[name][...] = joined([fin_hu[span, left : left + hid] for span in spans], fblk)
+    vectors = g_vec[:, 0:chans]
+    mine = vectors[:, 0:cblk]
+    for k in range(1, RING):
+        mine = jnp.where(k == s, vectors[:, k * cblk : (k + 1) * cblk], mine)
+    r["to_taps"][...] = mine[0:4]
+    for k, name in enumerate(("to_cbias", "to_rbias", "to_ibias", "to_decay")):
+        r[name][...] = mine[4 + k]
+    piece = g_vec.shape[1] - chans
+    for k, name in enumerate(("to_gain_one", "to_gain_two")):
+        total = jnp.zeros((1, blk), F32)
+        for j in range(4):
+            for m in range(piece // blk):
+                part = g_vec[4 * k + j : 4 * k + j + 1, chans + m * blk : chans + (m + 1) * blk]
+                total = jnp.where(j * (piece // blk) + m == place, part, total)
+        r[name][...] = total[0]
 
 
 def split_block(
@@ -1194,33 +1320,27 @@
     blk, cblk, fblk = (w_gate.shape[0], w_recur.shape[0], w_down.shape[0])
     tokens = GROUP * count * here
     rows = GROUP * count
-    s, b = (lax.axis_index("seq"), lax.axis_index("batch"))
-    ids = jnp.broadcast_to(
-        segments.astype(BF16).reshape(count * here, 1), (count * here, LANES)
-    )
-    first = jnp.concatenate([w_gate, w_recur], axis=0)
-    second = jnp.concatenate([w_input, w_inject], axis=0)
-    xw = jnp.concatenate([by_member(first, cblk), by_member(second, cblk)], axis=-1)
-    xhu = jnp.concatenate([by_member(w_hidden, fblk), by_member(w_upward, fblk)], axis=-1)
-    rate = -DECAY_SCALE * jax.nn.softplus(decay_param)
-    vectors = jnp.concatenate(
-        [conv_taps, jnp.stack([conv_bias, recur_bias, inject_bias, rate])], axis=0
-    ).reshape(8, RING, GROUP, cblk)
-    vec = lax.dynamic_index_in_dim(vectors, b, axis=2, keepdims=False).reshape(8, chans)
-    gains = jnp.stack([gain_one, gain_two])
-
     wide = chans + LANES
     size_one = GROUP * blk
     operands = {
-        "x": inputs.reshape(count * here, width),
-        "cot": cotangent.reshape(count * here, width),
-        "seg": ids,
-        "xw": xw.reshape(GROUP * (blk + cblk), 2 * chans),
-        "xhu": xhu.reshape(GROUP * blk, 2 * hid),
-        "own_o": w_output,
-        "own_d": w_down,
-        "gains": gains,
-        "vec": vec,
+        "hbm_x": inputs.reshape(count * here, width),
+        "hbm_cot": cotangent.reshape(count * here, width),
+        "hbm_seg": segments,
+        "hbm_w_gate": w_gate,
+        "hbm_w_input": w_input,
+        "hbm_w_recur": w_recur,
+        "hbm_w_inject": w_inject,
+        "hbm_w_output": w_output,
+        "hbm_w_hidden": w_hidden,
+        "hbm_w_upward": w_upward,
+        "hbm_w_down": w_down,
+        "hbm_gain_one": gain_one,
+        "hbm_gain_two": gain_two,
+        "hbm_conv_taps": conv_taps,
+        "hbm_conv_bias": conv_bias,
+        "hbm_recur_bias": recur_bias,
+        "hbm_inject_bias": inject_bias,
+        "hbm_decay_param": decay_param,
     }
     piece = width // 4
     outputs = {
@@ -1233,6 +1353,16 @@
         "g_vec": ((8, chans + piece), F32),
     }
     scratch = {
+        "x": ((count * here, width), F32),
+        "cot": ((count * here, width), F32),
+        "out_own": ((count * here, width), F32),
+        "gin_own": ((count * here, width), F32),
+        "seg": (segments.shape, jnp.int32),
+        "gains": ((2, width), F32),
+        "taps": (conv_taps.shape, F32),
+        "biases": ((4, channels), F32),
+        "vecs": ((GROUP, 16, chans), F32),
+        "vec": ((16, chans), F32),
         "w_one": ((width, 2 * chans), BF16),
         "w_ri": ((GROUP, RING, cblk, 2 * chans), BF16),
         "w_o": ((chans, width), BF16),
@@ -1257,7 +1387,7 @@
         "rgate": ((rows, here, chans), F32),
         "igate": ((rows, here, chans), F32),
         "carry": ((rows, here, chans), F32),
-        "pre": ((here, 2 * hid), F32),
+        "pre": ((GROUP * here, 512), F32),
         "core_in": ((2, 2, here, width), BF16),
         "x_in": ((2, here, width), BF16),
         "pre_f": ((RING, 2 * rows, chans), F32),
@@ -1277,50 +1407,51 @@
         "vs": ((RING, 8, chans + piece), F32),
         "vb": ((GROUP, 8, chans + piece), F32),
     }
-    names = [*operands, *outputs, *scratch, "send", "recv"]
+    names = [*operands, *outputs, *scratch, "send", "recv", "local"]
     in_vmem = pl.BlockSpec(memory_space=pltpu.VMEM)
+    in_hbm = pl.BlockSpec(memory_space=pl.ANY)
+    shapes = lambda specs: [jax.ShapeDtypeStruct(shape, kind) for shape, kind in specs.values()]
     got = pl.pallas_call(
         functools.partial(fused, names),
-        out_shape=[jax.ShapeDtypeStruct(shape, kind) for shape, kind in outputs.values()],
-        in_specs=[in_vmem] * len(operands),
-        out_specs=[in_vmem] * len(outputs),
+        out_shape=shapes(outputs),
+        in_specs=[in_hbm] * len(operands),
+        out_specs=[in_hbm] * 2 + [in_vmem] * (len(outputs) - 2),
         scratch_shapes=[pltpu.VMEM(shape, kind) for shape, kind in scratch.values()]
-        + [pltpu.SemaphoreType.DMA((SLOTS,))] * 2,
+        + [pltpu.SemaphoreType.DMA((SLOTS,))] * 2
+        + [pltpu.SemaphoreType.DMA((20,))],
         compiler_params=pltpu.CompilerParams(
             collective_id=0, has_side_effects=True, vmem_limit_bytes=VMEM_BYTES
         ),
         name="block",
     )(*operands.values())
-    out, gin, fin, fin_hu, g_o, g_d, g_vec = got
-    fin = fin.reshape(GROUP, blk + cblk, 2 * chans)
-    fin_hu = fin_hu.reshape(GROUP, blk, 2 * hid)
-    first = from_members(fin[:, :, :chans], cblk).astype(F32)
-    second = from_members(fin[:, :, chans:], cblk).astype(F32)
-    hidden = from_members(fin_hu[:, :, :hid], fblk).astype(F32)
-    upward = from_members(fin_hu[:, :, hid:], fblk).astype(F32)
-    mine = lax.dynamic_slice_in_dim(g_vec, s * cblk, cblk, axis=1)
-    place = s * GROUP + b
-    gain_sums = g_vec[:, chans:].reshape(2, width)
-    gain_mine = lax.dynamic_slice_in_dim(gain_sums, place * blk, blk, axis=1)
-    slope = jax.nn.sigmoid(lax.dynamic_slice_in_dim(decay_param, place * cblk, cblk))
+    finals = {
+        "to_gate": ((blk, channels), F32),
+        "to_input": ((blk, channels), F32),
+        "to_recur": ((cblk, channels), F32),
+        "to_inject": ((cblk, channels), F32),
+        "to_o": ((cblk, width), F32),
+        "to_hidden": ((blk, GROUP * hid), F32),
+        "to_upward": ((blk, GROUP * hid), F32),
+        "to_d": ((fblk, width), F32),
+        "to_gain_one": ((blk,), F32),
+        "to_gain_two": ((blk,), F32),
+        "to_taps": ((4, cblk), F32),
+        "to_cbias": ((cblk,), F32),
+        "to_rbias": ((cblk,), F32),
+        "to_ibias": ((cblk,), F32),
+        "to_decay": ((cblk,), F32),
+    }
+    done = pl.pallas_call(
+        functools.partial(finish, [*list(outputs)[2:], *finals]),
+        out_shape=shapes(finals),
+        in_specs=[in_vmem] * (len(outputs) - 2),
+        out_specs=[in_vmem] * len(finals),
+        name="finish",
+    )(*got[2:])
     return (
-        out.reshape(count, here, width),
-        gin.reshape(count, here, width),
-        first[:blk],
-        second[:blk],
-        first[blk:],
-        second[blk:],
-        g_o,
-        hidden,
-        upward,
-        g_d,
-        gain_mine[0],
-        gain_mine[1],
-        mine[0:4],
-        mine[4],
-        mine[5],
-        mine[6],
-        mine[7] * slope,
+        got[0].reshape(count, here, width),
+        got[1].reshape(count, here, width),
+        *done,
     )
 
 

time: 390 us -> 296 us (0.76)
  Pallas kernels: 352 us -> 292 us
  local copies, waits for them, and re-layouts: 31.6 us -> 2.57 us
    pallas_call x1 -> x2, Pallas kernels: 352 us -> 292 us  [the longest x1 288 us: split_block(): pl.pallas_call(functools.partial(fused, names), out_shape=shapes(outputs)...]
    slice x13 -> x0, local copies, waits for them, and re-layouts: 10.3 us -> none  [the longest x3 2.57 us: split_block(): first[blk:]]
    unnamed x54 -> x6, local copies, waits for them, and re-layouts: 12 us -> 2.57 us
where the time goes in v2:
time: 296 us; the launch traced here: 295 us
  Pallas kernels  292 us (99%)
    pallas_call x1, Pallas kernels, split_block(): pl.pallas_call(functools.partial(fused, names), out_shape=shapes(outputs)...  288 us

profile of v2, /device:TPU:0, one launch (start us, length us, event | category | flops | bytes accessed | tf_op | source)
XLA Modules:
  0.0 295.5 jit_solution(13915209879542855163)
XLA Ops:
  0.7 287.5 %block.1 = (f32[256,1024]{1,0:T(8,128)}, f32[256,1024]{1,0:T(8,128)}, bf16[320,768]{1,0:T(8,128)(2,1)}, bf16[128,1536]{1,0:T(8,128)(2,1)}, f32[48,1024]{1,0:T(8,...) custom-call(f32[256,1024]{1,0:T(8,128)} %bitcast.4, f32[256,1024]{1,0:T(8,128)} %bitcast.5, s32[2,128]{1,0:T(2,128)} %refs_2_.1, ...), custom_call_target="tpu_custom_call" | custom-call | tf_op jit(solution)/shard_map/block/pallas_call | solution.py:1414
  288.2 0.0 copy-start.1
  288.2 4.7 %finish.1 = (f32[32,1536]{1,0:T(8,128)}, f32[32,1536]{1,0:T(8,128)}, f32[48,1536]{1,0:T(8,128)}, f32[48,1536]{1,0:T(8,128)}, f32[48,1024]{1,0:T(8,128)}, /*index...) custom-call(bf16[320,768]{1,0:T(8,128)(2,1)} %get-tuple-element.41.r, ...), custom_call_target="tpu_custom_call" | custom-call | tf_op jit(solution)/shard_map/finish/pallas_call | solution.py:1444
  292.9 0.0 copy-done.1
  292.9 0.0 copy-start
  292.9 1.0 copy.37
  293.9 0.6 copy-done
  294.5 1.0 copy.38
Async XLA Ops:
  288.2 4.7 %copy-start.1 = (f32[256,1024]{1,0:T(8,128)S(1)}, f32[256,1024]{1,0:T(8,128)}, u32[]{:S(2)}) copy-start(f32[256,1024]{1,0:T(8,128)} %get-tuple-element.39) | copy-start | bytes 3145732
  292.9 1.6 copy-start

commit v3 on v2

--- a/solution.py
+++ b/solution.py
@@ -10,8 +10,8 @@
 EPSILON = 1e-06
 DECAY_SCALE = 8.0
 FLOOR_TERM = 0.01
-SLOTS = 240
-VMEM_BYTES = 62 << 20
+SLOTS = 360
+VMEM_BYTES = 63 << 20
 
 
 def shifted(array, axis, by):
@@ -304,8 +304,7 @@
 LANES = 128
 EDGE = 8
 STEP = 32
-DEPTH, PAIR, GROUP = (4, 2, 4)
-RING = DEPTH * PAIR
+GROUP, RING = (4, 8)
 
 
 def dot_nn(left, right):
@@ -383,7 +382,7 @@
     out_hbm, gin_hbm, fin, fin_hu, g_o, g_d, g_vec = (
         r[k] for k in ("out", "gin", "fin", "fin_hu", "g_o", "g_d", "g_vec")
     )
-    x, cot, out, gin, vec, gains = (r[k] for k in ("x", "cot", "out_own", "gin_own", "vec", "gains"))
+    x, cot, out, gin, vec, gains = (r[k] for k in ("x", "cot", "out_own", "cot", "vec", "gains"))
     w_one, w_ri, w_o, w_hu, w_d = (r[k] for k in ("w_one", "w_ri", "w_o", "w_hu", "w_d"))
     norm, gout, norm_two, gres, conv, mix = (
         r[k] for k in ("norm", "gout", "norm_two", "gres", "conv", "mix")
@@ -405,21 +404,27 @@
     groups = [slice(g * LANES, (g + 1) * LANES) for g in range(chans // LANES)]
     marks = slice(chans, chans + LANES)
 
-    s = lax.axis_index("seq")
-    b = lax.axis_index("batch")
-    z, y = (s // PAIR, s % PAIR)
-    mate, across, corner = (
-        (b // 2) * 2 + (1 - b % 2),
-        (1 - b // 2) * 2 + b % 2,
-        (1 - b // 2) * 2 + (1 - b % 2),
-    )
+    s, b = (lax.axis_index("seq"), lax.axis_index("batch"))
+    mate, across = (b + 1 - 2 * (b % 2), b + 2 - 4 * (b // 2))
+    corner = across + 1 - 2 * (b % 2)
     to_mate, to_across, to_corner = ((s, mate), (s, across), (s, corner))
     group_peers = [(mate, to_mate), (across, to_across), (corner, to_corner)]
-    to_pair = (z * PAIR + 1 - y, b)
-    far = [lax.rem(z + k, DEPTH) for k in range(DEPTH)]
-    near = [lax.rem(z + DEPTH - k, DEPTH) for k in range(DEPTH)]
+    flips = {"h": 4 - 8 * (s // 4), "l": 2 - 4 * (s // 2 % 2), "y": 1 - 2 * (s % 2)}
+
+    def turned(axes):
+        place = s
+        for axis in axes:
+            place = place + flips[axis]
+        return place
+
+    def reach(axes):
+        return (turned(axes), b)
+
     ring_to = [lax.rem(s + k, RING) for k in range(RING)]
     ring_from = [lax.rem(s + RING - k, RING) for k in range(RING)]
+
+    def ring_device(q):
+        return (q, b)
 
     def fetch(slot, src, dst):
         copy = pltpu.make_async_copy(src, dst, r["local"].at[slot])
@@ -445,10 +450,8 @@
             for j, side in enumerate(sides)
         ]
         place += 2 * blk
-    fetched["own"] = [
-        fetch(12, r["hbm_w_output"], w_o.at[at(s * cblk, cblk, 16)]),
-        fetch(13, r["hbm_w_down"], w_d.at[at(s * fblk, fblk, 16)]),
-    ]
+    fetched["own_o"] = [fetch(12, r["hbm_w_output"], w_o.at[at(s * cblk, cblk, 16)])]
+    fetched["own_d"] = [fetch(13, r["hbm_w_down"], w_d.at[at(s * fblk, fblk, 16)])]
     fetched["vec"] = [fetch(14, r["hbm_conv_taps"], r["taps"])] + [
         fetch(15 + k, r["hbm_" + name], r["biases"].at[k])
         for k, name in enumerate(("conv_bias", "recur_bias", "inject_bias", "decay_param"))
@@ -464,69 +467,89 @@
     for _, to in group_peers:
         pl.semaphore_signal(barrier, inc=1, device_id=to, device_id_type=MESH)
     for k in range(1, RING):
-        pl.semaphore_signal(barrier, inc=1, device_id=(ring_to[k], b), device_id_type=MESH)
+        pl.semaphore_signal(barrier, inc=1, device_id=ring_device(ring_to[k]), device_id_type=MESH)
 
     class Chunk:
         pass
 
-    def chunk(block, piece, pieces, y_block, y_piece, z_block, z_piece):
+    def chunk(axes, block, piece, pieces, first_sum, later_sum):
         c = Chunk()
-        c.block, c.piece, c.pieces = (block, piece, pieces)
-        c.y_block, c.y_piece, c.z_block, c.z_piece = (y_block, y_piece, z_block, z_piece)
-        c.gather_z = net.slots(DEPTH)
-        c.gather_y = net.slots(DEPTH)
-        c.sum_y = net.slots(DEPTH)
-        c.sum_z = net.slots(DEPTH)
-        c.spread = net.slots(3)
-        c.home = net.slots(3)
+        c.axes, c.back, c.block, c.piece, c.pieces = (axes[:3], axes[-3:], block, piece, pieces)
+        c.first_sum, c.later_sum = (first_sum, later_sum)
+        c.gather, c.sums = (net.slots(7), net.slots(7))
+        c.spread, c.home = (net.slots(3), net.slots(3))
         return c
 
-    def flat_chunk(ref, size, step, cols, y_ref, z_ref):
-        def row(base, i):
-            return (at(base * size + i * step, step, 16), cols)
-
+    def tall_chunk(axes, ref, size, first_ref, later_ref):
         return chunk(
-            lambda q: ref.at[at(q * size, size, 16), cols],
-            lambda q, i: ref.at[row(q, i)],
-            size // step,
-            lambda q: y_ref.at[at(q * size, size, 16), slice(0, cols.stop - cols.start)],
-            lambda q, i: y_ref.at[at(q * size + i * step, step, 16), slice(0, cols.stop - cols.start)],
-            lambda q: z_ref.at[pl.ds(q * size, size), slice(0, cols.stop - cols.start)],
-            lambda q, i: z_ref.at[at(q * size + i * step, step, 16), slice(0, cols.stop - cols.start)],
+            axes,
+            lambda q: ref.at[at(q * size, size, 16)],
+            lambda q, i: ref.at[at(q * size + i * 16, 16, 16)],
+            size // 16,
+            lambda k: first_ref.at[pl.ds(k * size, size)],
+            lambda k: later_ref.at[pl.ds(k * size, size)],
         )
 
+    def wide_chunk(axes, ref, cols, first_ref, later_ref):
+        return chunk(
+            axes,
+            lambda q: ref.at[q, :, cols],
+            lambda q, i: ref.at[q, at(i * 16, 16, 16), cols],
+            GROUP * blk // 16,
+            lambda k: first_ref.at[k],
+            lambda k: later_ref.at[k],
+        )
+
+    class Late:
+        def __init__(self, first, cols):
+            self.first, self.cols, self.at = (first, cols, self)
+
+        def __getitem__(self, k):
+            size = GROUP * blk
+            return norm_two.at[pl.ds((self.first + k) * size, size), self.cols]
+
+    tokens = rows * here
     two = 2 * chans
-    size_one = GROUP * blk
-    one = flat_chunk(
-        w_one, size_one, blk, slice(0, two), norm_two, norm_two.at[pl.ds(DEPTH * size_one, (DEPTH - 1) * size_one)]
-    )
+    gate_side, in_side = (slice(0, chans), slice(chans, two))
+    gat = wide_chunk("hly", w_one, gate_side, None, None)
+    gat_sum = wide_chunk("hly", r["dw_gate"], gate_side, Late(0, gate_side), Late(4, gate_side))
+    inp = wide_chunk("hly", w_one, in_side, None, None)
+    inp_sum = wide_chunk("hly", r["dw_in"], gate_side, Late(0, in_side), Late(4, in_side))
     ri = chunk(
+        "hly hyl",
         lambda q: w_ri.at[:, q],
         lambda q, i: w_ri.at[i, q],
         GROUP,
-        lambda q: r["y_ri"].at[q],
-        lambda q, i: r["y_ri"].at[q, i],
-        lambda q: r["z_ri"].at[q],
-        lambda q, i: r["z_ri"].at[q, i],
-    )
-    wo = flat_chunk(w_o, cblk, 16, slice(0, width), r["y_o"], r["z_o"])
-    hi = flat_chunk(w_hu, size_one, blk, slice(0, hid), r["y_h"], r["z_h"])
-    up = flat_chunk(w_hu, size_one, blk, slice(hid, 2 * hid), r["y_u"], r["z_u"])
-    dn = flat_chunk(w_d, fblk, 16, slice(0, width), r["y_d"], r["z_d"])
+        lambda k: r["y_ri"].at[k],
+        lambda k: r["z_ri"].at[k],
+    )
+    wo = tall_chunk("hly", w_o, cblk, r["y_o"], r["z_o"])
+    hi = wide_chunk("hly", w_hu, slice(0, hid), r["y_h"], r["z_h"])
+    up = wide_chunk("hly", w_hu, slice(hid, 2 * hid), r["y_u"], r["z_u"])
+    dn = tall_chunk("hyl", w_d, fblk, None, None)
+    dn_sum = tall_chunk("hyl", r["dw_d"], fblk, r["y_d"], r["z_d"])
+
+    def cube_place(ref, cols):
+        return lambda q: ref.at[s, at(q * blk, blk, 16), cols]
 
     rec = blk + cblk
     xhu = gri.at[pl.ds(GROUP * rec, 2 * GROUP * blk)]
-    one.source = lambda q: gri.at[at(q * rec, blk, 16)]
-    one.place = lambda q: w_one.at[at(s * size_one + q * blk, blk, 16)]
-    one.result = lambda q: fin.at[at(q * rec, blk, 16)]
+    gat.source = lambda q: gri.at[at(q * rec, blk, 16), gate_side]
+    gat.place = cube_place(w_one, gate_side)
+    gat_sum.place = cube_place(r["dw_gate"], gate_side)
+    gat_sum.result = lambda q: fin.at[at(q * rec, blk, 16), gate_side]
+    inp.source = lambda q: gri.at[at(q * rec, blk, 16), in_side]
+    inp.place = cube_place(w_one, in_side)
+    inp_sum.place = cube_place(r["dw_in"], gate_side)
+    inp_sum.result = lambda q: fin.at[at(q * rec, blk, 16), in_side]
     ri.source = lambda q: gri.at[at(q * rec + blk, cblk, 16)]
     ri.place = lambda q: w_ri.at[q, s]
     ri.result = lambda q: fin.at[at(q * rec + blk, cblk, 16)]
     hi.source = lambda q: xhu.at[at(q * blk, blk, 16)]
-    hi.place = lambda q: w_hu.at[at(s * size_one + q * blk, blk, 16), slice(0, hid)]
+    hi.place = cube_place(w_hu, slice(0, hid))
     hi.result = lambda q: fin_hu.at[at(q * blk, blk, 16), slice(0, hid)]
     up.source = lambda q: xhu.at[at((GROUP + q) * blk, blk, 16)]
-    up.place = lambda q: w_hu.at[at(s * size_one + q * blk, blk, 16), slice(hid, 2 * hid)]
+    up.place = cube_place(w_hu, slice(hid, 2 * hid))
     up.result = lambda q: fin_hu.at[at(q * blk, blk, 16), slice(hid, 2 * hid)]
 
     def member_cols(array, q, parts):
@@ -550,60 +573,82 @@
         for (peer, to), slot in zip(group_peers, c.spread):
             net.got(c.place(peer), to, slot)
 
-    def gz(c, *which):
-        for k in which:
-            net.put(c.block(s), c.block(s), (far[k] * PAIR + y, b), c.gather_z[k])
-
-    def gy(c):
-        net.put(c.block(s), c.block(s), to_pair, c.gather_y[0])
-
-    def gr(c, *which):
-        for k in which:
-            from_z = near[k] * PAIR + y
-            net.got(c.block(from_z), (from_z, b), c.gather_z[k])
-            net.put(c.block(from_z), c.block(from_z), to_pair, c.gather_y[k])
+    def g0(c, *which):
+        for slot in which or range(3):
+            axis = c.axes[slot]
+            net.put(c.block(s), c.block(s), reach(axis), c.gather[slot])
+
+    def g1(c):
+        i, j, k = c.axes
+        net.got(c.block(turned(i)), reach(i), c.gather[0])
+        net.put(c.block(turned(i)), c.block(turned(i)), reach(j), c.gather[3])
+        net.put(c.block(turned(i)), c.block(turned(i)), reach(k), c.gather[4])
+
+    def g2(c):
+        i, j, k = c.axes
+        net.got(c.block(turned(j)), reach(j), c.gather[1])
+        net.put(c.block(turned(j)), c.block(turned(j)), reach(k), c.gather[5])
+
+    def g3(c):
+        i, j, k = c.axes
+        net.got(c.block(turned(i + j)), reach(j), c.gather[3])
+        net.put(c.block(turned(i + j)), c.block(turned(i + j)), reach(k), c.gather[6])
 
     def gather_wait(c):
-        for k in range(DEPTH):
-            net.got(c.block(near[k] * PAIR + 1 - y), to_pair, c.gather_y[k])
+        i, j, k = c.axes
+        for slot, axes in ((2, k), (4, i + k), (5, j + k), (6, i + j + k)):
+            net.got(c.block(turned(axes)), reach(k), c.gather[slot])
 
     def sp(c, *which):
-        for k in which:
-            net.put(c.block(far[k] * PAIR + 1 - y), c.y_block(far[k]), to_pair, c.sum_y[k])
+        i, j, k = c.back
+        for slot in which:
+            axes = ("", i, j, i + j)[slot]
+            net.put(c.block(turned(axes + k)), c.first_sum(slot), reach(k), c.sums[slot], "sum")
+
+    def added(c, axes, parts, keep):
+        def add(i):
+            total = c.piece(turned(axes), i)[...].astype(F32)
+            for ref in parts:
+                total = total + part_of(c, ref, i).astype(F32)
+            keep(i, total)
+
+        loop(c.pieces, add)
+
+    def part_of(c, ref, i):
+        if len(ref.shape) == 2:
+            return ref[at(i * 16, 16, 16), :]
+        return ref[i]
+
+    def back_to(c, axes):
+        def keep(i, total):
+            c.piece(turned(axes), i)[...] = total.astype(BF16)
+
+        return keep
 
     def se(c, *which):
-        for k in which:
-            sum_pair_end(c, k)
-
-    def sum_pair_end(c, k):
-        net.got(c.y_block(far[k]), to_pair, c.sum_y[k])
-        mine = far[k] * PAIR + y
-
-        def add(i):
-            total = c.piece(mine, i)[...].astype(F32) + c.y_piece(far[k], i)[...].astype(F32)
-            c.piece(mine, i)[...] = total.astype(BF16)
-
-        loop(c.pieces, add)
-        if k:
-            net.put(c.block(mine), c.z_block(k - 1), (mine, b), c.sum_z[k])
+        i, j, k = c.back
+        for slot in which:
+            axes = {2: j, 3: i + j}[slot]
+            net.got(c.first_sum(slot), reach(k), c.sums[slot])
+            added(c, axes, [c.first_sum(slot)], back_to(c, axes))
+            net.put(c.block(turned(axes)), c.later_sum(slot - 2), reach(j), c.sums[slot + 2], "sum")
+
+    def sf(c):
+        i, j, k = c.back
+        net.got(c.first_sum(1), reach(k), c.sums[1])
+        net.got(c.later_sum(1), reach(j), c.sums[5])
+        added(c, i, [c.first_sum(1), c.later_sum(1)], back_to(c, i))
+        net.put(c.block(turned(i)), c.later_sum(2), reach(i), c.sums[6], "sum")
 
     def sum_end(c, keep):
-        for k in range(1, DEPTH):
-            net.got(c.z_block(k - 1), (near[k] * PAIR + y, b), c.sum_z[k])
-
-        def add(i):
-            total = c.piece(s, i)[...].astype(F32)
-            for k in range(DEPTH - 1):
-                total = total + c.z_piece(k, i)[...].astype(F32)
-            keep(i, total)
-
-        loop(c.pieces, add)
+        i, j, k = c.back
+        net.got(c.first_sum(0), reach(k), c.sums[0])
+        net.got(c.later_sum(0), reach(j), c.sums[4])
+        net.got(c.later_sum(2), reach(i), c.sums[6])
+        added(c, "", [c.first_sum(0), c.later_sum(0), c.later_sum(2)], keep)
 
     def sum_end_spread(c):
-        def keep(i, total):
-            c.piece(s, i)[...] = total.astype(BF16)
-
-        sum_end(c, keep)
+        sum_end(c, back_to(c, ""))
         for (peer, to), slot in zip(group_peers, c.home):
             net.put(c.place(peer), c.result(b), to, slot)
         c.result(b)[...] = c.place(b)[...]
@@ -707,33 +752,49 @@
     norm_rows, gout_rows, two_rows, gres_rows = (token_rows(ref) for ref in (norm, gout, norm_two, gres))
     conv_cols = lambda q, h: conv.at[pl.ds(h * half, half), at(q * chans, chans, LANES)]
 
-    fetch_wait("w_gate", "w_input")
-    prepare(one, blk, cblk, "w_gate", "w_input")
+    fetch_wait("w_input", "own_o")
+    prepare(inp, blk, cblk, "w_input")
     fetch_wait("x", "seg", "gain_one", "gain_two")
     gain_one, gain_two = (gains[0:1], gains[1:2])
     pl.semaphore_wait(barrier, 3 + RING - 1)
-    spread(one)
-    for h in range(2):
+    spread(inp)
+
+    def norm_half(h):
         ids = r["seg"][h : h + 1, :].astype(F32)
         norm[at((h * GROUP + b) * here, here, 16), width : width + LANES] = jnp.transpose(
             jnp.broadcast_to(ids, (here, here))
         ).astype(BF16)
 
-        def norm_tile(i, h=h):
+        def norm_tile(i):
             v = own(x, h, i)[...]
             sixteen(norm_rows(b, h), i)[:, 0:width] = (v * rms(v) * gain_one).astype(BF16)
 
         loop(tiles16, norm_tile)
-        share(norm_rows, norm_slots, h)
+
+    fetch_wait("w_gate")
+    prepare(gat, blk, cblk, "w_gate")
+    spread(gat)
     fetch_wait("w_recur", "w_inject")
     prepare(ri, cblk, cblk, "w_recur", "w_inject")
     spread(ri)
-    spread_wait(one)
-    gz(one, 1, 3, 2)
-    gy(one)
+    spread_wait(inp)
+    g0(inp)
+    norm_half(0)
+    share(norm_rows, norm_slots, 0)
+    spread_wait(gat)
+    g0(gat)
+    norm_half(1)
+    share(norm_rows, norm_slots, 1)
+    g1(inp)
+    g2(inp)
     fetch_wait("w_hidden")
     prepare(hi, blk, fblk, "w_hidden")
+    g1(gat)
+    g3(inp)
     spread(hi)
+    spread_wait(ri)
+    g0(ri)
+    g2(gat)
     fetch_wait("w_upward")
     prepare(up, blk, fblk, "w_upward")
     spread(up)
@@ -760,55 +821,55 @@
     def _():
         tgx[:, here : here + EDGE, :] = jnp.full((rows, EDGE, chans + LANES), -1.0, F32)
 
-    gr(one, 1)
     share_relay(norm_rows, norm_slots, 0)
-    gr(one, 3)
     fetch_wait("cot")
     for h in range(2):
         def low_tile(i, h=h):
             sixteen(gout_rows(b, h), i)[...] = own(cot, h, i)[...].astype(BF16)
 
         loop(tiles16, low_tile)
-    share_relay(norm_rows, norm_slots, 1)
-    gr(one, 2)
-    spread_wait(ri)
-    gy(ri)
-    gz(ri, 1)
+    gather_wait(inp)
     share_end(norm_rows, norm_slots, 0)
-    gather_wait(one)
 
     for h in range(2):
         if h:
+            share_relay(norm_rows, norm_slots, h)
             share_end(norm_rows, norm_slots, h)
         span = pl.ds(h * half, half)
         block = slice(h * GROUP, (h + 1) * GROUP)
-        got = dot_nn(norm[span, 0:width], w_one[...]).reshape(GROUP, here, two)
-        gate_pre[block] = got[:, :, 0:chans]
-        brx[block, EDGE : EDGE + here, 0:chans] = got[:, :, chans:two]
+        got = dot_nn(norm[span, 0:width], w_one[:, :, in_side].reshape(width, chans))
+        brx[block, EDGE : EDGE + here, 0:chans] = got.reshape(GROUP, here, chans)
         ids = norm[span, width : width + LANES].astype(F32).reshape(GROUP, here, LANES)
         brx[block, EDGE : EDGE + here, marks] = ids
         tgx[block, 0:here, marks] = ids
 
-    def halo_out():
-        return pltpu.make_async_remote_copy(
-            src_ref=brx.at[:, pl.ds(here, EDGE)],
-            dst_ref=brx.at[:, pl.ds(0, EDGE)],
-            send_sem=net.send.at[halo_slot],
-            recv_sem=net.recv.at[halo_slot],
-            device_id=(ring_to[1], b),
-            device_id_type=MESH,
-        )
-
-    @pl.when(s < RING - 1)
-    def _():
-        halo_out().start()
-
-    gz(ri, 3, 2)
-    gr(ri, 1)
-
-    @pl.when(s > 0)
-    def _():
-        net.got(brx.at[:, pl.ds(0, EDGE)], (ring_from[1], b), halo_slot)
+    def edge_copies(ref, src, dst, slot, step, gives, takes):
+        def copy(where):
+            return pltpu.make_async_remote_copy(
+                src_ref=ref.at[:, pl.ds(src, EDGE)],
+                dst_ref=ref.at[:, pl.ds(dst, EDGE)],
+                send_sem=net.send.at[slot],
+                recv_sem=net.recv.at[slot],
+                device_id=(where, b),
+                device_id_type=MESH,
+            )
+
+        def out(act):
+            @pl.when(gives)
+            def _():
+                act(copy(lax.rem(s + step, RING)))
+
+        def arrive():
+            @pl.when(takes)
+            def _():
+                copy(lax.rem(s + RING - step, RING)).wait_recv()
+
+        return (out, arrive)
+
+    edge_out, edge_in = edge_copies(brx, here, 0, halo_slot, 1, s < RING - 1, s > 0)
+    edge_out(lambda one: one.start())
+    g3(gat)
+    edge_in()
 
     for h in range(2):
         def conv_tile(q, start, lanes, g):
@@ -821,20 +882,15 @@
 
         over(h, conv_tile)
         share(conv_cols, conv_slots, h)
-    for h in range(2):
-        share(gout_rows, gout_slots, h)
-    gr(ri, 3)
-    fetch_wait("own")
-    gy(wo)
-    gz(wo, 1, 3, 2)
+        g2(ri) if h else g1(ri)
+    g3(ri)
+    g0(wo)
+    spread_wait(hi)
+    g0(hi)
     share_relay(conv_cols, conv_slots, 0)
-    spread_wait(hi)
-    gy(hi)
-    gr(ri, 2)
+    g1(wo)
+    g2(wo)
     share_relay(conv_cols, conv_slots, 1)
-    gr(wo, 1, 3, 2)
-    gz(hi, 1, 3)
-    spread_wait(up)
     share_end(conv_cols, conv_slots, 0)
     gather_wait(ri)
 
@@ -859,6 +915,10 @@
             stx[q, pl.ds(EDGE + start, STEP), lanes] = scale * ig * conv_out[q, span, lanes]
 
         over(h, gate_tile)
+        if h == 0:
+            g3(wo)
+        else:
+            spread_wait(up)
 
     def ends(p, state):
         mult = carry[:, p, :]
@@ -866,26 +926,39 @@
 
     begin = (jnp.ones((rows, chans), F32), jnp.zeros((rows, chans), F32))
     product, tail = lax.fori_loop(0, here, ends, begin, unroll=8)
-    pre_f[s, 0:rows] = product
-    pre_f[s, rows : 2 * rows] = tail
-    for k in range(1, RING):
-        net.put(pre_f.at[s], pre_f.at[s], (ring_to[k], b), pre_slots[k])
-    gr(hi, 1, 3)
-    gz(hi, 2)
-    gy(up)
-    gz(up, 1)
-
-    for h in range(2):
+    def hand_round(ref, product, tail, slots):
+        ref[s, 0:rows] = product
+        ref[s, rows : 2 * rows] = tail
+        for k in range(1, RING):
+            net.put(ref.at[s], ref.at[s], ring_device(ring_to[k]), slots[k])
+
+    def entering(ref, slots, forward):
+        for k in range(1, RING):
+            net.got(ref.at[ring_from[k]], ring_device(ring_from[k]), slots[k])
+        state = jnp.zeros((rows, chans), F32)
+        for q in range(RING - 1) if forward else range(RING - 1, 0, -1):
+            longer = ref[q, rows : 2 * rows] + ref[q, 0:rows] * state
+            state = jnp.where(q < s if forward else q > s, longer, state)
+        return state
+
+    hand_round(pre_f, product, tail, pre_slots)
+    g1(hi)
+    g2(hi)
+    g0(up)
+    fetch_wait("own_d")
+    g0(dn)
+    gather_wait(gat)
+
+    for h in range(2):
+        got = dot_nn(norm[pl.ds(h * half, half), 0:width], w_one[:, :, gate_side].reshape(width, chans))
+        gate_pre[h * GROUP : (h + 1) * GROUP] = got.reshape(GROUP, here, chans)
+
         def act_tile(q, start, lanes, g):
             span = pl.ds(start, STEP)
             tgx[q, span, lanes] = gelu_parts(gate_pre[q, span, lanes])[0]
 
         over(h, act_tile)
-    for k in range(1, RING):
-        net.got(pre_f.at[ring_from[k]], (ring_from[k], b), pre_slots[k])
-    state = jnp.zeros((rows, chans), F32)
-    for q in range(RING - 1):
-        state = jnp.where(q < s, pre_f[q, rows : 2 * rows] + pre_f[q, 0:rows] * state, state)
+    state = entering(pre_f, pre_slots, True)
     stx[:, EDGE - 1, :] = state
 
     def scan(p, state):
@@ -894,6 +967,7 @@
         return state
 
     lax.fori_loop(0, here, scan, state, unroll=8)
+    g3(hi)
     gather_wait(wo)
 
     for h in range(2):
@@ -905,16 +979,9 @@
         span = pl.ds(h * half, half)
         part[span, :] = dot_nn(mix[span, :], w_o[...]).astype(BF16)
         merge(part_rows, first_in, out_slots, h)
-    gr(hi, 2)
-    gr(up, 1)
-    gz(up, 3, 2)
-    for h in range(2):
-        share_relay(gout_rows, gout_slots, h)
     for h in range(2):
         merge_relay(part_rows, first_in, second_in, out_slots, h, tiles16, sixteen)
-    gr(up, 3)
-    gy(dn)
-    gz(dn, 1, 3, 2)
+    g1(up)
     for h in range(2):
         merge_end(first_in, second_in, out_slots, h)
 
@@ -926,9 +993,13 @@
         loop(tiles16, resid_tile)
         share(two_rows, two_slots, h)
         if h == 0:
-            gr(up, 2)
+            g2(up)
+            g1(dn)
+    for h in range(2):
+        share(gout_rows, gout_slots, h)
+    g3(up)
+    g2(dn)
     share_relay(two_rows, two_slots, 0)
-    gr(dn, 1)
     share_relay(two_rows, two_slots, 1)
     gather_wait(hi)
     gather_wait(up)
@@ -939,8 +1010,8 @@
         for j in range(hid // 256):
             left = slice(j * 256, j * 256 + 256)
             right = slice(hid + j * 256, hid + j * 256 + 256)
-            pre[:, 0:256] = dot_nn(norm_two[span, :], w_hu[:, left])
-            pre[:, 256:512] = dot_nn(norm_two[span, :], w_hu[:, right])
+            pre[:, 0:256] = dot_nn(norm_two[span, :], w_hu[:, :, left].reshape(width, 256))
+            pre[:, 256:512] = dot_nn(norm_two[span, :], w_hu[:, :, right].reshape(width, 256))
 
             def tile(i, h=h, j=j):
                 rows_t = at(i * STEP, STEP, STEP)
@@ -955,14 +1026,18 @@
                     ghu[flat_t, second] = act.astype(BF16)
 
             loop(half // STEP, tile)
+        share_relay(gout_rows, gout_slots, h)
         if h == 0:
-            gr(dn, 3)
-    gr(dn, 2)
+            g3(dn)
     for h in range(2):
         share_end(gout_rows, gout_slots, h)
+    for j in range(2):
+        cols = slice(j * hid // 2, (j + 1) * hid // 2)
+        r["dw_d"][cols, :] = dot_tn(prod[:, cols], gout[...]).astype(BF16)
+    sp(dn_sum, 3, 2, 1, 0)
     gather_wait(dn)
 
-    net.flush()
+    net.flush("part")
     for h in range(2):
         span = pl.ds(h * half, half)
         for j in range(hid // 256):
@@ -973,19 +1048,26 @@
             ghu[span, right] = (back * ghu[span, right].astype(F32)).astype(BF16)
         for j in range(2):
             cols = slice(j * width // 2, (j + 1) * width // 2)
-            part[span, cols] = dot_nt(ghu[span, :], w_hu[cols, :]).astype(BF16)
+            part[span, cols] = dot_nt(ghu[span, :], w_hu[4 * j : 4 * j + 4].reshape(width // 2, 2 * hid)).astype(BF16)
         merge(part_rows, first_in, gnt_slots, h)
     for h in range(2):
         merge_relay(part_rows, first_in, second_in, gnt_slots, h, tiles16, sixteen)
 
+    se(dn_sum, 3)
+    net.flush("")
     for j in range(2):
         def grad_hu(i, j=j):
             cols = at(i * 256, 256, LANES)
             side = slice(j * hid, (j + 1) * hid)
-            w_hu[at(i * 256, 256, 16), side] = dot_tn(norm_two[:, cols], ghu[:, side]).astype(BF16)
+            got = dot_tn(norm_two[:, cols], ghu[:, side]).astype(BF16)
+            w_hu[pl.ds(2 * i, 2), :, side] = got.reshape(2, GROUP * blk, hid)
 
         loop(width // 256, grad_hu)
-        sp(up if j else hi, 1, 3, 2, 0) if j == 0 else sp(up, 1, 3)
+        if j == 0:
+            sp(hi, 3, 2, 1, 0)
+            se(dn_sum, 2)
+        else:
+            sp(up, 3)
 
     for h in range(2):
         merge_end(first_in, second_in, gnt_slots, h)
@@ -999,23 +1081,27 @@
         loop(tiles16, second_norm)
         share(gres_rows, gres_slots, h)
         if h == 0:
-            se(hi, 1, 3)
+            sf(dn_sum)
     net.flush("part")
     for h in range(2):
         span = pl.ds(h * half, half)
         part[span, :] = dot_nn(prod[span, :], w_d[...]).astype(BF16)
     share_relay(gres_rows, gres_slots, 0)
-    for j in range(2):
-        cols = slice(j * hid // 2, (j + 1) * hid // 2)
-        w_d[cols, :] = dot_tn(prod[:, cols], gout[...]).astype(BF16)
-    se(hi, 2, 0)
+    se(hi, 3)
     share_relay(gres_rows, gres_slots, 1)
+    se(hi, 2)
 
     for h in range(2):
         share_end(gres_rows, gres_slots, h)
+        if h:
+            for k in range(2):
+                merge(part_rows, first_in, down_slots, k)
         block = slice(h * GROUP, (h + 1) * GROUP)
         got = dot_nt(gres[pl.ds(h * half, half), :], w_o[...])
         tgx[block, 0:here, 0:chans] = got.reshape(GROUP, here, chans)
+        if h:
+            for k in range(2):
+                merge_relay(part_rows, first_in, second_in, down_slots, k, tiles16, sixteen)
 
         def mix_back(q, start, lanes, g):
             span = pl.ds(start, STEP)
@@ -1033,26 +1119,16 @@
         return (state[0] * mult, mult * (tgx[:, p, 0:chans] + state[1]))
 
     product, tail = lax.fori_loop(0, here, ends_back, begin, unroll=8)
-    pre_b[s, 0:rows] = product
-    pre_b[s, rows : 2 * rows] = tail
-    for k in range(1, RING):
-        net.put(pre_b.at[s], pre_b.at[s], (ring_to[k], b), back_slots[k])
-    sp(up, 2, 0)
-    sp(dn, 1, 3)
-
-    for h in range(2):
-        merge(part_rows, first_in, down_slots, h)
+    hand_round(pre_b, product, tail, back_slots)
+    sp(up, 2, 1, 0)
 
     w_o[...] = dot_tn(mix[...], gres[...]).astype(BF16)
-    for h in range(2):
-        merge_relay(part_rows, first_in, second_in, down_slots, h, tiles16, sixteen)
-    se(up, 1, 3)
-
-    for k in range(1, RING):
-        net.got(pre_b.at[ring_from[k]], (ring_from[k], b), back_slots[k])
-    state = jnp.zeros((rows, chans), F32)
-    for q in range(RING - 1, 0, -1):
-        state = jnp.where(q > s, pre_b[q, rows : 2 * rows] + pre_b[q, 0:rows] * state, state)
+    for j in range(2):
+        cols = slice(j * width // 2, (j + 1) * width // 2)
+        got = dot_tn(norm[:, cols], ggb[:, gate_side]).astype(BF16)
+        r["dw_gate"][4 * j : 4 * j + 4] = got.reshape(4, GROUP * blk, chans)
+
+    state = entering(pre_b, back_slots, False)
 
     def scan_back(i, state):
         p = here - 1 - i
@@ -1062,6 +1138,8 @@
 
     lax.fori_loop(0, here, scan_back, state, unroll=8)
 
+    sp(gat_sum, 3, 2, 1, 0)
+    sp(wo, 3, 2, 1, 0)
     thru_cols = lambda q, h: ghu.at[pl.ds(h * half, half), at(q * chans, chans, LANES)]
     thru_first = lambda h, slot: prod.at[pl.ds(h * half, half), pl.ds(slot * chans, chans)]
     thru_second = lambda h: gout.at[pl.ds(h * half, half), pl.ds(0, chans)]
@@ -1102,8 +1180,8 @@
                 loop(tiles16, out_tile)
         merge(thru_cols, thru_first, thru_slots, h)
         if h == 0:
-            se(up, 2, 0)
-            sp(dn, 2, 0)
+            sf(hi)
+            se(up, 3)
     leave_out = fetch(0, out, out_hbm)
     for h in range(2):
         merge_relay(thru_cols, thru_first, thru_second, thru_slots, h, half // 16, sixteen)
@@ -1113,9 +1191,9 @@
         w_ri[i] = got.astype(BF16).reshape(RING, cblk, two)
 
     loop(GROUP, grad_ri)
-    se(dn, 1, 3)
-    sp(ri, 1)
-    se(dn, 2, 0)
+    sp(ri, 3)
+    se(up, 2)
+    se(gat_sum, 3, 2)
 
     for h in range(2):
         merge_end(thru_first, thru_second, thru_slots, h)
@@ -1127,28 +1205,15 @@
             tgx[q, pl.ds(start, STEP), lanes] += total
 
         over(h, conv_grad)
-
-    def halo_in():
-        return pltpu.make_async_remote_copy(
-            src_ref=tgx.at[:, pl.ds(0, EDGE)],
-            dst_ref=tgx.at[:, pl.ds(here, EDGE)],
-            send_sem=net.send.at[halo_back],
-            recv_sem=net.recv.at[halo_back],
-            device_id=(ring_from[1], b),
-            device_id_type=MESH,
-        )
-
-    @pl.when(s > 0)
-    def _():
-        halo_in().start()
-
-    sp(ri, 3, 2, 0)
-    sp(wo, 1, 3, 2, 0)
-
-    @pl.when(s < RING - 1)
-    def _():
-        net.got(tgx.at[:, pl.ds(here, EDGE)], (ring_to[1], b), halo_back)
-
+        if h == 0:
+            sf(up)
+
+    head_out, head_in = edge_copies(tgx, 0, here, halo_back, RING - 1, s > 0, s < RING - 1)
+    head_out(lambda one: one.start())
+    sp(ri, 2, 1, 0)
+    se(ri, 3)
+    head_in()
+    se(wo, 3, 2)
     net.flush("part")
     for h in range(2):
         def conv_back(q, start, lanes, g):
@@ -1166,21 +1231,23 @@
             ggb[flat(q, start), slice(chans + g * LANES, chans + (g + 1) * LANES)] = total.astype(BF16)
 
         over(h, conv_back)
+    for j in range(2):
+        cols = slice(j * width // 2, (j + 1) * width // 2)
+        got = dot_tn(norm[:, cols], ggb[:, in_side]).astype(BF16)
+        r["dw_in"][4 * j : 4 * j + 4] = got.reshape(4, GROUP * blk, chans)
+    sp(inp_sum, 3, 2, 1, 0)
+    for h in range(2):
         span = pl.ds(h * half, half)
         for j in range(2):
             cols = slice(j * width // 2, (j + 1) * width // 2)
-            part[span, cols] = dot_nt(ggb[span, :], w_one[cols, :]).astype(BF16)
+            part[span, cols] = dot_nt(ggb[span, :], w_one[4 * j : 4 * j + 4].reshape(width // 2, two)).astype(BF16)
         merge(part_rows, first_in, gn_slots, h)
     for h in range(2):
         merge_relay(part_rows, first_in, second_in, gn_slots, h, tiles16, sixteen)
 
-    def grad_one(i):
-        cols = at(i * 256, 256, LANES)
-        w_one[at(i * 256, 256, 16), :] = dot_tn(norm[:, cols], ggb[...]).astype(BF16)
-
-    loop(width // 256, grad_one)
-    sp(one, 1, 3, 2, 0)
-    se(ri, 1, 3)
+    se(ri, 2)
+    sf(gat_sum)
+    se(inp_sum, 3, 2)
 
     for h in range(2):
         merge_end(first_in, second_in, gn_slots, h)
@@ -1190,8 +1257,6 @@
             own(gin, h, i)[...] = own(gin, h, i)[...] + back
 
         loop(tiles16, first_norm)
-        if h == 0:
-            se(ri, 2, 0)
     leave_gin = fetch(1, gin, gin_hbm)
 
     for k in range(8):
@@ -1203,7 +1268,7 @@
         for j in range(4):
             vs[s, 4 * k + j : 4 * k + j + 1, chans : chans + piece] = total[:, j * piece : (j + 1) * piece]
     for k in range(1, RING):
-        net.put(vs.at[s], vs.at[s], (ring_to[k], b), vec_slots[k])
+        net.put(vs.at[s], vs.at[s], ring_device(ring_to[k]), vec_slots[k])
 
     def keep_down(i, total):
         g_d[at(i * 16, 16, 16), :] = total
@@ -1211,22 +1276,24 @@
     def keep_out(i, total):
         g_o[at(i * 16, 16, 16), :] = total
 
+    sf(ri)
+    sf(wo)
+    sum_end(dn_sum, keep_down)
     sum_end_spread(hi)
     sum_end_spread(up)
-    se(wo, 1, 3, 2, 0)
-    sum_end(dn, keep_down)
-    se(one, 1, 3, 2, 0)
+    sf(inp_sum)
+    sum_end_spread(gat_sum)
     sum_end_spread(ri)
     sum_end(wo, keep_out)
+    sum_end_spread(inp_sum)
     for k in range(1, RING):
-        net.got(vs.at[ring_from[k]], (ring_from[k], b), vec_slots[k])
+        net.got(vs.at[ring_from[k]], ring_device(ring_from[k]), vec_slots[k])
     total = vs[0]
     for q in range(1, RING):
         total = total + vs[q]
     vb[b] = total
     for (peer, to), slot in zip(group_peers, last_slots):
         net.put(vb.at[b], vb.at[b], to, slot)
-    sum_end_spread(one)
     for (peer, to), slot in zip(group_peers, last_slots):
         net.got(vb.at[peer], to, slot)
     g_vec[:, 0:chans] = total[:, 0:chans]
@@ -1234,19 +1301,14 @@
     for q in range(1, GROUP):
         summed = summed + vb[q, :, chans : chans + piece]
     g_vec[:, chans : chans + piece] = summed
-    for c in (hi, up, ri, one):
+    for c in (hi, up, gat_sum, inp_sum, ri):
         home_wait(c)
     net.flush()
     leave_out.wait()
     leave_gin.wait()
 
-    @pl.when(s < RING - 1)
-    def _():
-        halo_out().wait_send()
-
-    @pl.when(s > 0)
-    def _():
-        halo_in().wait_send()
+    edge_out(lambda one: one.wait_send())
+    head_out(lambda one: one.wait_send())
 
 
 def finish(names, *refs):
@@ -1321,7 +1383,6 @@
     tokens = GROUP * count * here
     rows = GROUP * count
     wide = chans + LANES
-    size_one = GROUP * blk
     operands = {
         "hbm_x": inputs.reshape(count * here, width),
         "hbm_cot": cotangent.reshape(count * here, width),
@@ -1356,17 +1417,19 @@
         "x": ((count * here, width), F32),
         "cot": ((count * here, width), F32),
         "out_own": ((count * here, width), F32),
-        "gin_own": ((count * here, width), F32),
         "seg": (segments.shape, jnp.int32),
         "gains": ((2, width), F32),
         "taps": (conv_taps.shape, F32),
         "biases": ((4, channels), F32),
         "vecs": ((GROUP, 16, chans), F32),
         "vec": ((16, chans), F32),
-        "w_one": ((width, 2 * chans), BF16),
+        "w_one": ((RING, GROUP * blk, 2 * chans), BF16),
+        "dw_gate": ((RING, GROUP * blk, chans), BF16),
+        "dw_in": ((RING, GROUP * blk, chans), BF16),
+        "dw_d": ((hid, width), BF16),
         "w_ri": ((GROUP, RING, cblk, 2 * chans), BF16),
         "w_o": ((chans, width), BF16),
-        "w_hu": ((width, 2 * hid), BF16),
+        "w_hu": ((RING, GROUP * blk, 2 * hid), BF16),
         "w_d": ((hid, width), BF16),
         "norm": ((tokens, width + LANES), BF16),
         "gout": ((tokens, width), BF16),
@@ -1392,16 +1455,16 @@
         "x_in": ((2, here, width), BF16),
         "pre_f": ((RING, 2 * rows, chans), F32),
         "pre_b": ((RING, 2 * rows, chans), F32),
-        "y_ri": ((DEPTH, GROUP, cblk, 2 * chans), BF16),
-        "z_ri": ((DEPTH - 1, GROUP, cblk, 2 * chans), BF16),
-        "y_o": ((DEPTH * cblk, width), BF16),
-        "z_o": (((DEPTH - 1) * cblk, width), BF16),
-        "y_h": ((DEPTH * size_one, hid), BF16),
-        "z_h": (((DEPTH - 1) * size_one, hid), BF16),
-        "y_u": ((DEPTH * size_one, hid), BF16),
-        "z_u": (((DEPTH - 1) * size_one, hid), BF16),
-        "y_d": ((DEPTH * fblk, width), BF16),
-        "z_d": (((DEPTH - 1) * fblk, width), BF16),
+        "y_ri": ((4, GROUP, cblk, 2 * chans), BF16),
+        "z_ri": ((3, GROUP, cblk, 2 * chans), BF16),
+        "y_o": ((4 * cblk, width), BF16),
+        "z_o": (((3) * cblk, width), BF16),
+        "y_h": ((4, GROUP * blk, hid), BF16),
+        "z_h": ((3, GROUP * blk, hid), BF16),
+        "y_u": ((4, GROUP * blk, hid), BF16),
+        "z_u": ((3, GROUP * blk, hid), BF16),
+        "y_d": ((4 * fblk, width), BF16),
+        "z_d": (((3) * fblk, width), BF16),
         "acc": ((8, 8, chans), F32),
         "gain_acc": ((2, 8, width), F32),
         "vs": ((RING, 8, chans + piece), F32),

time: 296 us -> 274 us (0.926)
  Pallas kernels: 292 us -> 270 us
    pallas_call x1, Pallas kernels: 288 us -> 265 us  [split_block(): pl.pallas_call(functools.partial(fused, names), out_shape=shapes(outputs)...]
where the time goes in v3:
time: 274 us; the launch traced here: 273 us
  Pallas kernels  270 us (99%)
    pallas_call x1, Pallas kernels, split_block(): pl.pallas_call(functools.partial(fused, names), out_shape=shapes(outputs)...  265 us

profile of v3, /device:TPU:0, one launch (start us, length us, event | category | flops | bytes accessed | tf_op | source)
XLA Modules:
  0.0 272.8 jit_solution(11750670193369756957)
XLA Ops:
  0.7 264.8 %block.1 = (f32[256,1024]{1,0:T(8,128)}, f32[256,1024]{1,0:T(8,128)}, bf16[320,768]{1,0:T(8,128)(2,1)}, bf16[128,1536]{1,0:T(8,128)(2,1)}, f32[48,1024]{1,0:T(8,...) custom-call(f32[256,1024]{1,0:T(8,128)} %bitcast.4, f32[256,1024]{1,0:T(8,128)} %bitcast.5, s32[2,128]{1,0:T(2,128)} %refs_2_.1, ...), custom_call_target="tpu_custom_call" | custom-call | tf_op jit(solution)/shard_map/block/pallas_call | solution.py:1477
  265.5 0.0 copy-start.1
  265.5 4.7 %finish.1 = (f32[32,1536]{1,0:T(8,128)}, f32[32,1536]{1,0:T(8,128)}, f32[48,1536]{1,0:T(8,128)}, f32[48,1536]{1,0:T(8,128)}, f32[48,1024]{1,0:T(8,128)}, /*index...) custom-call(bf16[320,768]{1,0:T(8,128)(2,1)} %get-tuple-element.41.r, ...), custom_call_target="tpu_custom_call" | custom-call | tf_op jit(solution)/shard_map/finish/pallas_call | solution.py:1507
  270.2 0.0 copy-done.1
  270.2 0.0 copy-start
  270.2 1.0 copy.37
  271.2 0.6 copy-done
  271.8 1.0 copy.38
Async XLA Ops:
  265.5 4.7 %copy-start.1 = (f32[256,1024]{1,0:T(8,128)S(1)}, f32[256,1024]{1,0:T(8,128)}, u32[]{:S(2)}) copy-start(f32[256,1024]{1,0:T(8,128)} %get-tuple-element.39) | copy-start | bytes 3145732
  270.2 1.6 copy-start

commit v4 on v3

--- a/solution.py
+++ b/solution.py
@@ -10,7 +10,7 @@
 EPSILON = 1e-06
 DECAY_SCALE = 8.0
 FLOOR_TERM = 0.01
-SLOTS = 360
+SLOTS = 390
 VMEM_BYTES = 63 << 20
 
 
@@ -300,6 +300,43 @@
 
 
 MESH = pl.DeviceIdType.MESH
+PLAN = {
+    "f1": ["wait inp", "g0 inp 012"],
+    "f2": ["wait gat", "g0 gat 012"],
+    "f3": ["g1 inp", "g2 inp"],
+    "f4": ["g1 gat", "g3 inp"],
+    "f5": ["wait ra", "g0 ra 012", "wait rb", "g0 rb 01", "g2 gat"],
+    "f91": ["g0 rb 2", "g1 ra", "g3 gat"],
+    "conv0": ["g1 rb", "g2 ra"],
+    "conv1": ["g2 rb", "g3 ra", "g3 rb", "g0 wo 012"],
+    "f10": ["g1 wo", "g2 wo", "wait hi", "g0 hi 012"],
+    "f11": ["g3 wo"],
+    "gate1": ["wait up"],
+    "f12": ["g1 hi", "g2 hi", "g0 up 012", "g0 dn 012"],
+    "f14": ["g3 hi", "g1 up"],
+    "resid0": ["g2 up", "g1 dn"],
+    "f15": ["g3 up", "g2 dn"],
+    "hid0": ["g3 dn"],
+    "f18": ["sp dn 3210"],
+    "b2": ["se dn 3"],
+    "grad0": ["sp hi 3210", "se dn 2"],
+    "grad1": ["sp up 3"],
+    "norm0": ["sf dn"],
+    "b4": ["se hi 3"],
+    "b5": ["se hi 2"],
+    "b6": ["sp up 210"],
+    "b8": ["sp gat 3210", "sp wo 3210"],
+    "thru0": ["sf hi", "se up 3"],
+    "b10": ["se up 2", "se gat 32"],
+    "edge0": ["sp ra 32", "sp rb 32", "sf up"],
+    "edge1": ["sp ra 10", "sp rb 10", "se ra 32", "se rb 3"],
+    "taps1": ["se wo 32"],
+    "b13": ["sp inp 3210"],
+    "b14": ["se rb 2", "sf ra"],
+    "first0": ["sf rb"],
+    "t0": ["se inp 32", "sf gat", "sf wo", "end dn", "end hi", "end up", "sf inp", "end gat", "end ra", "end rb"],
+    "t1": ["end wo", "end inp"],
+}
 F32, BF16 = (jnp.float32, jnp.bfloat16)
 LANES = 128
 EDGE = 8
@@ -512,17 +549,21 @@
     two = 2 * chans
     gate_side, in_side = (slice(0, chans), slice(chans, two))
     gat = wide_chunk("hly", w_one, gate_side, None, None)
-    gat_sum = wide_chunk("hly", r["dw_gate"], gate_side, Late(0, gate_side), Late(4, gate_side))
+    gat_sum = wide_chunk("hyl", r["dw_gate"], gate_side, Late(0, gate_side), Late(4, gate_side))
     inp = wide_chunk("hly", w_one, in_side, None, None)
     inp_sum = wide_chunk("hly", r["dw_in"], gate_side, Late(0, in_side), Late(4, in_side))
-    ri = chunk(
-        "hly hyl",
-        lambda q: w_ri.at[:, q],
-        lambda q, i: w_ri.at[i, q],
-        GROUP,
-        lambda k: r["y_ri"].at[k],
-        lambda k: r["z_ri"].at[k],
-    )
+    def gate_chunk(axes, cols, first_ref, later_ref):
+        return chunk(
+            axes,
+            lambda q: w_ri.at[:, q, :, cols],
+            lambda q, i: w_ri.at[i, q, :, cols],
+            GROUP,
+            lambda k: first_ref.at[k],
+            lambda k: later_ref.at[k],
+        )
+
+    ra = gate_chunk("hly hyl", gate_side, r["y_ra"], r["z_ra"])
+    rb = gate_chunk("hyl hly", in_side, r["y_rb"], r["z_rb"])
     wo = tall_chunk("hly", w_o, cblk, r["y_o"], r["z_o"])
     hi = wide_chunk("hly", w_hu, slice(0, hid), r["y_h"], r["z_h"])
     up = wide_chunk("hly", w_hu, slice(hid, 2 * hid), r["y_u"], r["z_u"])
@@ -542,9 +583,10 @@
     inp.place = cube_place(w_one, in_side)
     inp_sum.place = cube_place(r["dw_in"], gate_side)
     inp_sum.result = lambda q: fin.at[at(q * rec, blk, 16), in_side]
-    ri.source = lambda q: gri.at[at(q * rec + blk, cblk, 16)]
-    ri.place = lambda q: w_ri.at[q, s]
-    ri.result = lambda q: fin.at[at(q * rec + blk, cblk, 16)]
+    for c, cols in ((ra, gate_side), (rb, in_side)):
+        c.source = lambda q, cols=cols: gri.at[at(q * rec + blk, cblk, 16), cols]
+        c.place = lambda q, cols=cols: w_ri.at[q, s, :, cols]
+        c.result = lambda q, cols=cols: fin.at[at(q * rec + blk, cblk, 16), cols]
     hi.source = lambda q: xhu.at[at(q * blk, blk, 16)]
     hi.place = cube_place(w_hu, slice(0, hid))
     hi.result = lambda q: fin_hu.at[at(q * blk, blk, 16), slice(0, hid)]
@@ -672,11 +714,11 @@
     def token_rows(ref):
         return lambda q, h: ref.at[at((h * GROUP + q) * here, here, 16)]
 
-    def merge(view, first, slots, h):
-        net.put(view(corner, h), first(h, 1), to_mate, slots[3 * h], "part")
-        net.put(view(mate, h), first(h, 0), to_mate, slots[3 * h + 1], "part")
-
-    def merge_relay(view, first, second, slots, h, parts, tile):
+    def merge(view, first, slots, h, tag="part"):
+        net.put(view(corner, h), first(h, 1), to_mate, slots[3 * h], tag)
+        net.put(view(mate, h), first(h, 0), to_mate, slots[3 * h + 1], tag)
+
+    def merge_relay(view, first, second, slots, h, parts, tile, tag="part"):
         net.got(first(h, 1), to_mate, slots[3 * h])
 
         def add(i):
@@ -684,7 +726,7 @@
             v[...] = (v[...].astype(F32) + tile(first(h, 1), i)[...].astype(F32)).astype(BF16)
 
         loop(parts, add)
-        net.put(view(across, h), second(h), to_across, slots[3 * h + 2], "part")
+        net.put(view(across, h), second(h), to_across, slots[3 * h + 2], tag)
 
     def merge_end(first, second, slots, h):
         net.got(first(h, 0), to_mate, slots[3 * h + 1])
@@ -717,10 +759,10 @@
         gain_acc[index] += term[0:8] + term[8:16]
         return scaler * (scaled - values * (scaler * scaler * inner))
 
-    def over(h, body):
+    def over(h, body, starts=range(0, here, STEP)):
         def row(i):
             q = h * GROUP + i
-            for start in range(0, here, STEP):
+            for start in starts:
                 for g, lanes in enumerate(groups):
                     body(q, start, lanes, g)
 
@@ -739,10 +781,43 @@
         now = brx[q, pl.ds(EDGE + start, STEP), marks]
         return (now == brx[q, pl.ds(EDGE + start - k, STEP), marks]).astype(F32)
 
+    def keep_down(i, total):
+        g_d[at(i * 16, 16, 16), :] = total
+
+    def keep_out(i, total):
+        g_o[at(i * 16, 16, 16), :] = total
+
+    def finish_sum(c):
+        if c is dn:
+            sum_end(dn_sum, keep_down)
+        elif c is wo:
+            sum_end(wo, keep_out)
+        else:
+            sum_end_spread(summing.get(c, c))
+
+    moved = {"inp": inp, "gat": gat, "ra": ra, "rb": rb, "wo": wo, "hi": hi, "up": up, "dn": dn}
+    summing = {gat: gat_sum, inp: inp_sum, dn: dn_sum}
+    acts = {
+        "wait": spread_wait,
+        "g0": g0,
+        "g1": g1,
+        "g2": g2,
+        "g3": g3,
+        "sp": lambda c, *which: sp(summing.get(c, c), *which),
+        "se": lambda c, *which: se(summing.get(c, c), *which),
+        "sf": lambda c: sf(summing.get(c, c)),
+        "end": finish_sum,
+    }
+
+    def tick(name):
+        for event in PLAN.get(name, ()):
+            act, which, *slots = event.split()
+            acts[act](moved[which], *map(int, "".join(slots)))
+
     norm_slots, gout_slots, conv_slots = (net.slots(6), net.slots(6), net.slots(6))
     two_slots, gres_slots = (net.slots(6), net.slots(6))
     out_slots, gnt_slots, down_slots, thru_slots, gn_slots = (net.slots(6) for _ in range(5))
-    halo_slot, halo_back = net.slots(2)
+    halo_slots, halo_back = (net.slots(2), net.slots(2))
     pre_slots, back_slots, vec_slots, last_slots = (
         net.slots(RING),
         net.slots(RING),
@@ -774,30 +849,28 @@
     fetch_wait("w_gate")
     prepare(gat, blk, cblk, "w_gate")
     spread(gat)
-    fetch_wait("w_recur", "w_inject")
-    prepare(ri, cblk, cblk, "w_recur", "w_inject")
-    spread(ri)
-    spread_wait(inp)
-    g0(inp)
+    fetch_wait("w_recur")
+    prepare(ra, cblk, cblk, "w_recur")
+    spread(ra)
+    fetch_wait("w_inject")
+    prepare(rb, cblk, cblk, "w_inject")
+    spread(rb)
+    tick("f1")
     norm_half(0)
     share(norm_rows, norm_slots, 0)
-    spread_wait(gat)
-    g0(gat)
+    tick("f2")
     norm_half(1)
     share(norm_rows, norm_slots, 1)
-    g1(inp)
-    g2(inp)
+    tick("f3")
     fetch_wait("w_hidden")
     prepare(hi, blk, fblk, "w_hidden")
-    g1(gat)
-    g3(inp)
+    tick("f4")
     spread(hi)
-    spread_wait(ri)
-    g0(ri)
-    g2(gat)
+    tick("f5")
     fetch_wait("w_upward")
     prepare(up, blk, fblk, "w_upward")
     spread(up)
+    tick("f6")
 
     fetch_wait("vec")
     log_of = lambda grown: jnp.log(grown)
@@ -822,15 +895,49 @@
         tgx[:, here : here + EDGE, :] = jnp.full((rows, EDGE, chans + LANES), -1.0, F32)
 
     share_relay(norm_rows, norm_slots, 0)
-    fetch_wait("cot")
+    tick("f7")
+    fetch_wait("cot", "own_d")
     for h in range(2):
         def low_tile(i, h=h):
             sixteen(gout_rows(b, h), i)[...] = own(cot, h, i)[...].astype(BF16)
 
         loop(tiles16, low_tile)
+    tick("f8")
     gather_wait(inp)
     share_end(norm_rows, norm_slots, 0)
 
+    def edge_copies(ref, src, dst, slots, step, gives, takes):
+        def copy(h, where):
+            block = pl.ds(h * GROUP, GROUP)
+            return pltpu.make_async_remote_copy(
+                src_ref=ref.at[block, pl.ds(src, EDGE)],
+                dst_ref=ref.at[block, pl.ds(dst, EDGE)],
+                send_sem=net.send.at[slots[h]],
+                recv_sem=net.recv.at[slots[h]],
+                device_id=(where, b),
+                device_id_type=MESH,
+            )
+
+        def out(h):
+            @pl.when(gives)
+            def _():
+                copy(h, lax.rem(s + step, RING)).start()
+
+        def arrive(h):
+            @pl.when(takes)
+            def _():
+                copy(h, lax.rem(s + RING - step, RING)).wait_recv()
+
+        def left():
+            @pl.when(gives)
+            def _():
+                for h in range(2):
+                    copy(h, lax.rem(s + step, RING)).wait_send()
+
+        return (out, arrive, left)
+
+
+    edge_out, edge_in, edge_left = edge_copies(brx, here, 0, halo_slots, 1, s < RING - 1, s > 0)
     for h in range(2):
         if h:
             share_relay(norm_rows, norm_slots, h)
@@ -842,57 +949,31 @@
         ids = norm[span, width : width + LANES].astype(F32).reshape(GROUP, here, LANES)
         brx[block, EDGE : EDGE + here, marks] = ids
         tgx[block, 0:here, marks] = ids
-
-    def edge_copies(ref, src, dst, slot, step, gives, takes):
-        def copy(where):
-            return pltpu.make_async_remote_copy(
-                src_ref=ref.at[:, pl.ds(src, EDGE)],
-                dst_ref=ref.at[:, pl.ds(dst, EDGE)],
-                send_sem=net.send.at[slot],
-                recv_sem=net.recv.at[slot],
-                device_id=(where, b),
-                device_id_type=MESH,
-            )
-
-        def out(act):
-            @pl.when(gives)
-            def _():
-                act(copy(lax.rem(s + step, RING)))
-
-        def arrive():
-            @pl.when(takes)
-            def _():
-                copy(lax.rem(s + RING - step, RING)).wait_recv()
-
-        return (out, arrive)
-
-    edge_out, edge_in = edge_copies(brx, here, 0, halo_slot, 1, s < RING - 1, s > 0)
-    edge_out(lambda one: one.start())
-    g3(gat)
-    edge_in()
-
-    for h in range(2):
-        def conv_tile(q, start, lanes, g):
-            total = vec[4:5, lanes] + vec[0:1, lanes] * brx[q, pl.ds(EDGE + start, STEP), lanes]
-            for k in range(1, 4):
-                lag = brx[q, pl.ds(EDGE + start - k, STEP), lanes]
-                total = total + vec[k : k + 1, lanes] * lag * same(q, start, k)
-            conv_out[q, pl.ds(start, STEP), lanes] = total
-            conv[flat(q, start), at(b * chans + g * LANES, LANES, LANES)] = total.astype(BF16)
-
-        over(h, conv_tile)
+        edge_out(h)
+        tick(f"f9{h}")
+
+    def conv_tile(q, start, lanes, g):
+        total = vec[4:5, lanes] + vec[0:1, lanes] * brx[q, pl.ds(EDGE + start, STEP), lanes]
+        for k in range(1, 4):
+            lag = brx[q, pl.ds(EDGE + start - k, STEP), lanes]
+            total = total + vec[k : k + 1, lanes] * lag * same(q, start, k)
+        conv_out[q, pl.ds(start, STEP), lanes] = total
+        conv[flat(q, start), at(b * chans + g * LANES, LANES, LANES)] = total.astype(BF16)
+
+    for h in range(2):
+        over(h, conv_tile, range(STEP, here, STEP))
+    for h in range(2):
+        edge_in(h)
+        over(h, conv_tile, [0])
         share(conv_cols, conv_slots, h)
-        g2(ri) if h else g1(ri)
-    g3(ri)
-    g0(wo)
-    spread_wait(hi)
-    g0(hi)
+        tick(f"conv{h}")
     share_relay(conv_cols, conv_slots, 0)
-    g1(wo)
-    g2(wo)
+    tick("f10")
     share_relay(conv_cols, conv_slots, 1)
+    tick("f11")
     share_end(conv_cols, conv_slots, 0)
-    gather_wait(ri)
+    gather_wait(ra)
+    gather_wait(rb)
 
     for h in range(2):
         if h:
@@ -915,10 +996,7 @@
             stx[q, pl.ds(EDGE + start, STEP), lanes] = scale * ig * conv_out[q, span, lanes]
 
         over(h, gate_tile)
-        if h == 0:
-            g3(wo)
-        else:
-            spread_wait(up)
+        tick(f"gate{h}")
 
     def ends(p, state):
         mult = carry[:, p, :]
@@ -942,11 +1020,7 @@
         return state
 
     hand_round(pre_f, product, tail, pre_slots)
-    g1(hi)
-    g2(hi)
-    g0(up)
-    fetch_wait("own_d")
-    g0(dn)
+    tick("f12")
     gather_wait(gat)
 
     for h in range(2):
@@ -958,6 +1032,7 @@
             tgx[q, span, lanes] = gelu_parts(gate_pre[q, span, lanes])[0]
 
         over(h, act_tile)
+        tick(f"act{h}")
     state = entering(pre_f, pre_slots, True)
     stx[:, EDGE - 1, :] = state
 
@@ -967,7 +1042,7 @@
         return state
 
     lax.fori_loop(0, here, scan, state, unroll=8)
-    g3(hi)
+    tick("f13")
     gather_wait(wo)
 
     for h in range(2):
@@ -979,9 +1054,10 @@
         span = pl.ds(h * half, half)
         part[span, :] = dot_nn(mix[span, :], w_o[...]).astype(BF16)
         merge(part_rows, first_in, out_slots, h)
+        tick(f"mix{h}")
     for h in range(2):
         merge_relay(part_rows, first_in, second_in, out_slots, h, tiles16, sixteen)
-    g1(up)
+    tick("f14")
     for h in range(2):
         merge_end(first_in, second_in, out_slots, h)
 
@@ -992,15 +1068,14 @@
 
         loop(tiles16, resid_tile)
         share(two_rows, two_slots, h)
-        if h == 0:
-            g2(up)
-            g1(dn)
+        tick(f"resid{h}")
     for h in range(2):
         share(gout_rows, gout_slots, h)
-    g3(up)
-    g2(dn)
+    tick("f15")
     share_relay(two_rows, two_slots, 0)
+    tick("f16")
     share_relay(two_rows, two_slots, 1)
+    tick("f17")
     gather_wait(hi)
     gather_wait(up)
 
@@ -1027,14 +1102,13 @@
 
             loop(half // STEP, tile)
         share_relay(gout_rows, gout_slots, h)
-        if h == 0:
-            g3(dn)
+        tick(f"hid{h}")
     for h in range(2):
         share_end(gout_rows, gout_slots, h)
     for j in range(2):
         cols = slice(j * hid // 2, (j + 1) * hid // 2)
         r["dw_d"][cols, :] = dot_tn(prod[:, cols], gout[...]).astype(BF16)
-    sp(dn_sum, 3, 2, 1, 0)
+    tick("f18")
     gather_wait(dn)
 
     net.flush("part")
@@ -1050,10 +1124,11 @@
             cols = slice(j * width // 2, (j + 1) * width // 2)
             part[span, cols] = dot_nt(ghu[span, :], w_hu[4 * j : 4 * j + 4].reshape(width // 2, 2 * hid)).astype(BF16)
         merge(part_rows, first_in, gnt_slots, h)
+        tick(f"back{h}")
     for h in range(2):
         merge_relay(part_rows, first_in, second_in, gnt_slots, h, tiles16, sixteen)
-
-    se(dn_sum, 3)
+    tick("b2")
+
     net.flush("")
     for j in range(2):
         def grad_hu(i, j=j):
@@ -1063,11 +1138,7 @@
             w_hu[pl.ds(2 * i, 2), :, side] = got.reshape(2, GROUP * blk, hid)
 
         loop(width // 256, grad_hu)
-        if j == 0:
-            sp(hi, 3, 2, 1, 0)
-            se(dn_sum, 2)
-        else:
-            sp(up, 3)
+        tick(f"grad{j}")
 
     for h in range(2):
         merge_end(first_in, second_in, gnt_slots, h)
@@ -1080,16 +1151,16 @@
 
         loop(tiles16, second_norm)
         share(gres_rows, gres_slots, h)
-        if h == 0:
-            sf(dn_sum)
+        tick(f"norm{h}")
     net.flush("part")
     for h in range(2):
         span = pl.ds(h * half, half)
         part[span, :] = dot_nn(prod[span, :], w_d[...]).astype(BF16)
+    tick("b3")
     share_relay(gres_rows, gres_slots, 0)
-    se(hi, 3)
+    tick("b4")
     share_relay(gres_rows, gres_slots, 1)
-    se(hi, 2)
+    tick("b5")
 
     for h in range(2):
         share_end(gres_rows, gres_slots, h)
@@ -1112,6 +1183,7 @@
             tgx[q, span, lanes] = back * act
 
         over(h, mix_back)
+        tick(f"mixb{h}")
 
     def ends_back(i, state):
         p = here - 1 - i
@@ -1120,7 +1192,7 @@
 
     product, tail = lax.fori_loop(0, here, ends_back, begin, unroll=8)
     hand_round(pre_b, product, tail, back_slots)
-    sp(up, 2, 1, 0)
+    tick("b6")
 
     w_o[...] = dot_tn(mix[...], gres[...]).astype(BF16)
     for j in range(2):
@@ -1128,6 +1200,7 @@
         got = dot_tn(norm[:, cols], ggb[:, gate_side]).astype(BF16)
         r["dw_gate"][4 * j : 4 * j + 4] = got.reshape(4, GROUP * blk, chans)
 
+    tick("b7")
     state = entering(pre_b, back_slots, False)
 
     def scan_back(i, state):
@@ -1138,8 +1211,7 @@
 
     lax.fori_loop(0, here, scan_back, state, unroll=8)
 
-    sp(gat_sum, 3, 2, 1, 0)
-    sp(wo, 3, 2, 1, 0)
+    tick("b8")
     thru_cols = lambda q, h: ghu.at[pl.ds(h * half, half), at(q * chans, chans, LANES)]
     thru_first = lambda h, slot: prod.at[pl.ds(h * half, half), pl.ds(slot * chans, chans)]
     thru_second = lambda h: gout.at[pl.ds(h * half, half), pl.ds(0, chans)]
@@ -1170,7 +1242,7 @@
             pair = slice(2 * j, 2 * j + 2)
             got = dot_nt(gri[span, :], w_ri[pair].reshape(2 * chans, two))
             ghu[span, 2 * j * chans : 2 * (j + 1) * chans] = got.astype(BF16)
-        if h:
+        if h == 0:
             for k in range(2):
                 merge_end(first_in, second_in, down_slots, k)
 
@@ -1178,76 +1250,68 @@
                     own(out, k, i)[...] = own(out, k, i)[...] + merged(k, i)
 
                 loop(tiles16, out_tile)
-        merge(thru_cols, thru_first, thru_slots, h)
-        if h == 0:
-            sf(hi)
-            se(up, 3)
+        merge(thru_cols, thru_first, thru_slots, h, "thru")
+        tick(f"thru{h}")
     leave_out = fetch(0, out, out_hbm)
     for h in range(2):
-        merge_relay(thru_cols, thru_first, thru_second, thru_slots, h, half // 16, sixteen)
+        merge_relay(thru_cols, thru_first, thru_second, thru_slots, h, half // 16, sixteen, "thru")
+    tick("b9")
 
     def grad_ri(i):
         got = dot_tn(conv[:, at(i * chans, chans, LANES)], gri[...])
         w_ri[i] = got.astype(BF16).reshape(RING, cblk, two)
 
     loop(GROUP, grad_ri)
-    sp(ri, 3)
-    se(up, 2)
-    se(gat_sum, 3, 2)
-
+    tick("b10")
+
+    head_out, head_in, head_left = edge_copies(tgx, 0, here, halo_back, RING - 1, s > 0, s < RING - 1)
+
+    def conv_grad(q, start, lanes, g):
+        span = flat(q, start)
+        total = ghu[span, at(b * chans + g * LANES, LANES, LANES)].astype(F32)
+        total = total + prod[span, lanes].astype(F32) + gout[span, lanes].astype(F32)
+        tgx[q, pl.ds(start, STEP), lanes] += total
+
+    def conv_back(q, start, lanes, g):
+        now = tgx[q, pl.ds(start, STEP), lanes]
+        ids = tgx[q, pl.ds(start, STEP), marks]
+        total = vec[0:1, lanes] * now
+        add_to(4, lanes, now)
+        add_to(0, lanes, now * brx[q, pl.ds(EDGE + start, STEP), lanes])
+        for k in range(1, 4):
+            later = pl.ds(start + k, STEP)
+            match = (tgx[q, later, marks] == ids).astype(F32)
+            total = total + vec[k : k + 1, lanes] * tgx[q, later, lanes] * match
+            lag = brx[q, pl.ds(EDGE + start - k, STEP), lanes]
+            add_to(k, lanes, now * lag * same(q, start, k))
+        ggb[flat(q, start), slice(chans + g * LANES, chans + (g + 1) * LANES)] = total.astype(BF16)
+
+    net.flush("part")
     for h in range(2):
         merge_end(thru_first, thru_second, thru_slots, h)
-
-        def conv_grad(q, start, lanes, g, h=h):
-            span = flat(q, start)
-            total = ghu[span, at(b * chans + g * LANES, LANES, LANES)].astype(F32)
-            total = total + prod[span, lanes].astype(F32) + gout[span, lanes].astype(F32)
-            tgx[q, pl.ds(start, STEP), lanes] += total
-
         over(h, conv_grad)
-        if h == 0:
-            sf(up)
-
-    head_out, head_in = edge_copies(tgx, 0, here, halo_back, RING - 1, s > 0, s < RING - 1)
-    head_out(lambda one: one.start())
-    sp(ri, 2, 1, 0)
-    se(ri, 3)
-    head_in()
-    se(wo, 3, 2)
-    net.flush("part")
-    for h in range(2):
-        def conv_back(q, start, lanes, g):
-            now = tgx[q, pl.ds(start, STEP), lanes]
-            ids = tgx[q, pl.ds(start, STEP), marks]
-            total = vec[0:1, lanes] * now
-            add_to(4, lanes, now)
-            add_to(0, lanes, now * brx[q, pl.ds(EDGE + start, STEP), lanes])
-            for k in range(1, 4):
-                later = pl.ds(start + k, STEP)
-                match = (tgx[q, later, marks] == ids).astype(F32)
-                total = total + vec[k : k + 1, lanes] * tgx[q, later, lanes] * match
-                lag = brx[q, pl.ds(EDGE + start - k, STEP), lanes]
-                add_to(k, lanes, now * lag * same(q, start, k))
-            ggb[flat(q, start), slice(chans + g * LANES, chans + (g + 1) * LANES)] = total.astype(BF16)
-
-        over(h, conv_back)
-    for j in range(2):
-        cols = slice(j * width // 2, (j + 1) * width // 2)
-        got = dot_tn(norm[:, cols], ggb[:, in_side]).astype(BF16)
-        r["dw_in"][4 * j : 4 * j + 4] = got.reshape(4, GROUP * blk, chans)
-    sp(inp_sum, 3, 2, 1, 0)
-    for h in range(2):
+        head_out(h)
+        tick(f"edge{h}")
+        over(h, conv_back, range(0, here - STEP, STEP))
+        head_in(h)
+        over(h, conv_back, [here - STEP])
+        tick(f"taps{h}")
         span = pl.ds(h * half, half)
         for j in range(2):
             cols = slice(j * width // 2, (j + 1) * width // 2)
             part[span, cols] = dot_nt(ggb[span, :], w_one[4 * j : 4 * j + 4].reshape(width // 2, two)).astype(BF16)
         merge(part_rows, first_in, gn_slots, h)
-    for h in range(2):
-        merge_relay(part_rows, first_in, second_in, gn_slots, h, tiles16, sixteen)
-
-    se(ri, 2)
-    sf(gat_sum)
-    se(inp_sum, 3, 2)
+        tick(f"gain{h}")
+        if h == 0:
+            merge_relay(part_rows, first_in, second_in, gn_slots, h, tiles16, sixteen)
+    for j in range(2):
+        cols = slice(j * width // 2, (j + 1) * width // 2)
+        got = dot_tn(norm[:, cols], ggb[:, in_side]).astype(BF16)
+        r["dw_in"][4 * j : 4 * j + 4] = got.reshape(4, GROUP * blk, chans)
+    tick("b13")
+    merge_relay(part_rows, first_in, second_in, gn_slots, 1, tiles16, sixteen)
+    tick("b14")
+
 
     for h in range(2):
         merge_end(first_in, second_in, gn_slots, h)
@@ -1257,6 +1321,7 @@
             own(gin, h, i)[...] = own(gin, h, i)[...] + back
 
         loop(tiles16, first_norm)
+        tick(f"first{h}")
     leave_gin = fetch(1, gin, gin_hbm)
 
     for k in range(8):
@@ -1270,22 +1335,7 @@
     for k in range(1, RING):
         net.put(vs.at[s], vs.at[s], ring_device(ring_to[k]), vec_slots[k])
 
-    def keep_down(i, total):
-        g_d[at(i * 16, 16, 16), :] = total
-
-    def keep_out(i, total):
-        g_o[at(i * 16, 16, 16), :] = total
-
-    sf(ri)
-    sf(wo)
-    sum_end(dn_sum, keep_down)
-    sum_end_spread(hi)
-    sum_end_spread(up)
-    sf(inp_sum)
-    sum_end_spread(gat_sum)
-    sum_end_spread(ri)
-    sum_end(wo, keep_out)
-    sum_end_spread(inp_sum)
+    tick("t0")
     for k in range(1, RING):
         net.got(vs.at[ring_from[k]], ring_device(ring_from[k]), vec_slots[k])
     total = vs[0]
@@ -1294,6 +1344,7 @@
     vb[b] = total
     for (peer, to), slot in zip(group_peers, last_slots):
         net.put(vb.at[b], vb.at[b], to, slot)
+    tick("t1")
     for (peer, to), slot in zip(group_peers, last_slots):
         net.got(vb.at[peer], to, slot)
     g_vec[:, 0:chans] = total[:, 0:chans]
@@ -1301,14 +1352,14 @@
     for q in range(1, GROUP):
         summed = summed + vb[q, :, chans : chans + piece]
     g_vec[:, chans : chans + piece] = summed
-    for c in (hi, up, gat_sum, inp_sum, ri):
+    for c in (hi, up, gat_sum, ra, rb, inp_sum):
         home_wait(c)
     net.flush()
     leave_out.wait()
     leave_gin.wait()
 
-    edge_out(lambda one: one.wait_send())
-    head_out(lambda one: one.wait_send())
+    edge_left()
+    head_left()
 
 
 def finish(names, *refs):
@@ -1455,8 +1506,10 @@
         "x_in": ((2, here, width), BF16),
         "pre_f": ((RING, 2 * rows, chans), F32),
         "pre_b": ((RING, 2 * rows, chans), F32),
-        "y_ri": ((4, GROUP, cblk, 2 * chans), BF16),
-        "z_ri": ((3, GROUP, cblk, 2 * chans), BF16),
+        "y_ra": ((4, GROUP, cblk, chans), BF16),
+        "z_ra": ((3, GROUP, cblk, chans), BF16),
+        "y_rb": ((4, GROUP, cblk, chans), BF16),
+        "z_rb": ((3, GROUP, cblk, chans), BF16),
         "y_o": ((4 * cblk, width), BF16),
         "z_o": (((3) * cblk, width), BF16),
         "y_h": ((4, GROUP * blk, hid), BF16),

time: 274 us -> 257 us (0.938)
  Pallas kernels: 270 us -> 253 us
    pallas_call x1, Pallas kernels: 265 us -> 249 us  [split_block(): pl.pallas_call(functools.partial(fused, names), out_shape=shapes(outputs)...]
where the time goes in v4:
time: 257 us
  Pallas kernels  253 us (98%)
  local copies, waits for them, and re-layouts  2.57 us (1%)
    pallas_call x1, Pallas kernels, split_block(): pl.pallas_call(functools.partial(fused, names), out_shape=shapes(outputs)...  249 us

profile of v4, /device:TPU:0, one launch (start us, length us, event | category | flops | bytes accessed | tf_op | source)
XLA Modules:
  0.0 256.7 jit_solution(12964243421390448795)
XLA Ops:
  0.7 248.8 %block.1 = (f32[256,1024]{1,0:T(8,128)}, f32[256,1024]{1,0:T(8,128)}, bf16[320,768]{1,0:T(8,128)(2,1)}, bf16[128,1536]{1,0:T(8,128)(2,1)}, f32[48,1024]{1,0:T(8,...) custom-call(f32[256,1024]{1,0:T(8,128)} %bitcast.4, f32[256,1024]{1,0:T(8,128)} %bitcast.5, s32[2,128]{1,0:T(2,128)} %refs_2_.1, ...), custom_call_target="tpu_custom_call" | custom-call | tf_op jit(solution)/shard_map/block/pallas_call | solution.py:1530
  249.5 0.0 copy-start.1
  249.5 4.7 %finish.1 = (f32[32,1536]{1,0:T(8,128)}, f32[32,1536]{1,0:T(8,128)}, f32[48,1536]{1,0:T(8,128)}, f32[48,1536]{1,0:T(8,128)}, f32[48,1024]{1,0:T(8,128)}, /*index...) custom-call(bf16[320,768]{1,0:T(8,128)(2,1)} %get-tuple-element.41.r, ...), custom_call_target="tpu_custom_call" | custom-call | tf_op jit(solution)/shard_map/finish/pallas_call | solution.py:1560
  254.2 0.0 copy-done.1
  254.2 0.0 copy-start
  254.2 1.0 copy.37
  255.2 0.6 copy-done
  255.8 1.0 copy.38
Async XLA Ops:
  249.5 4.7 %copy-start.1 = (f32[256,1024]{1,0:T(8,128)S(1)}, f32[256,1024]{1,0:T(8,128)}, u32[]{:S(2)}) copy-start(f32[256,1024]{1,0:T(8,128)} %get-tuple-element.39) | copy-start | bytes 3145732
  254.2 1.6 copy-start
